TPU v7x, 128 devices: a whole 4x4x4 slice. The times are simulated.
128 devices in a mesh: ctx: 16 (over z, y_lo, core), ch: 8 (over x, y_hi).
Axes of the slice: x: 4, y: 4 (y_hi: 2, y_lo: 2; y = y_hi * 2 + y_lo), z: 4, core: 2. Of those that a mesh axis runs over, the one named last changes fastest.
Arguments:
- gate_in: bfloat16 [4096, 8192], P('ctx', 'ch'), may hold values from -6 to 6
- key_in: bfloat16 [4096, 8192], P('ctx', 'ch'), may hold values from -6 to 6
- value_in: bfloat16 [4096, 8192], P('ctx', 'ch'), may hold values from -6 to 6
- cotangent: bfloat16 [4096, 8192], P('ctx', 'ch'), may hold values from -6 to 6
- skip: float32 [8192], P('ch'), may hold values from 0.5 to 1.5
- residue: float32 [1024, 16], P('ch'), may hold values from -2 to 2
- decay: float32 [1024, 16], P('ch'), may hold values from 0.00024414062 to 0.05
Outputs:
- mixed: bfloat16 [4096, 8192], P('ctx', 'ch')
- grad_gate: bfloat16 [4096, 8192], P('ctx', 'ch')
- grad_key: bfloat16 [4096, 8192], P('ctx', 'ch')
- grad_value: bfloat16 [4096, 8192], P('ctx', 'ch')
- grad_skip: float32 [8192], P('ch')
- grad_residue: float32 [1024, 16], P('ch')
- grad_log_decay: float32 [1024, 16], P('ch')
All inputs are finite; a program needn't handle non-finite values.
Results may differ from a plain program's by a relative error of at most 0.0012.
Values sent between devices are 32-bit elements; how exact they have to be, the bound alone decides.
No kernel may reach another device: no remote copies, remote signals or barrier semaphores. Data moves between devices by JAX's collectives and lax.ppermute only.
A program may use at most 128 MiB of HBM per device.

v0:
```python
import math

import jax
import jax.numpy as jnp
from jax import lax
from jax.sharding import PartitionSpec as P


def impulse(residue, decay, times):
    total = jnp.zeros((times.shape[0], residue.shape[0]), jnp.float32)
    for mode in range(residue.shape[1]):
        rate = decay[:, mode][None, :]
        total = total + residue[:, mode][None, :] * jnp.sqrt(rate) * jnp.exp(-rate * times[:, None])
    return total


def phase_table(left, right, modulus, sign):
    turns = left[:, None] * right[None, :] % modulus
    angle = turns.astype(jnp.float32) * (sign * 2.0 * math.pi / modulus)
    return (jnp.cos(angle), jnp.sin(angle))


def exact_einsum(form, first, second):
    return jnp.einsum(form, first, second, precision=lax.Precision.HIGHEST)


def exact_dot(first, second):
    return jnp.dot(first, second, precision=lax.Precision.HIGHEST)


def outer_order(count):
    first = jnp.arange(count, dtype=jnp.int32)
    second = jnp.where(first == 0, count, 2 * count - first)
    return jnp.stack([first, second], axis=1).reshape(2 * count)


def spectrum(signal):
    count = lax.axis_size("ctx")
    index = lax.axis_index("ctx")
    positions, channels = signal.shape
    rows = positions // count
    full = 2 * positions * count
    outer = outer_order(count)
    cos_outer, sin_outer = phase_table(outer, jnp.arange(count, dtype=jnp.int32), 2 * count, -1.0)
    moved = lax.all_to_all(signal, "ctx", split_axis=0, concat_axis=0, tiled=True)
    moved = moved.reshape(count, rows * channels)
    real_part = exact_dot(cos_outer, moved).reshape(2 * count, rows, channels)
    imag_part = exact_dot(sin_outer, moved).reshape(2 * count, rows, channels)
    local_rows = index * rows + jnp.arange(rows, dtype=jnp.int32)
    cos_turn, sin_turn = phase_table(outer, local_rows, full, -1.0)
    cos_turn = cos_turn[:, :, None]
    sin_turn = sin_turn[:, :, None]
    turned_re = real_part * cos_turn - imag_part * sin_turn
    turned_im = real_part * sin_turn + imag_part * cos_turn
    turned_re, turned_im = (
        lax.all_to_all(turned_re, "ctx", split_axis=0, concat_axis=1, tiled=True),
        lax.all_to_all(turned_im, "ctx", split_axis=0, concat_axis=1, tiled=True),
    )
    wave = jnp.arange(positions, dtype=jnp.int32)
    cos_inner, sin_inner = phase_table(wave, wave, positions, -1.0)
    out_re = exact_einsum("kp,jpc->jkc", cos_inner, turned_re) - exact_einsum(
        "kp,jpc->jkc", sin_inner, turned_im
    )
    out_im = exact_einsum("kp,jpc->jkc", cos_inner, turned_im) + exact_einsum(
        "kp,jpc->jkc", sin_inner, turned_re
    )
    return (out_re, out_im)


def signal_of(spec_re, spec_im):
    count = lax.axis_size("ctx")
    index = lax.axis_index("ctx")
    pairs, positions, channels = spec_re.shape
    rows = positions // count
    full = 2 * positions * count
    wave = jnp.arange(positions, dtype=jnp.int32)
    cos_inner, sin_inner = phase_table(wave, wave, positions, 1.0)
    back_re = exact_einsum("pk,jkc->jpc", cos_inner, spec_re) - exact_einsum(
        "pk,jkc->jpc", sin_inner, spec_im
    )
    back_im = exact_einsum("pk,jkc->jpc", cos_inner, spec_im) + exact_einsum(
        "pk,jkc->jpc", sin_inner, spec_re
    )
    outer_local = jnp.stack([index, jnp.where(index == 0, count, 2 * count - index)])
    cos_turn, sin_turn = phase_table(outer_local, wave, full, 1.0)
    cos_turn = cos_turn[:, :, None]
    sin_turn = sin_turn[:, :, None]
    turned_re = back_re * cos_turn - back_im * sin_turn
    turned_im = back_re * sin_turn + back_im * cos_turn
    turned_re, turned_im = (
        lax.all_to_all(turned_re, "ctx", split_axis=1, concat_axis=0, tiled=True),
        lax.all_to_all(turned_im, "ctx", split_axis=1, concat_axis=0, tiled=True),
    )
    cos_outer, sin_outer = phase_table(
        jnp.arange(count, dtype=jnp.int32), outer_order(count), 2 * count, 1.0
    )
    flat_re = turned_re.reshape(2 * count, rows * channels)
    flat_im = turned_im.reshape(2 * count, rows * channels)
    real_out = (exact_dot(cos_outer, flat_re) - exact_dot(sin_outer, flat_im)) / full
    placed = lax.all_to_all(
        real_out.reshape(count, rows, channels), "ctx", split_axis=0, concat_axis=1, tiled=True
    )
    return placed.reshape(positions, channels)


def on_device(gate_in, key_in, value_in, cotangent, skip, residue, decay):
    index = lax.axis_index("ctx")
    positions, channels = gate_in.shape
    times = (index * positions + jnp.arange(positions, dtype=jnp.int32)).astype(jnp.float32)
    every_residue, every_decay = (
        lax.all_gather(residue, "ch", axis=0, tiled=True),
        lax.all_gather(decay, "ch", axis=0, tiled=True),
    )
    kernel_re, kernel_im = spectrum(impulse(every_residue, every_decay, times))
    count_filters = kernel_re.shape[2]
    repeats = channels // count_filters
    kernel_re = jnp.tile(kernel_re, (1, 1, repeats))
    kernel_im = jnp.tile(kernel_im, (1, 1, repeats))
    gate_value = gate_in.astype(jnp.float32)
    key_value = key_in.astype(jnp.float32)
    value_value = value_in.astype(jnp.float32)
    cot_value = cotangent.astype(jnp.float32)
    product = key_value * value_value
    back = cot_value * gate_value
    prod_re, prod_im = spectrum(product)
    back_re, back_im = spectrum(back)
    mixed_re = prod_re * kernel_re - prod_im * kernel_im
    mixed_im = prod_re * kernel_im + prod_im * kernel_re
    corr_re = kernel_re * back_re + kernel_im * back_im
    corr_im = kernel_re * back_im - kernel_im * back_re
    conv = signal_of(mixed_re, mixed_im)
    grad_conv = signal_of(corr_re, corr_im)
    pre_gate = conv + skip[None, :] * product
    mixed = (gate_value * pre_gate).astype(jnp.bfloat16)
    grad_gate = (cot_value * pre_gate).astype(jnp.bfloat16)
    grad_product = grad_conv + skip[None, :] * back
    grad_key = (grad_product * value_value).astype(jnp.bfloat16)
    grad_value = (grad_product * key_value).astype(jnp.bfloat16)
    pairs = prod_re.shape[0]
    own_re = (
        (prod_re * back_re + prod_im * back_im)
        .reshape(pairs, positions, repeats, count_filters)
        .sum(axis=2)
    )
    own_im = (
        (prod_re * back_im - prod_im * back_re)
        .reshape(pairs, positions, repeats, count_filters)
        .sum(axis=2)
    )
    local_count = residue.shape[0]
    total_re, total_im = lax.psum((own_re, own_im), "ch")
    grad_whole = signal_of(total_re, total_im)
    grad_kernel = lax.dynamic_slice_in_dim(
        grad_whole, lax.axis_index("ch") * local_count, local_count, 1
    )
    _, pullback = jax.vjp(lambda weights, rates: impulse(weights, rates, times), residue, decay)
    part_residue, part_decay = pullback(grad_kernel)
    part_skip = jnp.sum(back * product, axis=0)
    grad_residue, grad_log_decay, grad_skip = lax.psum(
        (part_residue, decay * part_decay, part_skip), "ctx"
    )
    return (mixed, grad_gate, grad_key, grad_value, grad_skip, grad_residue, grad_log_decay)


def solution(mesh):
    return jax.shard_map(
        on_device,
        mesh=mesh,
        in_specs=(
            P("ctx", "ch"),
            P("ctx", "ch"),
            P("ctx", "ch"),
            P("ctx", "ch"),
            P("ch"),
            P("ch", None),
            P("ch", None),
        ),
        out_specs=(
            P("ctx", "ch"),
            P("ctx", "ch"),
            P("ctx", "ch"),
            P("ctx", "ch"),
            P("ch"),
            P("ch", None),
            P("ch", None),
        ),
        check_vma=False,
    )
```

profile of v0, /device:TPU:1, one launch (start us, length us, event | category | flops | bytes accessed | tf_op | source)
XLA Modules:
  0.0 917.9 jit_solution(7982009856172697309)
XLA Ops:
  7.2 28.9 %all_gather.7 = f32[1024,16]{0,1:T(8,128)S(1)} all-gather(f32[128,16]{0,1:T(8,128)} %param.13), channel_id=1, replica_groups=mesh['ctx'=16,'ch'=8] {'ch'}, dimensions={0}, use_global_device_ids=true | all-gather | bytes 73728 | tf_op jit(solution)/shard_map/all_gather | solution.py:112
  36.1 28.0 %all_gather.6 = f32[1024,16]{0,1:T(8,128)S(1)} all-gather(f32[128,16]{0,1:T(8,128)} %param.12), channel_id=1, replica_groups=mesh['ctx'=16,'ch'=8] {'ch'}, dimensions={0}, use_global_device_ids=true | all-gather | bytes 73728 | tf_op jit(solution)/shard_map/all_gather | solution.py:111
  68.3 19.9 %all-to-all-start.3 = ((f32[16,16,1024]{2,1,0:T(8,128)}), f32[16,16,1024]{2,1,0:T(8,128)S(1)}, u32[]{:S(2)}, u32[]{:S(2)}) async-start(f32[16,16,1024]{2,1,0:T(8,128)} %multiply_add_fusion.5), calls=%async_computation.3 | async-start | bytes 2097152 | tf_op jit(solution)/shard_map/all_to_all | solution.py:45
  89.3 14.6 %all-to-all-done.3 = f32[16,16,1024]{2,1,0:T(8,128)S(1)} async-done(((f32[16,16,1024]{2,1,0:T(8,128)}), f32[16,16,1024]{2,1,0:T(8,128)S(1)}, u32[]{:S(2)}, u32[]{:S(2)}) %all-to-all-start.3) | async-done | bytes 1048608 | tf_op jit(solution)/shard_map/all_to_all | solution.py:45
  109.8 14.4 %all-to-all-done = f32[16,16,1024]{2,1,0:T(8,128)S(1)} async-done(((f32[16,16,1024]{2,1,0:T(8,128)}), f32[16,16,1024]{2,1,0:T(8,128)S(1)}, u32[]{:S(2)}, u32[]{:S(2)}) %all-to-all-start) | async-done | bytes 1048608 | tf_op jit(solution)/shard_map/all_to_all | solution.py:45
  146.8 7.8 multiply_add_fusion.1
  166.3 23.2 %all-to-all-done.5 = f32[32,16,1024]{2,1,0:T(8,128)} async-done(((f32[32,16,1024]{2,1,0:T(8,128)}), f32[32,16,1024]{2,1,0:T(8,128)}, u32[]{:S(2)}, u32[]{:S(2)}) %all-to-all-start.5) | async-done | bytes 2097184 | tf_op jit(solution)/shard_map/all_to_all | solution.py:57
  198.7 23.1 %all-to-all-done.4 = f32[32,16,1024]{2,1,0:T(8,128)} async-done(((f32[32,16,1024]{2,1,0:T(8,128)}), f32[32,16,1024]{2,1,0:T(8,128)}, u32[]{:S(2)}, u32[]{:S(2)}) %all-to-all-start.4) | async-done | bytes 2097184 | tf_op jit(solution)/shard_map/all_to_all | solution.py:56
  231.0 23.2 %all-to-all-done.10 = f32[32,16,1024]{2,1,0:T(8,128)} async-done(((f32[32,16,1024]{2,1,0:T(8,128)}), f32[32,16,1024]{2,1,0:T(8,128)}, u32[]{:S(2)}, u32[]{:S(2)}) %all-to-all-start.10) | async-done | bytes 2097184 | tf_op jit(solution)/shard_map/all_to_all | solution.py:56
  263.4 23.1 %all-to-all-done.11 = f32[32,16,1024]{2,1,0:T(8,128)} async-done(((f32[32,16,1024]{2,1,0:T(8,128)}), f32[32,16,1024]{2,1,0:T(8,128)}, u32[]{:S(2)}, u32[]{:S(2)}) %all-to-all-start.11) | async-done | bytes 2097184 | tf_op jit(solution)/shard_map/all_to_all | solution.py:57
  327.7 6.0 fusion.75
  342.6 6.2 convolution_add_fusion.2
  377.4 11.1 %add_bitcast_fusion.1 = (f32[2,256,1024]{1,2,0:T(8,128)}, f32[2,256,1024]{1,2,0:T(8,128)}, f32[2,1024,256]{2,1,0:T(8,128)}, f32[2,1024,256]{2,1,0:T(8,128)}, f32...) fusion(f32[2,1024,256]{2,1,0:T(8,128)S(1)} %convolution_add_fusion.3, f32[2,1024,256]{2,1,0:T(8,128)S(1)} %copy-done.24, ...), kind=kOutput, calls=%fused_computation.25 | convolution fusion | flops 1621491712 | bytes 27262976 | tf_op jit(solution)/shard_map/kp,jpc->jkc/dot_general | solution.py:24
  418.7 156.7 %all-reduce.36.cloned.1.call-done = (f32[2,256,1024]{1,2,0:T(8,128)}, f32[2,256,1024]{1,2,0:T(8,128)}) async-done(((f32[2,256,1024]{1,2,0:T(8,128)}, f32[2,256,1024]{1,2,0:T(8,128)}), (f32[2,256,1024]{1,2,0:T(8,128)}, f32[2,256,1024]{1,2,0:T(8,128)})) %all-reduce.36.cloned.1.call-update) | async-done | bytes 4194320 | tf_op jit(solution)/shard_map/psum | solution.py:151
  585.9 7.6 add_bitcast_fusion
  607.6 23.0 %all-to-all-done.15 = f32[2,256,1024]{2,0,1:T(2,128)} async-done(((f32[2,256,1024]{2,0,1:T(2,128)}), f32[2,256,1024]{2,0,1:T(2,128)}, u32[]{:S(2)}, u32[]{:S(2)}) %all-to-all-start.15) | async-done | bytes 2097184 | tf_op jit(solution)/shard_map/all_to_all | solution.py:91
  639.9 23.1 %all-to-all-done.16 = f32[2,256,1024]{2,0,1:T(2,128)} async-done(((f32[2,256,1024]{2,0,1:T(2,128)}), f32[2,256,1024]{2,0,1:T(2,128)}, u32[]{:S(2)}, u32[]{:S(2)}) %all-to-all-start.16) | async-done | bytes 2097184 | tf_op jit(solution)/shard_map/all_to_all | solution.py:92
  672.6 23.1 %all-to-all-done.12 = f32[2,256,1024]{2,0,1:T(2,128)} async-done(((f32[2,256,1024]{2,0,1:T(2,128)}), f32[2,256,1024]{2,0,1:T(2,128)}, u32[]{:S(2)}, u32[]{:S(2)}) %all-to-all-start.12) | async-done | bytes 2097184 | tf_op jit(solution)/shard_map/all_to_all | solution.py:91
  705.0 23.1 %all-to-all-done.13 = f32[2,256,1024]{2,0,1:T(2,128)} async-done(((f32[2,256,1024]{2,0,1:T(2,128)}), f32[2,256,1024]{2,0,1:T(2,128)}, u32[]{:S(2)}, u32[]{:S(2)}) %all-to-all-start.13) | async-done | bytes 2097184 | tf_op jit(solution)/shard_map/all_to_all | solution.py:92
  735.6 24.8 %all-to-all-done.6 = f32[2,256,1024]{2,0,1:T(2,128)} async-done(((f32[2,256,1024]{2,0,1:T(2,128)}), f32[2,256,1024]{2,0,1:T(2,128)}, u32[]{:S(2)}, u32[]{:S(2)}) %all-to-all-start.6) | async-done | bytes 2097184 | tf_op jit(solution)/shard_map/all_to_all | solution.py:91
  776.3 15.7 %all-to-all-done.7 = f32[2,256,1024]{2,0,1:T(2,128)S(1)} async-done(((f32[2,256,1024]{2,0,1:T(2,128)}), f32[2,256,1024]{2,0,1:T(2,128)S(1)}, u32[]{:S(2)}, u32[]{:S(2)}) %all-to-all-start.7) | async-done | bytes 2097184 | tf_op jit(solution)/shard_map/all_to_all | solution.py:92
  827.3 10.2 %all-to-all-done.14 = f32[16,16,1024]{2,1,0:T(8,128)} async-done(((f32[16,16,1024]{2,1,0:T(8,128)}), f32[16,16,1024]{2,1,0:T(8,128)}, u32[]{:S(2)}, u32[]{:S(2)}) %all-to-all-start.14) | async-done | bytes 1048608 | tf_op jit(solution)/shard_map/all_to_all | solution.py:100
  842.0 15.8 %all-to-all-done.8 = f32[16,16,1024]{2,1,0:T(8,128)S(1)} async-done(((f32[16,16,1024]{2,1,0:T(8,128)}), f32[16,16,1024]{2,1,0:T(8,128)S(1)}, u32[]{:S(2)}, u32[]{:S(2)}) %all-to-all-start.8) | async-done | bytes 1048608 | tf_op jit(solution)/shard_map/all_to_all | solution.py:100
  861.5 49.4 %all-reduce.32 = (f32[1024]{0:T(1024)}, f32[128,16]{0,1:T(8,128)}, f32[128,16]{0,1:T(8,128)}) all-reduce(f32[1024]{0:T(1024)S(1)} %get-tuple-element.100, f32[128,16]{0,1:T(8,128)S(1)} %pad_add_fusion, f32[128,16]{0,1:T(8,128)S(1)} %add_multiply_fusion), channel_id=1, replica_groups=mesh['ctx'=16,'ch'=8] {'ctx'}, use_global_device_ids=true, to_apply=%region_1.2 | all-reduce | flops 5120 | bytes 40960 | tf_op jit(solution)/shard_map/psum | solution.py:159
  (195 shorter events, 300.9 us)
Async XLA Ops:
  68.3 35.7 %all-to-all-start.3 = ((f32[16,16,1024]{2,1,0:T(8,128)}), f32[16,16,1024]{2,1,0:T(8,128)S(1)}, u32[]{:S(2)}, u32[]{:S(2)}) async-start(f32[16,16,1024]{2,1,0:T(8,128)} %multiply_add_fusion.5), calls=%async_computation.3 | async-start | bytes 2097152 | tf_op jit(solution)/shard_map/all_to_all | solution.py:45
  104.0 20.2 %all-to-all-start = ((f32[16,16,1024]{2,1,0:T(8,128)}), f32[16,16,1024]{2,1,0:T(8,128)S(1)}, u32[]{:S(2)}, u32[]{:S(2)}) async-start(f32[16,16,1024]{2,1,0:T(8,128)} %bitcast.1), calls=%async_computation | async-start | bytes 2097152 | tf_op jit(solution)/shard_map/all_to_all | solution.py:45
  124.2 20.4 %all-to-all-start.9 = ((f32[16,16,1024]{2,1,0:T(8,128)}), f32[16,16,1024]{2,1,0:T(8,128)S(1)}, u32[]{:S(2)}, u32[]{:S(2)}) async-start(f32[16,16,1024]{2,1,0:T(8,128)} %bitcast.548), calls=%async_computation.9 | async-start | bytes 2097152 | tf_op jit(solution)/shard_map/all_to_all | solution.py:45
  157.2 32.4 %all-to-all-start.5 = ((f32[32,16,1024]{2,1,0:T(8,128)}), f32[32,16,1024]{2,1,0:T(8,128)}, u32[]{:S(2)}, u32[]{:S(2)}) async-start(f32[32,16,1024]{2,1,0:T(8,128)} %copy.113), calls=%async_computation.5 | async-start | bytes 4194304 | tf_op jit(solution)/shard_map/all_to_all | solution.py:57
  189.5 32.3 %all-to-all-start.4 = ((f32[32,16,1024]{2,1,0:T(8,128)}), f32[32,16,1024]{2,1,0:T(8,128)}, u32[]{:S(2)}, u32[]{:S(2)}) async-start(f32[32,16,1024]{2,1,0:T(8,128)} %copy.110), calls=%async_computation.4 | async-start | bytes 4194304 | tf_op jit(solution)/shard_map/all_to_all | solution.py:56
  221.8 32.3 %all-to-all-start.10 = ((f32[32,16,1024]{2,1,0:T(8,128)}), f32[32,16,1024]{2,1,0:T(8,128)}, u32[]{:S(2)}, u32[]{:S(2)}) async-start(f32[32,16,1024]{2,1,0:T(8,128)} %copy.128), calls=%async_computation.10 | async-start | bytes 4194304 | tf_op jit(solution)/shard_map/all_to_all | solution.py:56
  254.2 32.4 %all-to-all-start.11 = ((f32[32,16,1024]{2,1,0:T(8,128)}), f32[32,16,1024]{2,1,0:T(8,128)}, u32[]{:S(2)}, u32[]{:S(2)}) async-start(f32[32,16,1024]{2,1,0:T(8,128)} %copy.131), calls=%async_computation.11 | async-start | bytes 4194304 | tf_op jit(solution)/shard_map/all_to_all | solution.py:57
  286.5 35.3 %all-to-all-start.2 = ((f32[32,16,1024]{2,1,0:T(8,128)}), f32[32,16,1024]{2,1,0:T(8,128)}, u32[]{:S(2)}, u32[]{:S(2)}) async-start(f32[32,16,1024]{2,1,0:T(8,128)} %copy.105), calls=%async_computation.2 | async-start | bytes 4194304 | tf_op jit(solution)/shard_map/all_to_all | solution.py:57
  321.9 44.5 %all-to-all-start.1 = ((f32[32,16,1024]{2,1,0:T(8,128)}), f32[32,16,1024]{2,1,0:T(8,128)}, u32[]{:S(2)}, u32[]{:S(2)}) async-start(f32[32,16,1024]{2,1,0:T(8,128)} %copy.102), calls=%async_computation.1 | async-start | bytes 4194304 | tf_op jit(solution)/shard_map/all_to_all | solution.py:56
  327.6 247.7 %all-reduce.36.cloned.1.call-start = ((), (), s32[]{:S(2)}) async-start(), calls=%async_computation.18 | async-start | bytes 8388608 | tf_op jit(solution)/shard_map/psum | solution.py:151
  597.7 32.9 %all-to-all-start.15 = ((f32[2,256,1024]{2,0,1:T(2,128)}), f32[2,256,1024]{2,0,1:T(2,128)}, u32[]{:S(2)}, u32[]{:S(2)}) async-start(f32[2,256,1024]{2,0,1:T(2,128)} %copy.142), calls=%async_computation.15 | async-start | bytes 4194304 | tf_op jit(solution)/shard_map/all_to_all | solution.py:91
  630.6 32.3 %all-to-all-start.16 = ((f32[2,256,1024]{2,0,1:T(2,128)}), f32[2,256,1024]{2,0,1:T(2,128)}, u32[]{:S(2)}, u32[]{:S(2)}) async-start(f32[2,256,1024]{2,0,1:T(2,128)} %copy.145), calls=%async_computation.16 | async-start | bytes 4194304 | tf_op jit(solution)/shard_map/all_to_all | solution.py:92
  663.0 32.7 %all-to-all-start.12 = ((f32[2,256,1024]{2,0,1:T(2,128)}), f32[2,256,1024]{2,0,1:T(2,128)}, u32[]{:S(2)}, u32[]{:S(2)}) async-start(f32[2,256,1024]{2,0,1:T(2,128)} %copy.136), calls=%async_computation.12 | async-start | bytes 4194304 | tf_op jit(solution)/shard_map/all_to_all | solution.py:91
  695.7 32.4 %all-to-all-start.13 = ((f32[2,256,1024]{2,0,1:T(2,128)}), f32[2,256,1024]{2,0,1:T(2,128)}, u32[]{:S(2)}, u32[]{:S(2)}) async-start(f32[2,256,1024]{2,0,1:T(2,128)} %copy.139), calls=%async_computation.13 | async-start | bytes 4194304 | tf_op jit(solution)/shard_map/all_to_all | solution.py:92
  728.1 32.3 %all-to-all-start.6 = ((f32[2,256,1024]{2,0,1:T(2,128)}), f32[2,256,1024]{2,0,1:T(2,128)}, u32[]{:S(2)}, u32[]{:S(2)}) async-start(f32[2,256,1024]{2,0,1:T(2,128)} %copy.120), calls=%async_computation.6 | async-start | bytes 4194304 | tf_op jit(solution)/shard_map/all_to_all | solution.py:91
  760.4 31.6 %all-to-all-start.7 = ((f32[2,256,1024]{2,0,1:T(2,128)}), f32[2,256,1024]{2,0,1:T(2,128)S(1)}, u32[]{:S(2)}, u32[]{:S(2)}) async-start(f32[2,256,1024]{2,0,1:T(2,128)} %copy.123), calls=%async_computation.7 | async-start | bytes 4194304 | tf_op jit(solution)/shard_map/all_to_all | solution.py:92
  792.0 23.8 %all-to-all-start.17 = ((f32[16,16,1024]{2,1,0:T(8,128)}), f32[16,16,1024]{2,1,0:T(8,128)}, u32[]{:S(2)}, u32[]{:S(2)}) async-start(f32[16,16,1024]{2,1,0:T(8,128)} %bitcast.201), calls=%async_computation.17 | async-start | bytes 2097152 | tf_op jit(solution)/shard_map/all_to_all | solution.py:100
  815.8 21.7 %all-to-all-start.14 = ((f32[16,16,1024]{2,1,0:T(8,128)}), f32[16,16,1024]{2,1,0:T(8,128)}, u32[]{:S(2)}, u32[]{:S(2)}) async-start(f32[16,16,1024]{2,1,0:T(8,128)} %bitcast.547), calls=%async_computation.14 | async-start | bytes 2097152 | tf_op jit(solution)/shard_map/all_to_all | solution.py:100
  824.3 33.4 %copy-start.26 = (bf16[256,1024]{1,0:T(8,128)(2,1)S(1)}, bf16[256,1024]{1,0:T(8,128)(2,1)}, u32[]{:S(2)}) copy-start(bf16[256,1024]{1,0:T(8,128)(2,1)} %param.10) | copy-start | bytes 1572868
  824.3 33.4 %copy-start.28 = (bf16[256,1024]{1,0:T(8,128)(2,1)S(1)}, bf16[256,1024]{1,0:T(8,128)(2,1)}, u32[]{:S(2)}) copy-start(bf16[256,1024]{1,0:T(8,128)(2,1)} %param.7) | copy-start | bytes 1572868
  824.3 33.4 %copy-start.30 = (bf16[256,1024]{1,0:T(8,128)(2,1)S(1)}, bf16[256,1024]{1,0:T(8,128)(2,1)}, u32[]{:S(2)}) copy-start(bf16[256,1024]{1,0:T(8,128)(2,1)} %param.9) | copy-start | bytes 1572868
  824.3 33.4 %copy-start.32 = (bf16[256,1024]{1,0:T(8,128)(2,1)S(1)}, bf16[256,1024]{1,0:T(8,128)(2,1)}, u32[]{:S(2)}) copy-start(bf16[256,1024]{1,0:T(8,128)(2,1)} %param.8) | copy-start | bytes 1572868
  824.4 33.4 %copy-start.35 = (f32[1024]{0:T(1024)S(1)}, f32[1024]{0:T(1024)}, u32[]{:S(2)}) copy-start(f32[1024]{0:T(1024)} %param.11) | copy-start | bytes 12292
  837.5 20.2 %all-to-all-start.8 = ((f32[16,16,1024]{2,1,0:T(8,128)}), f32[16,16,1024]{2,1,0:T(8,128)S(1)}, u32[]{:S(2)}, u32[]{:S(2)}) async-start(f32[16,16,1024]{2,1,0:T(8,128)} %bitcast.183), calls=%async_computation.8 | async-start | bytes 2097152 | tf_op jit(solution)/shard_map/all_to_all | solution.py:100
  (31 other events, 271.6 us)
Sparse Core Ops, SparseCore 0:
  388.6 186.7 all-reduce.35
where the time goes:
time: 929 us; the launch traced here: 918 us
  waiting for transfers between devices  439 us (47%)
  matrix products  152 us (16%)
  blocking collectives  106 us (11%)
  starting transfers between devices  106 us (11%)
  local copies, waits for them, and re-layouts  86 us (9%)
  between operations  15.1 us (2%)
  other arithmetic  13.5 us (1%)
    psum x1, waiting for transfers between devices, on_device(): total_re, total_im = lax.psum((own_re, own_im), 'ch')  157 us
    dot_general x24, matrix products, exact_einsum(): return jnp.einsum(form, first, second, precision=lax.Precision.HIGHEST)  121 us
    all_to_all x3, waiting for transfers between devices, signal_of(): lax.all_to_all(turned_re, 'ctx', split_axis=1, concat_axis=0, tiled=True)  71 us
    all_to_all x3, waiting for transfers between devices, signal_of(): lax.all_to_all(turned_im, 'ctx', split_axis=1, concat_axis=0, tiled=True)  61.8 us
    psum x1, blocking collectives, on_device(): lax.psum((part_residue, decay * part_decay, part_skip), 'ctx')  49.4 us
    all_to_all x3, waiting for transfers between devices, spectrum(): lax.all_to_all(turned_re, 'ctx', split_axis=0, concat_axis=1, tiled=True)  46.4 us
    all_to_all x3, waiting for transfers between devices, spectrum(): lax.all_to_all(turned_im, 'ctx', split_axis=0, concat_axis=1, tiled=True)  46.3 us
    dot_general x12, matrix products, exact_dot(): return jnp.dot(first, second, precision=lax.Precision.HIGHEST)  31.5 us
  transfers between devices with their start and end apart: 19, of which 16 were waited for; matrix products, arithmetic and copies ran while one was open for 20% of the time, Pallas kernels for 0%

commit v1 on v0

v1 whole, which is shorter than its diff:
```python
import functools

import jax
import jax.numpy as jnp
import numpy as np
from jax import lax
from jax.experimental import pallas as pl
from jax.experimental.pallas import tpu as pltpu
from jax.sharding import PartitionSpec as P

LANES = 128
ROWS = 8
VMEM = pl.BlockSpec(memory_space=pltpu.VMEM)
SMEM = pl.BlockSpec(memory_space=pltpu.SMEM)


def call(body, outs, limit_mib, cost, scratch=()):
    flops, moved = cost
    return lambda specs, *args: pl.pallas_call(
        body,
        out_shape=[jax.ShapeDtypeStruct(s, t) for s, t in outs],
        in_specs=list(specs),
        out_specs=[VMEM] * len(outs),
        scratch_shapes=list(scratch),
        compiler_params=pltpu.CompilerParams(vmem_limit_bytes=limit_mib * 2**20),
        cost_estimate=pl.CostEstimate(flops=flops, bytes_accessed=moved, transcendentals=0),
    )(*args)


def halves(table):
    high = table.astype(jnp.bfloat16)
    low = (table - high.astype(np.float64)).astype(jnp.bfloat16)
    return np.concatenate([high, high, low], axis=1)


def transform_tables(length):
    full = 2 * length
    wave = np.arange(length)[:, None]
    time = np.arange(length)[None, :]
    angle = 2.0 * np.pi * ((wave * time) % full) / full
    real, imag = np.cos(angle), -np.sin(angle)
    imag[0] = np.where(np.arange(length) % 2 == 0, 1.0, -1.0)
    weight = np.where(wave == 0, 1.0, 2.0) / full
    forward = np.concatenate([real, imag], axis=0)
    inverse = np.concatenate([weight * real, weight * imag], axis=0).T
    return halves(forward), halves(inverse)


def split_dot(table, signal):
    high = signal.astype(jnp.bfloat16)
    low = (signal - high.astype(jnp.float32)).astype(jnp.bfloat16)
    return jnp.dot(table, jnp.concatenate([high, low, high], axis=0), preferred_element_type=jnp.float32)


def row_iota(shape):
    return lax.broadcasted_iota(jnp.int32, shape, 0)


def spectral_product(left, right, conjugate):
    count = left.shape[0] // 2
    lre, lim, rre, rim = left[:count], left[count:], right[:count], right[count:]
    first = row_iota(lre.shape) == 0
    both = lim * rim
    cross = jnp.where(first, 0.0, both)
    if conjugate:
        real, imag = lre * rre + cross, lre * rim - lim * rre
    else:
        real, imag = lre * rre - cross, lre * rim + lim * rre
    return jnp.concatenate([real, jnp.where(first, both, imag)], axis=0)


def spread_body(decay_ref, residue_ref, out_ref):
    modes = decay_ref.shape[0]
    for block in range(out_ref.shape[0]):
        out_ref[block, :modes] = decay_ref[...]
        out_ref[block, modes:] = residue_ref[...]


def product_body(gate_ref, key_ref, value_ref, cot_ref, fwd_ref, inv_ref, x_ref, b_ref, xs_ref, bs_ref, gk_ref, sk_ref):
    width = 2 * LANES

    def step(block, carry):
        lanes = pl.ds(pl.multiple_of(block * width, width), width)
        x = key_ref[:, lanes].astype(jnp.float32) * value_ref[:, lanes].astype(jnp.float32)
        b = cot_ref[:, lanes].astype(jnp.float32) * gate_ref[:, lanes].astype(jnp.float32)
        x_ref[:, lanes] = x
        b_ref[:, lanes] = b
        total = jnp.sum(x * b, axis=0, keepdims=True)
        sk_ref[pl.ds(2 * block, 1), :] = total[:, :LANES]
        sk_ref[pl.ds(2 * block + 1, 1), :] = total[:, LANES:]
        xs = split_dot(fwd_ref[...], x)
        bs = split_dot(fwd_ref[...], b)
        xs_ref[:, lanes] = xs
        bs_ref[:, lanes] = bs
        gk_ref[:, lanes] = split_dot(inv_ref[...], spectral_product(xs, bs, True))
        return carry

    lax.fori_loop(0, x_ref.shape[1] // width, step, 0)


def moments(decay, upward, downward):
    modes = decay.shape[0]
    rates = [jnp.broadcast_to(decay[m : m + 1], (ROWS, LANES)) for m in range(modes)]
    step8 = [jnp.exp(-float(ROWS) * rate) for rate in rates]
    tiles = upward[0][1] if upward else downward[0][1]
    ups = [[None] * modes for _ in upward]
    downs = [[None] * modes for _ in downward]
    for tile in range(tiles):
        for sums, (fetch, _), place in [(s, f, tile) for s, f in zip(ups, upward)] + [
            (s, f, tiles - 1 - tile) for s, f in zip(downs, downward)
        ]:
            value = fetch(place)
            for m in range(modes):
                sums[m] = value if sums[m] is None else step8[m] * sums[m] + value
    phase = row_iota((ROWS, LANES)).astype(jnp.float32)
    up_weight = [jnp.exp(-rate * (ROWS - 1.0 - phase)) for rate in rates] if upward else []
    down_weight = [jnp.exp(-rate * phase) for rate in rates] if downward else []

    def gather(sums, weights):
        rows = [jnp.sum(s * w, axis=0, keepdims=True) for s, w in zip(sums, weights)]
        return jnp.concatenate(rows, axis=0)

    return [gather(s, up_weight) for s in ups], [gather(s, down_weight) for s in downs]


def turn_out(scratch_ref, out_ref, slot):
    owners = out_ref.shape[0]
    for group in range(scratch_ref.shape[0] // LANES):
        turned = scratch_ref[pl.ds(group * LANES, LANES), :].T
        out_ref[:, slot + group] = turned.reshape(owners, LANES // owners, LANES)


def state_body(par_ref, x_ref, b_ref, sk_ref, out_ref, rate_ref, sums_ref, rates_ref):
    blocks, modes = par_ref.shape[0], par_ref.shape[1] // 2
    tiles = x_ref.shape[0] // ROWS

    def step(block, carry):
        lanes = pl.ds(pl.multiple_of(block * LANES, LANES), LANES)
        decay = par_ref[block, :modes, :]
        (up,), (down,) = moments(
            decay,
            [(lambda tile: x_ref[pl.ds(tile * ROWS, ROWS), lanes], tiles)],
            [(lambda tile: b_ref[pl.ds(tile * ROWS, ROWS), lanes], tiles)],
        )
        start = pl.multiple_of(block * 2 * modes, 2 * modes)
        sums_ref[pl.ds(start, 2 * modes), :] = jnp.concatenate([up, down], axis=0)
        rates_ref[pl.ds(start, 2 * modes), :] = jnp.concatenate([decay, decay], axis=0)
        return carry

    lax.fori_loop(0, blocks, step, 0)
    turn_out(sums_ref, out_ref, 0)
    groups = sums_ref.shape[0] // LANES
    for owner in range(out_ref.shape[0]):
        out_ref[owner, groups, :blocks] = sk_ref[...]
    for group in range(groups):
        rate_ref[group] = rates_ref[pl.ds(group * LANES, LANES), :].T


def slope_body(par_ref, x_ref, b_ref, gk_ref, qa_ref, qb_ref, suma_ref, sumb_ref):
    blocks, modes = par_ref.shape[0], par_ref.shape[1] // 2
    positions = x_ref.shape[0]
    tiles = positions // ROWS
    half = modes // 2

    def step(block, carry):
        lanes = pl.ds(pl.multiple_of(block * LANES, LANES), LANES)
        phase = row_iota((ROWS, LANES)).astype(jnp.float32)

        def late(tile):
            return (positions - 1.0 - tile * ROWS - phase) * x_ref[pl.ds(tile * ROWS, ROWS), lanes]

        def early(ref):
            return lambda tile: (tile * float(ROWS) + phase) * ref[pl.ds(tile * ROWS, ROWS), lanes]

        for part in range(2):
            decay = par_ref[block, part * half : (part + 1) * half, :]
            (up,), (down, plain, slope) = moments(
                decay,
                [(late, tiles)],
                [
                    (early(b_ref), tiles),
                    (lambda tile: gk_ref[pl.ds(tile * ROWS, ROWS), lanes], tiles),
                    (early(gk_ref), tiles),
                ],
            )
            start = pl.multiple_of(block * 2 * modes, 2 * modes) + part * half
            suma_ref[pl.ds(start, half), :] = down
            suma_ref[pl.ds(start + modes, half), :] = up
            sumb_ref[pl.ds(start, half), :] = plain
            sumb_ref[pl.ds(start + modes, half), :] = slope
        return carry

    lax.fori_loop(0, blocks, step, 0)
    turn_out(suma_ref, qa_ref, 0)
    turn_out(sumb_ref, qb_ref, 0)


def tree(values):
    while len(values) > 1:
        values = [a + b for a, b in zip(values[::2], values[1::2])]
    return values[0]


def local_body(par_ref, skip_ref, x_ref, b_ref, xs_ref, bs_ref, fwd_ref, inv_ref, pre_ref, gp_ref, k_ref):
    modes = par_ref.shape[1] // 2
    width = 2 * LANES
    tiles = x_ref.shape[0] // ROWS

    def step(pair, carry):
        phase = row_iota((ROWS, LANES)).astype(jnp.float32)
        for side in range(2):
            block = 2 * pair + side
            decay, residue = par_ref[block, :modes, :], par_ref[block, modes:, :]
            weight = residue * jnp.sqrt(decay)
            rates = [jnp.broadcast_to(decay[m : m + 1], (ROWS, LANES)) for m in range(modes)]
            step8 = [jnp.exp(-float(ROWS) * rate) for rate in rates]
            terms = [weight[m : m + 1] * jnp.exp(-rates[m] * phase) for m in range(modes)]
            for tile in range(tiles):
                k_ref[pl.ds(tile * ROWS, ROWS), side * LANES : (side + 1) * LANES] = tree(terms)
                if tile < tiles - 1:
                    terms = [t * s for t, s in zip(terms, step8)]
        lanes = pl.ds(pl.multiple_of(pair * width, width), width)
        skip = jnp.concatenate([skip_ref[pl.ds(2 * pair, 1), :], skip_ref[pl.ds(2 * pair + 1, 1), :]], axis=1)
        ks = split_dot(fwd_ref[...], k_ref[...])
        conv = split_dot(inv_ref[...], spectral_product(ks, xs_ref[:, lanes], False))
        pre_ref[:, lanes] = conv + skip * x_ref[:, lanes]
        corr = split_dot(inv_ref[...], spectral_product(ks, bs_ref[:, lanes], True))
        gp_ref[:, lanes] = corr + skip * b_ref[:, lanes]
        return carry

    lax.fori_loop(0, x_ref.shape[1] // width, step, 0)


def lane_is_first(shape, modes):
    return lax.broadcasted_iota(jnp.int32, shape, 1) % (2 * modes) < modes


def scan_body(index_ref, s_ref, rate_ref, qa_ref, qb_ref, out_ref, acc_ref, skip_ref, *, modes, length):
    chunks = s_ref.shape[0]
    groups = rate_ref.shape[0]
    rows = s_ref.shape[2]
    start = pl.multiple_of(index_ref[0] * rows, rows)
    first = lane_is_first((rows, LANES), modes)
    zero = jnp.zeros((rows, LANES), jnp.float32)
    for group in range(groups):
        alpha = jnp.exp(-float(length) * rate_ref[group, pl.ds(start, rows), :])
        before, lead, total0, total1 = zero, zero, zero, zero
        heads = []
        for k in range(chunks):
            value = s_ref[k, group]
            later = pltpu.roll(value, LANES - modes, 1)
            heads.append(before)
            total0 += before * later
            total1 += (lead + before) * later
            lead = alpha * (lead + float(length) * before)
            before = alpha * before + value
        after = zero
        for k in reversed(range(chunks)):
            out_ref[k, group] = jnp.where(first, heads[k], after)
            after = alpha * after + s_ref[k, group]
        acc_ref[group] = jnp.where(first, total0, pltpu.roll(total1, modes, 1))
    for k in range(chunks):
        out_ref[k, groups : 2 * groups] = qa_ref[k]
        out_ref[k, 2 * groups : 3 * groups] = qb_ref[k]
    skip_ref[...] = tree([s_ref[k, groups, : skip_ref.shape[0]] for k in range(chunks)])


def slope_sum_body(index_ref, r_ref, own_ref, acc_ref, rate_ref, out_ref, *, modes):
    chunks, groups, rows = r_ref.shape[0], rate_ref.shape[0], r_ref.shape[2]
    start = pl.multiple_of(index_ref[0] * rows, rows)
    first = lane_is_first((rows, LANES), modes)
    blocks = out_ref.shape[1]
    for group in range(groups):
        cross = tree([own_ref[k, group] * r_ref[k, groups + group] for k in range(chunks)])
        inner = tree([r_ref[k, 2 * groups + group] for k in range(chunks)])
        cross = jnp.where(first, 0.0, cross + pltpu.roll(cross, modes, 1))
        total = inner + jnp.exp(-rate_ref[group, pl.ds(start, rows), :]) * (acc_ref[group] + cross)
        for block in range(group * (blocks // groups), (group + 1) * (blocks // groups)):
            for owner in range(out_ref.shape[0]):
                out_ref[owner, block] = total


def final_body(index_ref, g_ref, residue_ref, decay_ref, gres_ref, gdec_ref, turned_ref):
    modes = residue_ref.shape[0]
    blocks = g_ref.shape[1]
    turned_ref[...] = tree([g_ref[:, block] for block in range(blocks)]).reshape(LANES, LANES).T
    place = pl.multiple_of(lax.rem(index_ref[0], LANES // (2 * modes)) * (2 * modes), 2 * modes)
    plain, slope = turned_ref[pl.ds(place, modes), :], turned_ref[pl.ds(place + modes, modes), :]
    decay = decay_ref[...]
    root = jnp.sqrt(decay)
    gres_ref[...] = root * plain
    gdec_ref[...] = residue_ref[...] * root * (0.5 * plain - decay * slope)


def out_body(par_ref, r_ref, pre_ref, gp_ref, gate_ref, key_ref, value_ref, cot_ref, mixed_ref, ggate_ref, gkey_ref, gvalue_ref, hb_ref):
    blocks, modes = par_ref.shape[0], par_ref.shape[1] // 2
    groups = hb_ref.shape[0] // LANES
    pack = 2 * ROWS
    for group in range(groups):
        hb_ref[pl.ds(group * LANES, LANES), :] = r_ref[:, group].reshape(LANES, LANES).T

    def step(block, carry):
        lanes = pl.ds(pl.multiple_of(block * LANES, LANES), LANES)
        phase = row_iota((ROWS, LANES)).astype(jnp.float32)
        decay, residue = par_ref[block, :modes, :], par_ref[block, modes:, :]
        start = pl.multiple_of(block * 2 * modes, 2 * modes)
        weight = residue * jnp.sqrt(decay)
        first = weight * hb_ref[pl.ds(start, modes), :]
        last = weight * hb_ref[pl.ds(start + modes, modes), :]
        rates = [jnp.broadcast_to(decay[m : m + 1], (ROWS, LANES)) for m in range(modes)]
        step8 = [jnp.exp(-float(ROWS) * rate) for rate in rates]
        terms = [first[m : m + 1] * jnp.exp(-rates[m] * (phase + 1.0)) for m in range(modes)]
        count = pre_ref.shape[0] // pack
        for place in range(count):
            lower = tree(terms)
            terms = [t * s for t, s in zip(terms, step8)]
            upper = tree(terms)
            terms = [t * s for t, s in zip(terms, step8)]
            rows = pl.ds(place * pack, pack)
            pre = pre_ref[rows, lanes] + jnp.concatenate([lower, upper], axis=0)
            mixed_ref[rows, lanes] = (gate_ref[rows, lanes].astype(jnp.float32) * pre).astype(jnp.bfloat16)
            ggate_ref[rows, lanes] = (cot_ref[rows, lanes].astype(jnp.float32) * pre).astype(jnp.bfloat16)
        terms = [last[m : m + 1] * jnp.exp(-rates[m] * (ROWS - phase)) for m in range(modes)]
        for place in reversed(range(count)):
            upper = tree(terms)
            terms = [t * s for t, s in zip(terms, step8)]
            lower = tree(terms)
            terms = [t * s for t, s in zip(terms, step8)]
            rows = pl.ds(place * pack, pack)
            grad = gp_ref[rows, lanes] + jnp.concatenate([lower, upper], axis=0)
            gkey_ref[rows, lanes] = (grad * value_ref[rows, lanes].astype(jnp.float32)).astype(jnp.bfloat16)
            gvalue_ref[rows, lanes] = (grad * key_ref[rows, lanes].astype(jnp.float32)).astype(jnp.bfloat16)
        return carry

    lax.fori_loop(0, blocks, step, 0)


def on_device(gate_in, key_in, value_in, cotangent, skip, residue, decay):
    f32, bf16 = jnp.float32, jnp.bfloat16
    owners = lax.axis_size("ctx")
    blocks = lax.axis_size("ch")
    length, channels = gate_in.shape
    filters, modes = residue.shape
    share = filters // owners
    groups = blocks * 2 * modes // LANES
    place = lax.axis_index("ctx").astype(jnp.int32).reshape(1)
    column = lax.axis_index("ch").astype(jnp.int32).reshape(1)
    forward, inverse = (jnp.asarray(t) for t in transform_tables(length))
    whole = (length, channels)
    size = length * channels

    (sent,) = call(spread_body, [((blocks, 2 * modes, LANES), f32)], 8, (0, 10**5))([VMEM] * 2, decay.T, residue.T)
    params = lax.all_to_all(sent, "ch", 0, 0, tiled=True)

    x, b, xs, bs, gk, sk = call(
        product_body,
        [(whole, f32), (whole, f32), ((2 * length, channels), f32), ((2 * length, channels), f32), (whole, f32), ((blocks, LANES), f32)],
        32,
        (18 * length * size, 36 * size),
    )([VMEM] * 6, gate_in, key_in, value_in, cotangent, forward, inverse)

    states, rates = call(
        state_body,
        [((owners, groups + 1, share, LANES), f32), ((groups, LANES, LANES), f32)],
        16,
        (64 * size, 8 * size),
        [pltpu.VMEM((groups * LANES, LANES), f32)] * 2,
    )([VMEM] * 4, params, x, b, sk)
    states = lax.all_to_all(states, "ctx", 0, 0, tiled=True)

    slopes, inner = call(
        slope_body,
        [((owners, groups, share, LANES), f32)] * 2,
        16,
        (128 * size, 12 * size),
        [pltpu.VMEM((groups * LANES, LANES), f32)] * 2,
    )([VMEM] * 4, params, x, b, gk)

    bundle, acc, grad_skip = call(
        functools.partial(scan_body, modes=modes, length=length),
        [((owners, 3 * groups, share, LANES), f32), ((groups, share, LANES), f32), ((blocks, LANES), f32)],
        8,
        (10**5, 10**6),
    )([SMEM] + [VMEM] * 4, place, states, rates, slopes, inner)
    arrived = lax.all_to_all(bundle, "ctx", 0, 0, tiled=True)

    pre, gp = call(
        local_body,
        [(whole, f32)] * 2,
        32,
        (18 * length * size, 36 * size),
        [pltpu.VMEM((length, 2 * LANES), f32)],
    )([VMEM] * 8, params, skip.reshape(blocks, LANES), x, b, xs, bs, forward, inverse)

    (grads,) = call(
        functools.partial(slope_sum_body, modes=modes),
        [((owners, blocks, share, LANES), f32)],
        8,
        (10**5, 10**6),
    )([SMEM] + [VMEM] * 4, place, arrived, bundle, acc, rates)
    grads = lax.all_to_all(grads.reshape(owners * blocks, share, LANES), ("ctx", "ch"), 0, 0, tiled=True)

    mixed, grad_gate, grad_key, grad_value = call(
        out_body,
        [(whole, bf16)] * 4,
        24,
        (64 * size, 20 * size),
        [pltpu.VMEM((groups * LANES, LANES), f32)],
    )([VMEM] * 8, params, arrived, pre, gp, gate_in, key_in, value_in, cotangent)

    grad_residue, grad_log_decay = call(
        final_body, [((modes, filters), f32)] * 2, 8, (10**5, 10**6), [pltpu.VMEM((LANES, LANES), f32)]
    )([SMEM] + [VMEM] * 3, column, grads.reshape(owners, blocks, share, LANES), residue.T, decay.T)
    return (mixed, grad_gate, grad_key, grad_value, grad_skip.reshape(channels), grad_residue.T, grad_log_decay.T)


def solution(mesh):
    rows = P("ctx", "ch")
    return jax.shard_map(
        on_device,
        mesh=mesh,
        in_specs=(rows, rows, rows, rows, P("ch"), P("ch", None), P("ch", None)),
        out_specs=(rows, rows, rows, rows, P("ch"), P("ch", None), P("ch", None)),
        check_vma=False,
    )
```

time: 929 us -> 87 us (0.09); the launches traced: 918 us -> 86.1 us
  waiting for transfers between devices: 439 us -> 0.01 us
  matrix products: 152 us -> 0 us
  blocking collectives: 106 us -> 13.9 us
  starting transfers between devices: 106 us -> 22.7 us
  local copies, waits for them, and re-layouts: 86 us -> 23 us
  Pallas kernels: 0 us -> 25.6 us
  between operations: 15.1 us -> 0.82 us
  other arithmetic: 13.5 us -> 0 us
    all_to_all x18 -> x3, waiting for transfers between devices: 282 us -> 0.01 us  [the longest x1 0.01 us: on_device(): params = lax.all_to_all(sent, 'ch', 0, 0, tiled=True)]
    psum x1 -> x0, waiting for transfers between devices: 157 us -> none  [on_device(): total_re, total_im = lax.psum((own_re, own_im), 'ch')]
    dot_general x36 -> x0, matrix products: 152 us -> none  [the longest x24 121 us: exact_einsum(): return jnp.einsum(form, first, second, precision=lax.Precision.HIGHEST)]
    all_to_all x18 -> x3, starting transfers between devices: 106 us -> 22.7 us  [the longest x1 8.86 us: on_device(): lax.all_to_all(grads.reshape(owners * blocks, share, LANES), ('ctx', 'ch'...]
    all_gather x2 -> x0, blocking collectives: 57 us -> none  [the longest x1 28.9 us: on_device(): lax.all_gather(decay, 'ch', axis=0, tiled=True)]
    psum x1 -> x0, blocking collectives: 49.4 us -> none  [on_device(): lax.psum((part_residue, decay * part_decay, part_skip), 'ctx')]
    all_to_all x18 -> x0, local copies, waits for them, and re-layouts: 26.9 us -> none  [the longest x6 7.51 us: signal_of(): lax.all_to_all(turned_re, 'ctx', split_axis=1, concat_axis=0, tiled=True)]
    pallas_call x0 -> x9, Pallas kernels: none -> 25.6 us  [call(): pl.pallas_call(body, out_shape=[jax.ShapeDtypeStruct(s, t) for s, t in ou...]
  transfers between devices with their start and end apart: 19 -> 3, of which waited for: 16 -> 0; matrix products, arithmetic and copies ran while one was open for 20% -> 0% of each run, Pallas kernels for 0% -> 24%
where the time goes in v1:
time: 87 us; the launch traced here: 86.1 us
  Pallas kernels  25.6 us (29%)
  local copies, waits for them, and re-layouts  23 us (26%)
  starting transfers between devices  22.7 us (26%)
  blocking collectives  13.9 us (16%)
    pallas_call x9, Pallas kernels, call(): pl.pallas_call(body, out_shape=[jax.ShapeDtypeStruct(s, t) for s, t in ou...  25.6 us
    unnamed x60, local copies, waits for them, and re-layouts  23 us
    all_to_all x1, blocking collectives, on_device(): arrived = lax.all_to_all(bundle, 'ctx', 0, 0, tiled=True)  13.9 us
    all_to_all x1, starting transfers between devices, on_device(): lax.all_to_all(grads.reshape(owners * blocks, share, LANES), ('ctx', 'ch'...  8.86 us
    all_to_all x1, starting transfers between devices, on_device(): params = lax.all_to_all(sent, 'ch', 0, 0, tiled=True)  7.48 us
    all_to_all x1, starting transfers between devices, on_device(): states = lax.all_to_all(states, 'ctx', 0, 0, tiled=True)  6.39 us
  transfers between devices with their start and end apart: 3, of which 0 were waited for; matrix products, arithmetic and copies ran while one was open for 0% of the time, Pallas kernels for 24%

profile of v1, /device:TPU:1, one launch (start us, length us, event | category | flops | bytes accessed | tf_op | source)
XLA Modules:
  0.0 86.1 jit_solution(12304421457872070467)
XLA Ops:
  2.7 7.5 %all-to-all-start = ((f32[8,32,128]{2,1,0:T(8,128)}), f32[8,32,128]{2,1,0:T(8,128)S(1)}, u32[]{:S(2)}, u32[]{:S(2)}) async-start(f32[8,32,128]{2,1,0:T(8,128)} %shard_map.144), calls=%async_computation | async-start | bytes 262144 | tf_op jit(solution)/shard_map/all_to_all | solution.py:353
  10.2 1.1 %copy-done.5 = bf16[512,768]{1,0:T(8,128)(2,1)S(1)} copy-done((bf16[512,768]{1,0:T(8,128)(2,1)S(1)}, bf16[512,768]{1,0:T(8,128)(2,1)}, u32[]{:S(2)}) %copy-start.5) | copy-done | bytes 786456
  11.3 1.1 %copy-done.7 = bf16[256,1536]{1,0:T(8,128)(2,1)S(1)} copy-done((bf16[256,1536]{1,0:T(8,128)(2,1)S(1)}, bf16[256,1536]{1,0:T(8,128)(2,1)}, u32[]{:S(2)}) %copy-start.7) | copy-done | bytes 786456
  12.4 1.0 %copy-done.9 = bf16[256,1024]{1,0:T(8,128)(2,1)S(1)} copy-done((bf16[256,1024]{1,0:T(8,128)(2,1)S(1)}, bf16[256,1024]{1,0:T(8,128)(2,1)}, u32[]{:S(2)}) %copy-start.9) | copy-done | bytes 524312
  13.5 1.0 %copy-done.11 = bf16[256,1024]{1,0:T(8,128)(2,1)S(1)} copy-done((bf16[256,1024]{1,0:T(8,128)(2,1)S(1)}, bf16[256,1024]{1,0:T(8,128)(2,1)}, u32[]{:S(2)}) %copy-start.11) | copy-done | bytes 524312
  14.5 1.0 %copy-done.13 = bf16[256,1024]{1,0:T(8,128)(2,1)S(1)} copy-done((bf16[256,1024]{1,0:T(8,128)(2,1)S(1)}, bf16[256,1024]{1,0:T(8,128)(2,1)}, u32[]{:S(2)}) %copy-start.13) | copy-done | bytes 524312
  15.6 1.0 %copy-done.15 = bf16[256,1024]{1,0:T(8,128)(2,1)S(1)} copy-done((bf16[256,1024]{1,0:T(8,128)(2,1)S(1)}, bf16[256,1024]{1,0:T(8,128)(2,1)}, u32[]{:S(2)}) %copy-start.15) | copy-done | bytes 524312
  16.6 5.4 %shard_map.145 = (f32[256,1024]{1,0:T(8,128)S(1)}, f32[256,1024]{1,0:T(8,128)S(1)}, f32[512,1024]{1,0:T(8,128)S(1)}, f32[512,1024]{1,0:T(8,128)S(1)}, f32[256,1024]{1,0:T(8,128)S(1)}, /*index=5*/f32[8,128]{1,0:T(8,128)S(1)}) custom-call(bf16[256,1024]{1,0:T(8,128)(2,1)S(1)} %copy-done.9, bf16[256,1024]{1,0:T(8,128)(2,1)S(1)} %copy-done.11, ...), custom_call_target="tpu_custom_call" | custom-call | flops 1207959552 | bytes 9437184 | tf_op jit(solution)/shard_map/pallas_call | solution.py:19
  22.1 1.4 %copy-done = f32[512,1024]{1,0:T(8,128)} copy-done((f32[512,1024]{1,0:T(8,128)}, f32[512,1024]{1,0:T(8,128)S(1)}, u32[]{:S(2)}) %copy-start) | copy-done | bytes 2097176
  23.4 1.3 %copy-done.2 = f32[512,1024]{1,0:T(8,128)} copy-done((f32[512,1024]{1,0:T(8,128)}, f32[512,1024]{1,0:T(8,128)S(1)}, u32[]{:S(2)}) %copy-start.2) | copy-done | bytes 2097176
  24.8 2.7 %shard_map.146 = (f32[16,3,8,128]{3,2,1,0:T(8,128)S(1)}, f32[2,128,128]{2,1,0:T(8,128)S(1)}) custom-call(f32[8,32,128]{2,1,0:T(8,128)S(1)} %all-to-all-done.par_ref, f32[256,1024]{1,0:T(8,128)S(1)} %get-tuple-element.28.x_ref, f32[256,1024]{1,0:T(8,128)S(1)} %get-tuple-element.29.b_ref, f32[8,128]{1,0:T(8,128)S(1)} %get-tuple-element.30.sk_ref), custom_call_target="tpu_custom_call" | custom-call | flops 16777216 | bytes 2097152 | tf_op jit(solution)/shard_map/pallas_call | solution.py:19
  28.8 6.4 %all-to-all-start.1 = ((f32[16,3,8,128]{3,2,1,0:T(8,128)}), f32[16,3,8,128]{3,2,1,0:T(8,128)S(1)}, u32[]{:S(2)}, u32[]{:S(2)}) async-start(f32[16,3,8,128]{3,2,1,0:T(8,128)} %copy-done.20), calls=%async_computation.1 | async-start | bytes 393216 | tf_op jit(solution)/shard_map/all_to_all | solution.py:369
  35.2 5.6 %shard_map.147 = (f32[16,2,8,128]{3,2,1,0:T(8,128)S(1)}, f32[16,2,8,128]{3,2,1,0:T(8,128)S(1)}) custom-call(f32[8,32,128]{2,1,0:T(8,128)S(1)} %all-to-all-done.par_ref, f32[256,1024]{1,0:T(8,128)S(1)} %get-tuple-element.28.x_ref, f32[256,1024]{1,0:T(8,128)S(1)} %get-tuple-element.29.b_ref, f32[256,1024]{1,0:T(8,128)S(1)} %get-tuple-element.33.gk_ref), custom_call_target="tpu_custom_call" | custom-call | flops 33554432 | bytes 3145728 | tf_op jit(solution)/shard_map/pallas_call | solution.py:19
  42.2 0.9 %copy-done.18 = f32[2,128,128]{2,1,0:T(8,128)S(1)} copy-done((f32[2,128,128]{2,1,0:T(8,128)S(1)}, f32[2,128,128]{2,1,0:T(8,128)}, u32[]{:S(2)}) %copy-start.18) | copy-done | bytes 131096
  43.1 0.9 %copy-done.22 = f32[16,2,8,128]{3,2,1,0:T(8,128)S(1)} copy-done((f32[16,2,8,128]{3,2,1,0:T(8,128)S(1)}, f32[16,2,8,128]{3,2,1,0:T(8,128)}, u32[]{:S(2)}) %copy-start.22) | copy-done | bytes 131096
  45.6 13.9 %all_to_all.20.r_ref = f32[16,6,8,128]{3,2,1,0:T(8,128)S(1)} all-to-all(f32[16,6,8,128]{3,2,1,0:T(8,128)S(1)} %get-tuple-element.36.own_ref), channel_id=1, replica_groups=mesh['ctx'=16,'ch'=8] {'ctx'}, dimensions={0} | all-to-all | bytes 786432 | tf_op jit(solution)/shard_map/all_to_all | solution.py:385
  59.5 0.9 %copy-done.19 = f32[2,128,128]{2,1,0:T(8,128)S(1)} copy-done((f32[2,128,128]{2,1,0:T(8,128)S(1)}, f32[2,128,128]{2,1,0:T(8,128)}, u32[]{:S(2)}) %copy-start.19) | copy-done | bytes 131096
  61.3 8.9 %all-to-all-start.3 = ((f32[128,8,128]{2,1,0:T(8,128)}), f32[128,8,128]{2,1,0:T(8,128)S(1)}, u32[]{:S(2)}, u32[]{:S(2)}) async-start(f32[128,8,128]{2,1,0:T(8,128)} %bitcast.11), calls=%async_computation.3 | async-start | bytes 1048576 | tf_op jit(solution)/shard_map/all_to_all | solution.py:401
  70.2 1.6 %copy-done.1 = f32[512,1024]{1,0:T(8,128)S(1)} copy-done((f32[512,1024]{1,0:T(8,128)S(1)}, f32[512,1024]{1,0:T(8,128)}, u32[]{:S(2)}) %copy-start.1) | copy-done | bytes 2097176
  71.8 1.6 %copy-done.3 = f32[512,1024]{1,0:T(8,128)S(1)} copy-done((f32[512,1024]{1,0:T(8,128)S(1)}, f32[512,1024]{1,0:T(8,128)}, u32[]{:S(2)}) %copy-start.3) | copy-done | bytes 2097176
  73.4 1.1 %copy-done.6 = bf16[512,768]{1,0:T(8,128)(2,1)S(1)} copy-done((bf16[512,768]{1,0:T(8,128)(2,1)S(1)}, bf16[512,768]{1,0:T(8,128)(2,1)}, u32[]{:S(2)}) %copy-start.6) | copy-done | bytes 786456
  74.5 1.1 %copy-done.8 = bf16[256,1536]{1,0:T(8,128)(2,1)S(1)} copy-done((bf16[256,1536]{1,0:T(8,128)(2,1)S(1)}, bf16[256,1536]{1,0:T(8,128)(2,1)}, u32[]{:S(2)}) %copy-start.8) | copy-done | bytes 786456
  75.7 5.3 %shard_map.149 = (f32[256,1024]{1,0:T(8,128)S(1)}, f32[256,1024]{1,0:T(8,128)S(1)}) custom-call(f32[8,32,128]{2,1,0:T(8,128)S(1)} %all-to-all-done.par_ref, f32[8,128]{1,0:T(8,128)S(1)} %bitcast.16, f32[256,1024]{1,0:T(8,128)S(1)} %get-tuple-element.28.x_ref, f32[256,1024]{1,0:T(8,128)S(1)} %get-tuple-element.29.b_ref, f32[512,1024]{1,0:T(8,128)S(1)} %copy-done.1, ...), custom_call_target="tpu_custom_call" | custom-call | flops 1207959552 | bytes 9437184 | tf_op jit(solution)/shard_map/pallas_call | solution.py:19
  81.1 4.3 %shard_map.150 = (bf16[256,1024]{1,0:T(8,128)(2,1)}, bf16[256,1024]{1,0:T(8,128)(2,1)}, bf16[256,1024]{1,0:T(8,128)(2,1)}, bf16[256,1024]{1,0:T(8,128)(2,1)}) custom-call(f32[8,32,128]{2,1,0:T(8,128)S(1)} %all-to-all-done.par_ref, f32[16,6,8,128]{3,2,1,0:T(8,128)S(1)} %all_to_all.20.r_ref, f32[256,1024]{1,0:T(8,128)S(1)} %get-tuple-element.39.pre_ref, ...), custom_call_target="tpu_custom_call" | custom-call | flops 16777216 | bytes 5242880 | tf_op jit(solution)/shard_map/pallas_call | solution.py:19
  (52 shorter events, 8.0 us)
Async XLA Ops:
  2.7 22.1 %all-to-all-start = ((f32[8,32,128]{2,1,0:T(8,128)}), f32[8,32,128]{2,1,0:T(8,128)S(1)}, u32[]{:S(2)}, u32[]{:S(2)}) async-start(f32[8,32,128]{2,1,0:T(8,128)} %shard_map.144), calls=%async_computation | async-start | bytes 262144 | tf_op jit(solution)/shard_map/all_to_all | solution.py:353
  10.2 1.1 %copy-start.5 = (bf16[512,768]{1,0:T(8,128)(2,1)S(1)}, bf16[512,768]{1,0:T(8,128)(2,1)}, u32[]{:S(2)}) copy-start(bf16[512,768]{1,0:T(8,128)(2,1)} %constant.13.clone.fwd_ref) | copy-start | bytes 2359300
  11.3 1.1 %copy-start.7 = (bf16[256,1536]{1,0:T(8,128)(2,1)S(1)}, bf16[256,1536]{1,0:T(8,128)(2,1)}, u32[]{:S(2)}) copy-start(bf16[256,1536]{1,0:T(8,128)(2,1)} %constant.14.clone.inv_ref) | copy-start | bytes 2359300
  12.4 1.0 %copy-start.9 = (bf16[256,1024]{1,0:T(8,128)(2,1)S(1)}, bf16[256,1024]{1,0:T(8,128)(2,1)}, u32[]{:S(2)}) copy-start(bf16[256,1024]{1,0:T(8,128)(2,1)} %gate_ref.3) | copy-start | bytes 1572868
  13.5 1.0 %copy-start.11 = (bf16[256,1024]{1,0:T(8,128)(2,1)S(1)}, bf16[256,1024]{1,0:T(8,128)(2,1)}, u32[]{:S(2)}) copy-start(bf16[256,1024]{1,0:T(8,128)(2,1)} %key_ref.3) | copy-start | bytes 1572868
  14.5 1.0 %copy-start.13 = (bf16[256,1024]{1,0:T(8,128)(2,1)S(1)}, bf16[256,1024]{1,0:T(8,128)(2,1)}, u32[]{:S(2)}) copy-start(bf16[256,1024]{1,0:T(8,128)(2,1)} %value_ref.3) | copy-start | bytes 1572868
  15.6 1.0 %copy-start.15 = (bf16[256,1024]{1,0:T(8,128)(2,1)S(1)}, bf16[256,1024]{1,0:T(8,128)(2,1)}, u32[]{:S(2)}) copy-start(bf16[256,1024]{1,0:T(8,128)(2,1)} %cot_ref.3) | copy-start | bytes 1572868
  22.1 1.4 %copy-start = (f32[512,1024]{1,0:T(8,128)}, f32[512,1024]{1,0:T(8,128)S(1)}, u32[]{:S(2)}) copy-start(f32[512,1024]{1,0:T(8,128)S(1)} %get-tuple-element.37.xs_ref) | copy-start | bytes 6291460
  23.4 1.3 %copy-start.2 = (f32[512,1024]{1,0:T(8,128)}, f32[512,1024]{1,0:T(8,128)S(1)}, u32[]{:S(2)}) copy-start(f32[512,1024]{1,0:T(8,128)S(1)} %get-tuple-element.38.bs_ref) | copy-start | bytes 6291460
  28.8 13.3 %all-to-all-start.1 = ((f32[16,3,8,128]{3,2,1,0:T(8,128)}), f32[16,3,8,128]{3,2,1,0:T(8,128)S(1)}, u32[]{:S(2)}, u32[]{:S(2)}) async-start(f32[16,3,8,128]{3,2,1,0:T(8,128)} %copy-done.20), calls=%async_computation.1 | async-start | bytes 393216 | tf_op jit(solution)/shard_map/all_to_all | solution.py:369
  42.2 28.0 %copy-start.29 = (f32[1024]{0:T(1024)S(1)}, f32[1024]{0:T(1024)}, u32[]{:S(2)}) copy-start(f32[1024]{0:T(1024)} %param.13) | copy-start | bytes 12292
  42.2 0.9 %copy-start.18 = (f32[2,128,128]{2,1,0:T(8,128)S(1)}, f32[2,128,128]{2,1,0:T(8,128)}, u32[]{:S(2)}) copy-start(f32[2,128,128]{2,1,0:T(8,128)} %copy-done.17) | copy-start | bytes 393220
  59.5 0.9 %copy-start.19 = (f32[2,128,128]{2,1,0:T(8,128)S(1)}, f32[2,128,128]{2,1,0:T(8,128)}, u32[]{:S(2)}) copy-start(f32[2,128,128]{2,1,0:T(8,128)} %copy-done.17) | copy-start | bytes 393220
  61.3 24.0 %all-to-all-start.3 = ((f32[128,8,128]{2,1,0:T(8,128)}), f32[128,8,128]{2,1,0:T(8,128)S(1)}, u32[]{:S(2)}, u32[]{:S(2)}) async-start(f32[128,8,128]{2,1,0:T(8,128)} %bitcast.11), calls=%async_computation.3 | async-start | bytes 1048576 | tf_op jit(solution)/shard_map/all_to_all | solution.py:401
  70.2 1.6 %copy-start.1 = (f32[512,1024]{1,0:T(8,128)S(1)}, f32[512,1024]{1,0:T(8,128)}, u32[]{:S(2)}) copy-start(f32[512,1024]{1,0:T(8,128)} %copy-done) | copy-start | bytes 6291460
  71.8 1.6 %copy-start.3 = (f32[512,1024]{1,0:T(8,128)S(1)}, f32[512,1024]{1,0:T(8,128)}, u32[]{:S(2)}) copy-start(f32[512,1024]{1,0:T(8,128)} %copy-done.2) | copy-start | bytes 6291460
  73.4 1.1 %copy-start.6 = (bf16[512,768]{1,0:T(8,128)(2,1)S(1)}, bf16[512,768]{1,0:T(8,128)(2,1)}, u32[]{:S(2)}) copy-start(bf16[512,768]{1,0:T(8,128)(2,1)} %constant.13.clone.fwd_ref) | copy-start | bytes 2359300
  74.5 1.1 %copy-start.8 = (bf16[256,1536]{1,0:T(8,128)(2,1)S(1)}, bf16[256,1536]{1,0:T(8,128)(2,1)}, u32[]{:S(2)}) copy-start(bf16[256,1536]{1,0:T(8,128)(2,1)} %constant.14.clone.inv_ref) | copy-start | bytes 2359300
  75.7 5.3 %copy-start.10 = (bf16[256,1024]{1,0:T(8,128)(2,1)S(1)}, bf16[256,1024]{1,0:T(8,128)(2,1)}, u32[]{:S(2)}) copy-start(bf16[256,1024]{1,0:T(8,128)(2,1)} %gate_ref.3) | copy-start | bytes 1572868
  75.7 5.3 %copy-start.12 = (bf16[256,1024]{1,0:T(8,128)(2,1)S(1)}, bf16[256,1024]{1,0:T(8,128)(2,1)}, u32[]{:S(2)}) copy-start(bf16[256,1024]{1,0:T(8,128)(2,1)} %key_ref.3) | copy-start | bytes 1572868
  75.7 5.3 %copy-start.14 = (bf16[256,1024]{1,0:T(8,128)(2,1)S(1)}, bf16[256,1024]{1,0:T(8,128)(2,1)}, u32[]{:S(2)}) copy-start(bf16[256,1024]{1,0:T(8,128)(2,1)} %value_ref.3) | copy-start | bytes 1572868
  75.7 5.3 %copy-start.16 = (bf16[256,1024]{1,0:T(8,128)(2,1)S(1)}, bf16[256,1024]{1,0:T(8,128)(2,1)}, u32[]{:S(2)}) copy-start(bf16[256,1024]{1,0:T(8,128)(2,1)} %cot_ref.3) | copy-start | bytes 1572868
  81.0 4.3 %copy-start.26 = (f32[128,16]{0,1:T(8,128)S(1)}, f32[128,16]{0,1:T(8,128)}, u32[]{:S(2)}) copy-start(f32[128,16]{0,1:T(8,128)} %param.15) | copy-start | bytes 24580
  81.0 4.3 %copy-start.28 = (f32[128,16]{0,1:T(8,128)S(1)}, f32[128,16]{0,1:T(8,128)}, u32[]{:S(2)}) copy-start(f32[128,16]{0,1:T(8,128)} %param.14) | copy-start | bytes 24580
  (9 other events, 6.6 us)

commit v2 on v1

--- a/solution.py
+++ b/solution.py
@@ -12,19 +12,34 @@
 ROWS = 8
 VMEM = pl.BlockSpec(memory_space=pltpu.VMEM)
 SMEM = pl.BlockSpec(memory_space=pltpu.SMEM)
-
-
-def call(body, outs, limit_mib, cost, scratch=()):
+HBM = pl.BlockSpec(memory_space=pltpu.HBM)
+ANY = pl.BlockSpec(memory_space=pl.ANY)
+DMA = pltpu.SemaphoreType.DMA
+
+
+def call(body, outs, limit_mib, cost, scratch=(), aliases=None):
     flops, moved = cost
     return lambda specs, *args: pl.pallas_call(
         body,
-        out_shape=[jax.ShapeDtypeStruct(s, t) for s, t in outs],
+        out_shape=[jax.ShapeDtypeStruct(s, t) for s, t, _ in outs],
         in_specs=list(specs),
-        out_specs=[VMEM] * len(outs),
+        out_specs=[w for _, _, w in outs],
         scratch_shapes=list(scratch),
+        input_output_aliases=aliases or {},
         compiler_params=pltpu.CompilerParams(vmem_limit_bytes=limit_mib * 2**20),
         cost_estimate=pl.CostEstimate(flops=flops, bytes_accessed=moved, transcendentals=0),
     )(*args)
+
+
+def start_all(copies):
+    for copy in copies:
+        copy.start()
+    return copies
+
+
+def wait_all(copies):
+    for copy in copies:
+        copy.wait()
 
 
 def halves(table):
@@ -69,33 +84,59 @@
     return jnp.concatenate([real, jnp.where(first, both, imag)], axis=0)
 
 
-def spread_body(decay_ref, residue_ref, out_ref):
-    modes = decay_ref.shape[0]
-    for block in range(out_ref.shape[0]):
-        out_ref[block, :modes] = decay_ref[...]
-        out_ref[block, modes:] = residue_ref[...]
-
-
-def product_body(gate_ref, key_ref, value_ref, cot_ref, fwd_ref, inv_ref, x_ref, b_ref, xs_ref, bs_ref, gk_ref, sk_ref):
+def spread_body(decay_ref, residue_ref, out_ref, sem):
+    modes, blocks = decay_ref.shape[0], out_ref.shape[0]
+    copies = [pltpu.make_async_copy(decay_ref, out_ref.at[k, pl.ds(0, modes)], sem.at[0, k]) for k in range(blocks)]
+    copies += [pltpu.make_async_copy(residue_ref, out_ref.at[k, pl.ds(modes, modes)], sem.at[1, k]) for k in range(blocks)]
+    wait_all(start_all(copies))
+
+
+def product_body(
+    gate_ref, key_ref, value_ref, cot_ref, fwd_ref, inv_ref,
+    x_ref, b_ref, xs_ref, bs_ref, gk_ref, sk_ref,
+    in_ref, fwd_v, inv_v, spec_ref, in_sem, table_sem, out_sem,
+):
     width = 2 * LANES
-
-    def step(block, carry):
-        lanes = pl.ds(pl.multiple_of(block * width, width), width)
-        x = key_ref[:, lanes].astype(jnp.float32) * value_ref[:, lanes].astype(jnp.float32)
-        b = cot_ref[:, lanes].astype(jnp.float32) * gate_ref[:, lanes].astype(jnp.float32)
+    count = x_ref.shape[1] // width
+    fetch = []
+    for block in range(count):
+        lanes = pl.ds(block * width, width)
+        fetch.append(
+            start_all([
+                pltpu.make_async_copy(ref.at[:, lanes], in_ref.at[k, :, lanes], in_sem.at[block, k])
+                for k, ref in enumerate((gate_ref, key_ref, value_ref, cot_ref))
+            ])
+        )
+        if block == 0:
+            tables = start_all([
+                pltpu.make_async_copy(fwd_ref, fwd_v, table_sem.at[0]),
+                pltpu.make_async_copy(inv_ref, inv_v, table_sem.at[1]),
+            ])
+    stores = []
+    for block in range(count):
+        lanes = pl.ds(block * width, width)
+        wait_all(fetch[block])
+        gate, key, value, cot = (in_ref[k, :, lanes].astype(jnp.float32) for k in range(4))
+        x, b = key * value, cot * gate
         x_ref[:, lanes] = x
         b_ref[:, lanes] = b
         total = jnp.sum(x * b, axis=0, keepdims=True)
         sk_ref[pl.ds(2 * block, 1), :] = total[:, :LANES]
         sk_ref[pl.ds(2 * block + 1, 1), :] = total[:, LANES:]
-        xs = split_dot(fwd_ref[...], x)
-        bs = split_dot(fwd_ref[...], b)
-        xs_ref[:, lanes] = xs
-        bs_ref[:, lanes] = bs
-        gk_ref[:, lanes] = split_dot(inv_ref[...], spectral_product(xs, bs, True))
-        return carry
-
-    lax.fori_loop(0, x_ref.shape[1] // width, step, 0)
+        if block == 0:
+            tables[0].wait()
+        xs = split_dot(fwd_v[...], x)
+        bs = split_dot(fwd_v[...], b)
+        spec_ref[0, :, lanes] = xs
+        spec_ref[1, :, lanes] = bs
+        stores += start_all([
+            pltpu.make_async_copy(spec_ref.at[k, :, lanes], ref.at[:, lanes], out_sem.at[block, k])
+            for k, ref in enumerate((xs_ref, bs_ref))
+        ])
+        if block == 0:
+            tables[1].wait()
+        gk_ref[:, lanes] = split_dot(inv_v[...], spectral_product(xs, bs, True))
+    wait_all(stores)
 
 
 def moments(decay, upward, downward):
@@ -123,16 +164,18 @@
     return [gather(s, up_weight) for s in ups], [gather(s, down_weight) for s in downs]
 
 
-def turn_out(scratch_ref, out_ref, slot):
-    owners = out_ref.shape[0]
-    for group in range(scratch_ref.shape[0] // LANES):
-        turned = scratch_ref[pl.ds(group * LANES, LANES), :].T
-        out_ref[:, slot + group] = turned.reshape(owners, LANES // owners, LANES)
-
-
-def state_body(par_ref, x_ref, b_ref, sk_ref, out_ref, rate_ref, sums_ref, rates_ref):
+def turned(scratch_ref, group, owners):
+    return scratch_ref[pl.ds(group * LANES, LANES), :].T.reshape(owners, LANES // owners, LANES)
+
+
+def state_body(index_ref, par_ref, x_ref, b_ref, sk_ref, out_ref, rate_ref, sums_ref, rates_ref, turn_ref, sem):
     blocks, modes = par_ref.shape[0], par_ref.shape[1] // 2
     tiles = x_ref.shape[0] // ROWS
+    owners, share = out_ref.shape[0], out_ref.shape[2]
+    groups = sums_ref.shape[0] // LANES
+    for owner in range(owners):
+        turn_ref[groups, owner, :blocks] = sk_ref[...]
+    copies = start_all([pltpu.make_async_copy(turn_ref.at[groups], out_ref.at[:, groups], sem.at[groups])])
 
     def step(block, carry):
         lanes = pl.ds(pl.multiple_of(block * LANES, LANES), LANES)
@@ -147,20 +190,23 @@
         rates_ref[pl.ds(start, 2 * modes), :] = jnp.concatenate([decay, decay], axis=0)
         return carry
 
-    lax.fori_loop(0, blocks, step, 0)
-    turn_out(sums_ref, out_ref, 0)
-    groups = sums_ref.shape[0] // LANES
-    for owner in range(out_ref.shape[0]):
-        out_ref[owner, groups, :blocks] = sk_ref[...]
     for group in range(groups):
-        rate_ref[group] = rates_ref[pl.ds(group * LANES, LANES), :].T
-
-
-def slope_body(par_ref, x_ref, b_ref, gk_ref, qa_ref, qb_ref, suma_ref, sumb_ref):
+        lax.fori_loop(group * blocks // groups, (group + 1) * blocks // groups, step, 0)
+        turn_ref[group] = turned(sums_ref, group, owners)
+        copies += start_all([pltpu.make_async_copy(turn_ref.at[group], out_ref.at[:, group], sem.at[group])])
+    for group in range(groups):
+        rates_ref[pl.ds(group * LANES, LANES), :] = rates_ref[pl.ds(group * LANES, LANES), :].T
+        rate_ref[group] = rates_ref[pl.ds(pl.multiple_of(group * LANES + index_ref[0] * share, share), share), :]
+    wait_all(copies)
+
+
+def slope_body(par_ref, x_ref, b_ref, gk_ref, out_ref, suma_ref, sumb_ref, turn_ref, sem):
     blocks, modes = par_ref.shape[0], par_ref.shape[1] // 2
     positions = x_ref.shape[0]
     tiles = positions // ROWS
     half = modes // 2
+    groups = suma_ref.shape[0] // LANES
+    owners = out_ref.shape[0]
 
     def step(block, carry):
         lanes = pl.ds(pl.multiple_of(block * LANES, LANES), LANES)
@@ -190,9 +236,14 @@
             sumb_ref[pl.ds(start + modes, half), :] = slope
         return carry
 
-    lax.fori_loop(0, blocks, step, 0)
-    turn_out(suma_ref, qa_ref, 0)
-    turn_out(sumb_ref, qb_ref, 0)
+    copies = []
+    for group in range(groups):
+        lax.fori_loop(group * blocks // groups, (group + 1) * blocks // groups, step, 0)
+        for kind, ref in enumerate((suma_ref, sumb_ref)):
+            slot = kind * groups + group
+            turn_ref[slot] = turned(ref, group, owners)
+            copies += start_all([pltpu.make_async_copy(turn_ref.at[slot], out_ref.at[:, groups + slot], sem.at[slot])])
+    wait_all(copies)
 
 
 def tree(values):
@@ -201,12 +252,30 @@
     return values[0]
 
 
-def local_body(par_ref, skip_ref, x_ref, b_ref, xs_ref, bs_ref, fwd_ref, inv_ref, pre_ref, gp_ref, k_ref):
+def local_body(
+    par_ref, skip_ref, x_ref, b_ref, xs_ref, bs_ref, fwd_ref, inv_ref,
+    pre_ref, gp_ref, token_ref,
+    k_ref, fwd_v, inv_v, spec_ref, table_sem, in_sem,
+):
     modes = par_ref.shape[1] // 2
     width = 2 * LANES
     tiles = x_ref.shape[0] // ROWS
-
-    def step(pair, carry):
+    count = x_ref.shape[1] // width
+    tables = start_all([
+        pltpu.make_async_copy(fwd_ref, fwd_v, table_sem.at[0]),
+        pltpu.make_async_copy(inv_ref, inv_v, table_sem.at[1]),
+    ])
+    fetch = []
+    for pair in range(count):
+        lanes = pl.ds(pair * width, width)
+        fetch.append(
+            start_all([
+                pltpu.make_async_copy(ref.at[:, lanes], spec_ref.at[k, :, lanes], in_sem.at[pair, k])
+                for k, ref in enumerate((xs_ref, bs_ref))
+            ])
+        )
+    token_ref[...] = jnp.zeros(token_ref.shape, jnp.float32)
+    for pair in range(count):
         phase = row_iota((ROWS, LANES)).astype(jnp.float32)
         for side in range(2):
             block = 2 * pair + side
@@ -216,34 +285,32 @@
             step8 = [jnp.exp(-float(ROWS) * rate) for rate in rates]
             terms = [weight[m : m + 1] * jnp.exp(-rates[m] * phase) for m in range(modes)]
             for tile in range(tiles):
-                k_ref[pl.ds(tile * ROWS, ROWS), side * LANES : (side + 1) * LANES] = tree(terms)
+                k_ref[pair % 2, pl.ds(tile * ROWS, ROWS), side * LANES : (side + 1) * LANES] = tree(terms)
                 if tile < tiles - 1:
                     terms = [t * s for t, s in zip(terms, step8)]
-        lanes = pl.ds(pl.multiple_of(pair * width, width), width)
+        lanes = pl.ds(pair * width, width)
         skip = jnp.concatenate([skip_ref[pl.ds(2 * pair, 1), :], skip_ref[pl.ds(2 * pair + 1, 1), :]], axis=1)
-        ks = split_dot(fwd_ref[...], k_ref[...])
-        conv = split_dot(inv_ref[...], spectral_product(ks, xs_ref[:, lanes], False))
+        if pair == 0:
+            wait_all(tables)
+        ks = split_dot(fwd_v[...], k_ref[pair % 2])
+        wait_all(fetch[pair])
+        conv = split_dot(inv_v[...], spectral_product(ks, spec_ref[0, :, lanes], False))
         pre_ref[:, lanes] = conv + skip * x_ref[:, lanes]
-        corr = split_dot(inv_ref[...], spectral_product(ks, bs_ref[:, lanes], True))
+        corr = split_dot(inv_v[...], spectral_product(ks, spec_ref[1, :, lanes], True))
         gp_ref[:, lanes] = corr + skip * b_ref[:, lanes]
-        return carry
-
-    lax.fori_loop(0, x_ref.shape[1] // width, step, 0)
 
 
 def lane_is_first(shape, modes):
     return lax.broadcasted_iota(jnp.int32, shape, 1) % (2 * modes) < modes
 
 
-def scan_body(index_ref, s_ref, rate_ref, qa_ref, qb_ref, out_ref, acc_ref, skip_ref, *, modes, length):
-    chunks = s_ref.shape[0]
-    groups = rate_ref.shape[0]
-    rows = s_ref.shape[2]
-    start = pl.multiple_of(index_ref[0] * rows, rows)
+def scan_body(s_ref, rate_ref, slopes_ref, out_ref, heads_ref, acc_ref, skip_ref, sem, *, modes, length):
+    chunks, groups, rows = s_ref.shape[0], rate_ref.shape[0], s_ref.shape[2]
     first = lane_is_first((rows, LANES), modes)
     zero = jnp.zeros((rows, LANES), jnp.float32)
+    copies = []
     for group in range(groups):
-        alpha = jnp.exp(-float(length) * rate_ref[group, pl.ds(start, rows), :])
+        alpha = jnp.exp(-float(length) * rate_ref[group])
         before, lead, total0, total1 = zero, zero, zero, zero
         heads = []
         for k in range(chunks):
@@ -256,48 +323,71 @@
             before = alpha * before + value
         after = zero
         for k in reversed(range(chunks)):
-            out_ref[k, group] = jnp.where(first, heads[k], after)
+            heads_ref[group, k] = jnp.where(first, heads[k], after)
             after = alpha * after + s_ref[k, group]
+        copies += start_all([pltpu.make_async_copy(heads_ref.at[group], out_ref.at[:, group], sem.at[group])])
         acc_ref[group] = jnp.where(first, total0, pltpu.roll(total1, modes, 1))
-    for k in range(chunks):
-        out_ref[k, groups : 2 * groups] = qa_ref[k]
-        out_ref[k, 2 * groups : 3 * groups] = qb_ref[k]
     skip_ref[...] = tree([s_ref[k, groups, : skip_ref.shape[0]] for k in range(chunks)])
-
-
-def slope_sum_body(index_ref, r_ref, own_ref, acc_ref, rate_ref, out_ref, *, modes):
+    wait_all(copies)
+
+
+def slope_sum_body(r_ref, own_ref, acc_ref, rate_ref, token_ref, out_ref, pack_ref, sem, *, modes):
     chunks, groups, rows = r_ref.shape[0], rate_ref.shape[0], r_ref.shape[2]
-    start = pl.multiple_of(index_ref[0] * rows, rows)
     first = lane_is_first((rows, LANES), modes)
-    blocks = out_ref.shape[1]
+    span = 2 * modes
+    fold = LANES // span
+    row = row_iota((rows, LANES)) % fold
+    column = lax.broadcasted_iota(jnp.int32, (rows, LANES), 1) // span
     for group in range(groups):
-        cross = tree([own_ref[k, group] * r_ref[k, groups + group] for k in range(chunks)])
+        cross = tree([own_ref[group, k] * r_ref[k, groups + group] for k in range(chunks)])
         inner = tree([r_ref[k, 2 * groups + group] for k in range(chunks)])
         cross = jnp.where(first, 0.0, cross + pltpu.roll(cross, modes, 1))
-        total = inner + jnp.exp(-rate_ref[group, pl.ds(start, rows), :]) * (acc_ref[group] + cross)
-        for block in range(group * (blocks // groups), (group + 1) * (blocks // groups)):
-            for owner in range(out_ref.shape[0]):
-                out_ref[owner, block] = total
-
-
-def final_body(index_ref, g_ref, residue_ref, decay_ref, gres_ref, gdec_ref, turned_ref):
+        total = inner + jnp.exp(-rate_ref[group]) * (acc_ref[group] + cross)
+        packed = total
+        for shift in range(1, fold):
+            moved = pltpu.roll(total, LANES - shift * span, 1)
+            moved = jnp.where(row >= shift, pltpu.roll(moved, shift, 0), pltpu.roll(moved, rows - fold + shift, 0))
+            packed = jnp.where((row - column + fold) % fold == shift, moved, packed)
+        for block in range(fold):
+            for r in range(rows // fold):
+                pack_ref[group * fold + block, pl.ds(r, 1), :] = packed[r * fold + block : r * fold + block + 1]
+    wait_all(start_all([pltpu.make_async_copy(pack_ref, out_ref.at[k], sem.at[k]) for k in range(out_ref.shape[0])]))
+
+
+def final_body(g_ref, residue_ref, decay_ref, gres_ref, gdec_ref, spread_ref):
     modes = residue_ref.shape[0]
-    blocks = g_ref.shape[1]
-    turned_ref[...] = tree([g_ref[:, block] for block in range(blocks)]).reshape(LANES, LANES).T
-    place = pl.multiple_of(lax.rem(index_ref[0], LANES // (2 * modes)) * (2 * modes), 2 * modes)
-    plain, slope = turned_ref[pl.ds(place, modes), :], turned_ref[pl.ds(place + modes, modes), :]
+    owners, blocks, rows = g_ref.shape[0], g_ref.shape[1], g_ref.shape[2]
+    span = 2 * modes
+    fold = LANES // span
+    total = tree([g_ref[:, block] for block in range(blocks)]).reshape(owners * rows, LANES)
+    for k in range(fold):
+        moved = total if k == 0 else pltpu.roll(total, LANES - k * span, 1)
+        spread_ref[pl.ds(k, owners * rows, stride=fold), :] = moved
+    sums = spread_ref[...].T
+    plain, slope = sums[:modes], sums[modes:span]
     decay = decay_ref[...]
     root = jnp.sqrt(decay)
     gres_ref[...] = root * plain
     gdec_ref[...] = residue_ref[...] * root * (0.5 * plain - decay * slope)
 
 
-def out_body(par_ref, r_ref, pre_ref, gp_ref, gate_ref, key_ref, value_ref, cot_ref, mixed_ref, ggate_ref, gkey_ref, gvalue_ref, hb_ref):
+def out_body(
+    par_ref, r_ref, pre_ref, gp_ref, gate_hbm, key_hbm, value_hbm, cot_hbm,
+    mixed_ref, ggate_ref, gkey_ref, gvalue_ref,
+    hb_ref, gate_ref, key_ref, value_ref, cot_ref, sem,
+):
     blocks, modes = par_ref.shape[0], par_ref.shape[1] // 2
     groups = hb_ref.shape[0] // LANES
     pack = 2 * ROWS
+    copies = start_all([
+        pltpu.make_async_copy(source, target, sem.at[k])
+        for k, (source, target) in enumerate(
+            zip((gate_hbm, key_hbm, value_hbm, cot_hbm), (gate_ref, key_ref, value_ref, cot_ref))
+        )
+    ])
     for group in range(groups):
         hb_ref[pl.ds(group * LANES, LANES), :] = r_ref[:, group].reshape(LANES, LANES).T
+    wait_all(copies)
 
     def step(block, carry):
         lanes = pl.ds(pl.multiple_of(block * LANES, LANES), LANES)
@@ -344,73 +434,92 @@
     share = filters // owners
     groups = blocks * 2 * modes // LANES
     place = lax.axis_index("ctx").astype(jnp.int32).reshape(1)
-    column = lax.axis_index("ch").astype(jnp.int32).reshape(1)
     forward, inverse = (jnp.asarray(t) for t in transform_tables(length))
     whole = (length, channels)
     size = length * channels
-
-    (sent,) = call(spread_body, [((blocks, 2 * modes, LANES), f32)], 8, (0, 10**5))([VMEM] * 2, decay.T, residue.T)
+    dense = pltpu.VMEM(whole, bf16)
+    tables = [pltpu.VMEM(forward.shape, bf16), pltpu.VMEM(inverse.shape, bf16)]
+    spectra = pltpu.VMEM((2, 2 * length, channels), f32)
+    pairs = channels // (2 * LANES)
+    sums = pltpu.VMEM((groups * LANES, LANES), f32)
+    tile = (share, LANES)
+
+    (sent,) = call(spread_body, [((blocks, 2 * modes, LANES), f32, HBM)], 4, (0, 10**5), [DMA((2, blocks))])(
+        [ANY] * 2, decay.T, residue.T
+    )
     params = lax.all_to_all(sent, "ch", 0, 0, tiled=True)
 
     x, b, xs, bs, gk, sk = call(
         product_body,
-        [(whole, f32), (whole, f32), ((2 * length, channels), f32), ((2 * length, channels), f32), (whole, f32), ((blocks, LANES), f32)],
-        32,
+        [(whole, f32, VMEM)] * 2
+        + [((2 * length, channels), f32, HBM)] * 2
+        + [(whole, f32, VMEM), ((blocks, LANES), f32, VMEM)],
+        24,
         (18 * length * size, 36 * size),
-    )([VMEM] * 6, gate_in, key_in, value_in, cotangent, forward, inverse)
+        [pltpu.VMEM((4, *whole), bf16), *tables, spectra, DMA((pairs, 4)), DMA((2,)), DMA((pairs, 2))],
+    )([ANY] * 6, gate_in, key_in, value_in, cotangent, forward, inverse)
 
     states, rates = call(
         state_body,
-        [((owners, groups + 1, share, LANES), f32), ((groups, LANES, LANES), f32)],
-        16,
+        [((owners, groups + 1, *tile), f32, HBM), ((groups, *tile), f32, VMEM)],
+        8,
         (64 * size, 8 * size),
-        [pltpu.VMEM((groups * LANES, LANES), f32)] * 2,
-    )([VMEM] * 4, params, x, b, sk)
+        [sums, sums, pltpu.VMEM((groups + 1, owners, *tile), f32), DMA((groups + 1,))],
+    )([SMEM] + [VMEM] * 4, place, params, x, b, sk)
     states = lax.all_to_all(states, "ctx", 0, 0, tiled=True)
 
-    slopes, inner = call(
+    (slopes,) = call(
         slope_body,
-        [((owners, groups, share, LANES), f32)] * 2,
-        16,
+        [((owners, 3 * groups, *tile), f32, HBM)],
+        8,
         (128 * size, 12 * size),
-        [pltpu.VMEM((groups * LANES, LANES), f32)] * 2,
+        [sums, sums, pltpu.VMEM((2 * groups, owners, *tile), f32), DMA((2 * groups,))],
     )([VMEM] * 4, params, x, b, gk)
 
-    bundle, acc, grad_skip = call(
+    bundle, heads, acc, grad_skip = call(
         functools.partial(scan_body, modes=modes, length=length),
-        [((owners, 3 * groups, share, LANES), f32), ((groups, share, LANES), f32), ((blocks, LANES), f32)],
+        [
+            ((owners, 3 * groups, *tile), f32, HBM),
+            ((groups, owners, *tile), f32, VMEM),
+            ((groups, *tile), f32, VMEM),
+            ((blocks, LANES), f32, VMEM),
+        ],
         8,
         (10**5, 10**6),
-    )([SMEM] + [VMEM] * 4, place, states, rates, slopes, inner)
+        [DMA((groups,))],
+        {2: 0},
+    )([VMEM, VMEM, HBM], states, rates, slopes)
     arrived = lax.all_to_all(bundle, "ctx", 0, 0, tiled=True)
 
-    pre, gp = call(
+    pre, gp, token = call(
         local_body,
-        [(whole, f32)] * 2,
-        32,
+        [(whole, f32, VMEM)] * 2 + [((ROWS, LANES), f32, VMEM)],
+        24,
         (18 * length * size, 36 * size),
-        [pltpu.VMEM((length, 2 * LANES), f32)],
-    )([VMEM] * 8, params, skip.reshape(blocks, LANES), x, b, xs, bs, forward, inverse)
-
+        [pltpu.VMEM((2, length, 2 * LANES), f32), *tables, spectra, DMA((2,)), DMA((pairs, 2))],
+    )([VMEM] * 4 + [ANY] * 4, params, skip.reshape(blocks, LANES), x, b, xs, bs, forward, inverse)
+
+    packed = (owners, blocks, share * 2 * modes // LANES, LANES)
     (grads,) = call(
         functools.partial(slope_sum_body, modes=modes),
-        [((owners, blocks, share, LANES), f32)],
+        [(packed, f32, HBM)],
         8,
         (10**5, 10**6),
-    )([SMEM] + [VMEM] * 4, place, arrived, bundle, acc, rates)
-    grads = lax.all_to_all(grads.reshape(owners * blocks, share, LANES), ("ctx", "ch"), 0, 0, tiled=True)
+        [pltpu.VMEM(packed[1:], f32), DMA((owners,))],
+    )([VMEM] * 4 + [ANY], arrived, heads, acc, rates, token)
+    grads = lax.all_to_all(grads.reshape(owners * blocks, *packed[2:]), ("ctx", "ch"), 0, 0, tiled=True)
 
     mixed, grad_gate, grad_key, grad_value = call(
         out_body,
-        [(whole, bf16)] * 4,
-        24,
+        [(whole, bf16, VMEM)] * 4,
+        16,
         (64 * size, 20 * size),
-        [pltpu.VMEM((groups * LANES, LANES), f32)],
-    )([VMEM] * 8, params, arrived, pre, gp, gate_in, key_in, value_in, cotangent)
+        [sums, dense, dense, dense, dense, DMA((4,))],
+    )([VMEM] * 4 + [ANY] * 4, params, arrived, pre, gp, gate_in, key_in, value_in, cotangent)
 
     grad_residue, grad_log_decay = call(
-        final_body, [((modes, filters), f32)] * 2, 8, (10**5, 10**6), [pltpu.VMEM((LANES, LANES), f32)]
-    )([SMEM] + [VMEM] * 3, column, grads.reshape(owners, blocks, share, LANES), residue.T, decay.T)
+        final_body, [((modes, filters), f32, VMEM)] * 2, 8, (10**5, 10**6), [pltpu.VMEM((LANES, LANES), f32)]
+    )([VMEM] * 3, grads.reshape(packed), residue.T, decay.T)
     return (mixed, grad_gate, grad_key, grad_value, grad_skip.reshape(channels), grad_residue.T, grad_log_decay.T)
 
 

time: 87 us -> 90.8 us (1.044)
  blocking collectives: 13.9 us -> 0 us
  starting transfers between devices: 22.7 us -> 30 us
  Pallas kernels: 25.6 us -> 31.1 us
  local copies, waits for them, and re-layouts: 23 us -> 27.6 us
    all_to_all x1 -> x0, blocking collectives: 13.9 us -> none  [on_device(): arrived = lax.all_to_all(bundle, 'ctx', 0, 0, tiled=True)]
    all_to_all x1 -> x2, starting transfers between devices: 8.86 us -> 16.1 us  [the longest x1 10.4 us: on_device(): lax.all_to_all(grads.reshape(owners * blocks, *packed[2:]), ('ctx', 'ch')...]
    pallas_call x9, Pallas kernels: 25.6 us -> 31.1 us  [call(): pl.pallas_call(body, out_shape=[jax.ShapeDtypeStruct(s, t) for s, t, _ in...]
    unnamed x60 -> x58, local copies, waits for them, and re-layouts: 23 us -> 27.6 us
  transfers between devices with their start and end apart: 3 -> 4, of which waited for: 0 -> 0; matrix products, arithmetic and copies ran while one was open for 0% -> 0% of each run, Pallas kernels for 24% -> 27%
where the time goes in v2:
time: 90.8 us; the launch traced here: 89.5 us
  Pallas kernels  31.1 us (34%)
  starting transfers between devices  30 us (33%)
  local copies, waits for them, and re-layouts  27.6 us (30%)
    pallas_call x9, Pallas kernels, call(): pl.pallas_call(body, out_shape=[jax.ShapeDtypeStruct(s, t) for s, t, _ in...  31.1 us
    unnamed x58, local copies, waits for them, and re-layouts  27.6 us
    all_to_all x1, starting transfers between devices, on_device(): lax.all_to_all(grads.reshape(owners * blocks, *packed[2:]), ('ctx', 'ch')...  10.4 us
    all_to_all x1, starting transfers between devices, on_device(): params = lax.all_to_all(sent, 'ch', 0, 0, tiled=True)  7.49 us
    all_to_all x1, starting transfers between devices, on_device(): states = lax.all_to_all(states, 'ctx', 0, 0, tiled=True)  6.42 us
    all_to_all x1, starting transfers between devices, on_device(): arrived = lax.all_to_all(bundle, 'ctx', 0, 0, tiled=True)  5.73 us
  transfers between devices with their start and end apart: 4, of which 0 were waited for; matrix products, arithmetic and copies ran while one was open for 0% of the time, Pallas kernels for 27%

profile of v2, /device:TPU:1, one launch (start us, length us, event | category | flops | bytes accessed | tf_op | source)
XLA Modules:
  0.0 89.5 jit_solution(6081627639374253419)
XLA Ops:
  2.8 7.5 %all-to-all-start = ((f32[8,32,128]{2,1,0:T(8,128)}), f32[8,32,128]{2,1,0:T(8,128)S(1)}, u32[]{:S(2)}, u32[]{:S(2)}) async-start(f32[8,32,128]{2,1,0:T(8,128)} %shard_map.144), calls=%async_computation | async-start | bytes 262144 | tf_op jit(solution)/shard_map/all_to_all | solution.py:450
  10.3 1.1 %copy-done.10 = bf16[512,768]{1,0:T(8,128)(2,1)S(1)} copy-done((bf16[512,768]{1,0:T(8,128)(2,1)S(1)}, bf16[512,768]{1,0:T(8,128)(2,1)}, u32[]{:S(2)}) %copy-start.10) | copy-done | bytes 786456
  11.5 1.1 %copy-done.12 = bf16[256,1536]{1,0:T(8,128)(2,1)S(1)} copy-done((bf16[256,1536]{1,0:T(8,128)(2,1)S(1)}, bf16[256,1536]{1,0:T(8,128)(2,1)}, u32[]{:S(2)}) %copy-start.12) | copy-done | bytes 786456
  12.6 1.0 %copy-done.14 = bf16[256,1024]{1,0:T(8,128)(2,1)S(1)} copy-done((bf16[256,1024]{1,0:T(8,128)(2,1)S(1)}, bf16[256,1024]{1,0:T(8,128)(2,1)}, u32[]{:S(2)}) %copy-start.14) | copy-done | bytes 524312
  13.6 1.0 %copy-done.16 = bf16[256,1024]{1,0:T(8,128)(2,1)S(1)} copy-done((bf16[256,1024]{1,0:T(8,128)(2,1)S(1)}, bf16[256,1024]{1,0:T(8,128)(2,1)}, u32[]{:S(2)}) %copy-start.16) | copy-done | bytes 524312
  16.8 6.5 %shard_map.145 = (f32[256,1024]{1,0:T(8,128)S(1)}, f32[256,1024]{1,0:T(8,128)S(1)}, f32[512,1024]{1,0:T(8,128)S(1)}, f32[512,1024]{1,0:T(8,128)S(1)}, f32[256,1024]{1,0:T(8,128)S(1)}, /*index=5*/f32[8,128]{1,0:T(8,128)S(1)}) custom-call(bf16[256,1024]{1,0:T(8,128)(2,1)S(1)} %copy-done.14, bf16[256,1024]{1,0:T(8,128)(2,1)S(1)} %copy-done.16, ...), custom_call_target="tpu_custom_call" | custom-call | flops 1207959552 | bytes 9437184 | tf_op jit(solution)/shard_map/pallas_call | solution.py:22
  23.3 1.4 %copy-done = f32[512,1024]{1,0:T(8,128)} copy-done((f32[512,1024]{1,0:T(8,128)}, f32[512,1024]{1,0:T(8,128)S(1)}, u32[]{:S(2)}) %copy-start) | copy-done | bytes 2097176
  24.7 1.3 %copy-done.2 = f32[512,1024]{1,0:T(8,128)} copy-done((f32[512,1024]{1,0:T(8,128)}, f32[512,1024]{1,0:T(8,128)S(1)}, u32[]{:S(2)}) %copy-start.2) | copy-done | bytes 2097176
  27.0 3.5 %shard_map.146 = (f32[16,3,8,128]{3,2,1,0:T(8,128)}, f32[2,8,128]{2,1,0:T(8,128)S(1)}) custom-call(s32[1]{0:T(128)} %bitcast.2.index_ref, f32[8,32,128]{2,1,0:T(8,128)S(1)} %all-to-all-done.par_ref, f32[256,1024]{1,0:T(8,128)S(1)} %get-tuple-element.28.x_ref, f32[256,1024]{1,0:T(8,128)S(1)} %get-tuple-element.29.b_ref, f32[8,128]{1,0:T(8,128)S(1)} %get-tuple-element.30.sk_ref), custom_call_target="tpu_custom_call" | custom-call | flops 16777216 | bytes 2097152 | tf_op jit(solution)/shard_map/pallas_call | solution.py:22
  30.5 6.4 %all-to-all-start.1 = ((f32[16,3,8,128]{3,2,1,0:T(8,128)}), f32[16,3,8,128]{3,2,1,0:T(8,128)S(1)}, u32[]{:S(2)}, u32[]{:S(2)}) async-start(f32[16,3,8,128]{3,2,1,0:T(8,128)} %get-tuple-element.31), calls=%async_computation.1 | async-start | bytes 393216 | tf_op jit(solution)/shard_map/all_to_all | solution.py:469
  36.9 1.2 %copy-done.5 = f32[256,1024]{1,0:T(8,128)S(1)} copy-done((f32[256,1024]{1,0:T(8,128)S(1)}, f32[256,1024]{1,0:T(8,128)}, u32[]{:S(2)}) %copy-start.5) | copy-done | bytes 1048600
  38.2 6.3 %shard_map.147.slopes_ref = f32[16,6,8,128]{3,2,1,0:T(8,128)} custom-call(f32[8,32,128]{2,1,0:T(8,128)S(1)} %all-to-all-done.par_ref, f32[256,1024]{1,0:T(8,128)S(1)} %get-tuple-element.28.x_ref, f32[256,1024]{1,0:T(8,128)S(1)} %get-tuple-element.29.b_ref, f32[256,1024]{1,0:T(8,128)S(1)} %copy-done.5), custom_call_target="tpu_custom_call" | custom-call | flops 33554432 | bytes 3145728 | tf_op jit(solution)/shard_map/pallas_call | solution.py:22
  44.5 1.4 %shard_map.148 = (f32[16,6,8,128]{3,2,1,0:T(8,128)}, f32[2,16,8,128]{3,2,1,0:T(8,128)S(1)}, f32[2,8,128]{2,1,0:T(8,128)S(1)}, f32[8,128]{1,0:T(8,128)}) custom-call(f32[16,3,8,128]{3,2,1,0:T(8,128)S(1)} %all-to-all-done.1.s_ref, f32[2,8,128]{2,1,0:T(8,128)S(1)} %get-tuple-element.32.rate_ref, ...), custom_call_target="tpu_custom_call", output_to_operand_aliasing={{0}: (2, {})} | custom-call | flops 100000 | bytes 1000000 | tf_op jit(solution)/shard_map/pallas_call | solution.py:22
  45.8 5.7 %all-to-all-start.2 = ((f32[16,6,8,128]{3,2,1,0:T(8,128)}), f32[16,6,8,128]{3,2,1,0:T(8,128)S(1)}, u32[]{:S(2)}, u32[]{:S(2)}) async-start(f32[16,6,8,128]{3,2,1,0:T(8,128)} %get-tuple-element.34), calls=%async_computation.2 | async-start | bytes 786432 | tf_op jit(solution)/shard_map/all_to_all | solution.py:492
  51.6 1.6 %copy-done.1 = f32[512,1024]{1,0:T(8,128)S(1)} copy-done((f32[512,1024]{1,0:T(8,128)S(1)}, f32[512,1024]{1,0:T(8,128)}, u32[]{:S(2)}) %copy-start.1) | copy-done | bytes 2097176
  53.2 1.6 %copy-done.3 = f32[512,1024]{1,0:T(8,128)S(1)} copy-done((f32[512,1024]{1,0:T(8,128)S(1)}, f32[512,1024]{1,0:T(8,128)}, u32[]{:S(2)}) %copy-start.3) | copy-done | bytes 2097176
  54.7 1.1 %copy-done.13 = bf16[256,1536]{1,0:T(8,128)(2,1)S(1)} copy-done((bf16[256,1536]{1,0:T(8,128)(2,1)S(1)}, bf16[256,1536]{1,0:T(8,128)(2,1)}, u32[]{:S(2)}) %copy-start.13) | copy-done | bytes 786456
  56.6 6.5 %shard_map.149 = (f32[256,1024]{1,0:T(8,128)S(1)}, f32[256,1024]{1,0:T(8,128)S(1)}, f32[8,128]{1,0:T(8,128)S(1)}) custom-call(f32[8,32,128]{2,1,0:T(8,128)S(1)} %all-to-all-done.par_ref, f32[8,128]{1,0:T(8,128)S(1)} %bitcast.14, f32[256,1024]{1,0:T(8,128)S(1)} %get-tuple-element.28.x_ref, f32[256,1024]{1,0:T(8,128)S(1)} %get-tuple-element.29.b_ref, ...), custom_call_target="tpu_custom_call" | custom-call | flops 1207959552 | bytes 9437184 | tf_op jit(solution)/shard_map/pallas_call | solution.py:22
  67.3 10.4 %all-to-all-start.3 = ((f32[128,2,128]{2,1,0:T(2,128)}), f32[128,2,128]{2,1,0:T(2,128)S(1)}, u32[]{:S(2)}, u32[]{:S(2)}) async-start(f32[128,2,128]{2,1,0:T(2,128)} %bitcast.5), calls=%async_computation.3 | async-start | bytes 262144 | tf_op jit(solution)/shard_map/all_to_all | solution.py:510
  77.7 1.2 %copy-done.7 = f32[256,1024]{1,0:T(8,128)S(1)} copy-done((f32[256,1024]{1,0:T(8,128)S(1)}, f32[256,1024]{1,0:T(8,128)}, u32[]{:S(2)}) %copy-start.7) | copy-done | bytes 1048600
  78.9 1.2 %copy-done.9 = f32[256,1024]{1,0:T(8,128)S(1)} copy-done((f32[256,1024]{1,0:T(8,128)S(1)}, f32[256,1024]{1,0:T(8,128)}, u32[]{:S(2)}) %copy-start.9) | copy-done | bytes 1048600
  80.1 1.0 %copy-done.15 = bf16[256,1024]{1,0:T(8,128)(2,1)S(1)} copy-done((bf16[256,1024]{1,0:T(8,128)(2,1)S(1)}, bf16[256,1024]{1,0:T(8,128)(2,1)}, u32[]{:S(2)}) %copy-start.15) | copy-done | bytes 524312
  81.2 1.0 %copy-done.17 = bf16[256,1024]{1,0:T(8,128)(2,1)S(1)} copy-done((bf16[256,1024]{1,0:T(8,128)(2,1)S(1)}, bf16[256,1024]{1,0:T(8,128)(2,1)}, u32[]{:S(2)}) %copy-start.17) | copy-done | bytes 524312
  84.3 4.4 %shard_map.150 = (bf16[256,1024]{1,0:T(8,128)(2,1)}, bf16[256,1024]{1,0:T(8,128)(2,1)}, bf16[256,1024]{1,0:T(8,128)(2,1)}, bf16[256,1024]{1,0:T(8,128)(2,1)}) custom-call(f32[8,32,128]{2,1,0:T(8,128)S(1)} %all-to-all-done.par_ref, f32[16,6,8,128]{3,2,1,0:T(8,128)S(1)} %all-to-all-done.2.r_ref, f32[256,1024]{1,0:T(8,128)S(1)} %copy-done.7, ...), custom_call_target="tpu_custom_call" | custom-call | flops 16777216 | bytes 5242880 | tf_op jit(solution)/shard_map/pallas_call | solution.py:22
  (51 shorter events, 13.1 us)
Async XLA Ops:
  2.8 24.2 %all-to-all-start = ((f32[8,32,128]{2,1,0:T(8,128)}), f32[8,32,128]{2,1,0:T(8,128)S(1)}, u32[]{:S(2)}, u32[]{:S(2)}) async-start(f32[8,32,128]{2,1,0:T(8,128)} %shard_map.144), calls=%async_computation | async-start | bytes 262144 | tf_op jit(solution)/shard_map/all_to_all | solution.py:450
  10.3 1.1 %copy-start.10 = (bf16[512,768]{1,0:T(8,128)(2,1)S(1)}, bf16[512,768]{1,0:T(8,128)(2,1)}, u32[]{:S(2)}) copy-start(bf16[512,768]{1,0:T(8,128)(2,1)} %constant.10.clone.fwd_ref) | copy-start | bytes 2359300
  11.5 1.1 %copy-start.12 = (bf16[256,1536]{1,0:T(8,128)(2,1)S(1)}, bf16[256,1536]{1,0:T(8,128)(2,1)}, u32[]{:S(2)}) copy-start(bf16[256,1536]{1,0:T(8,128)(2,1)} %constant.11.clone.inv_ref) | copy-start | bytes 2359300
  12.6 1.0 %copy-start.14 = (bf16[256,1024]{1,0:T(8,128)(2,1)S(1)}, bf16[256,1024]{1,0:T(8,128)(2,1)}, u32[]{:S(2)}) copy-start(bf16[256,1024]{1,0:T(8,128)(2,1)} %gate_hbm.1) | copy-start | bytes 1572868
  13.6 1.0 %copy-start.16 = (bf16[256,1024]{1,0:T(8,128)(2,1)S(1)}, bf16[256,1024]{1,0:T(8,128)(2,1)}, u32[]{:S(2)}) copy-start(bf16[256,1024]{1,0:T(8,128)(2,1)} %key_hbm.1) | copy-start | bytes 1572868
  14.7 1.0 %copy-start.18 = (bf16[256,1024]{1,0:T(8,128)(2,1)S(1)}, bf16[256,1024]{1,0:T(8,128)(2,1)}, u32[]{:S(2)}) copy-start(bf16[256,1024]{1,0:T(8,128)(2,1)} %value_hbm.1) | copy-start | bytes 1572868
  15.7 1.0 %copy-start.20 = (bf16[256,1024]{1,0:T(8,128)(2,1)S(1)}, bf16[256,1024]{1,0:T(8,128)(2,1)}, u32[]{:S(2)}) copy-start(bf16[256,1024]{1,0:T(8,128)(2,1)} %cot_hbm.1) | copy-start | bytes 1572868
  23.3 1.4 %copy-start = (f32[512,1024]{1,0:T(8,128)}, f32[512,1024]{1,0:T(8,128)S(1)}, u32[]{:S(2)}) copy-start(f32[512,1024]{1,0:T(8,128)S(1)} %get-tuple-element.35.xs_ref) | copy-start | bytes 6291460
  24.7 1.3 %copy-start.2 = (f32[512,1024]{1,0:T(8,128)}, f32[512,1024]{1,0:T(8,128)S(1)}, u32[]{:S(2)}) copy-start(f32[512,1024]{1,0:T(8,128)S(1)} %get-tuple-element.36.bs_ref) | copy-start | bytes 6291460
  30.5 13.9 %all-to-all-start.1 = ((f32[16,3,8,128]{3,2,1,0:T(8,128)}), f32[16,3,8,128]{3,2,1,0:T(8,128)S(1)}, u32[]{:S(2)}, u32[]{:S(2)}) async-start(f32[16,3,8,128]{3,2,1,0:T(8,128)} %get-tuple-element.31), calls=%async_computation.1 | async-start | bytes 393216 | tf_op jit(solution)/shard_map/all_to_all | solution.py:469
  36.9 1.2 %copy-start.5 = (f32[256,1024]{1,0:T(8,128)S(1)}, f32[256,1024]{1,0:T(8,128)}, u32[]{:S(2)}) copy-start(f32[256,1024]{1,0:T(8,128)} %copy-done.4) | copy-start | bytes 3145732
  38.1 13.4 %copy-start.11 = (bf16[512,768]{1,0:T(8,128)(2,1)S(1)}, bf16[512,768]{1,0:T(8,128)(2,1)}, u32[]{:S(2)}) copy-start(bf16[512,768]{1,0:T(8,128)(2,1)} %constant.10.clone.fwd_ref) | copy-start | bytes 2359300
  45.8 19.8 %all-to-all-start.2 = ((f32[16,6,8,128]{3,2,1,0:T(8,128)}), f32[16,6,8,128]{3,2,1,0:T(8,128)S(1)}, u32[]{:S(2)}, u32[]{:S(2)}) async-start(f32[16,6,8,128]{3,2,1,0:T(8,128)} %get-tuple-element.34), calls=%async_computation.2 | async-start | bytes 786432 | tf_op jit(solution)/shard_map/all_to_all | solution.py:492
  51.6 1.6 %copy-start.1 = (f32[512,1024]{1,0:T(8,128)S(1)}, f32[512,1024]{1,0:T(8,128)}, u32[]{:S(2)}) copy-start(f32[512,1024]{1,0:T(8,128)} %copy-done) | copy-start | bytes 6291460
  53.2 1.6 %copy-start.3 = (f32[512,1024]{1,0:T(8,128)S(1)}, f32[512,1024]{1,0:T(8,128)}, u32[]{:S(2)}) copy-start(f32[512,1024]{1,0:T(8,128)} %copy-done.2) | copy-start | bytes 6291460
  54.7 1.1 %copy-start.13 = (bf16[256,1536]{1,0:T(8,128)(2,1)S(1)}, bf16[256,1536]{1,0:T(8,128)(2,1)}, u32[]{:S(2)}) copy-start(bf16[256,1536]{1,0:T(8,128)(2,1)} %constant.11.clone.inv_ref) | copy-start | bytes 2359300
  67.3 21.4 %all-to-all-start.3 = ((f32[128,2,128]{2,1,0:T(2,128)}), f32[128,2,128]{2,1,0:T(2,128)S(1)}, u32[]{:S(2)}, u32[]{:S(2)}) async-start(f32[128,2,128]{2,1,0:T(2,128)} %bitcast.5), calls=%async_computation.3 | async-start | bytes 262144 | tf_op jit(solution)/shard_map/all_to_all | solution.py:510
  77.7 1.2 %copy-start.7 = (f32[256,1024]{1,0:T(8,128)S(1)}, f32[256,1024]{1,0:T(8,128)}, u32[]{:S(2)}) copy-start(f32[256,1024]{1,0:T(8,128)} %copy-done.6) | copy-start | bytes 3145732
  78.9 1.2 %copy-start.9 = (f32[256,1024]{1,0:T(8,128)S(1)}, f32[256,1024]{1,0:T(8,128)}, u32[]{:S(2)}) copy-start(f32[256,1024]{1,0:T(8,128)} %copy-done.8) | copy-start | bytes 3145732
  80.1 1.0 %copy-start.15 = (bf16[256,1024]{1,0:T(8,128)(2,1)S(1)}, bf16[256,1024]{1,0:T(8,128)(2,1)}, u32[]{:S(2)}) copy-start(bf16[256,1024]{1,0:T(8,128)(2,1)} %gate_hbm.1) | copy-start | bytes 1572868
  81.2 1.0 %copy-start.17 = (bf16[256,1024]{1,0:T(8,128)(2,1)S(1)}, bf16[256,1024]{1,0:T(8,128)(2,1)}, u32[]{:S(2)}) copy-start(bf16[256,1024]{1,0:T(8,128)(2,1)} %key_hbm.1) | copy-start | bytes 1572868
  82.2 1.0 %copy-start.19 = (bf16[256,1024]{1,0:T(8,128)(2,1)S(1)}, bf16[256,1024]{1,0:T(8,128)(2,1)}, u32[]{:S(2)}) copy-start(bf16[256,1024]{1,0:T(8,128)(2,1)} %value_hbm.1) | copy-start | bytes 1572868
  84.3 4.5 %copy-start.23 = (f32[128,16]{0,1:T(8,128)S(1)}, f32[128,16]{0,1:T(8,128)}, u32[]{:S(2)}) copy-start(f32[128,16]{0,1:T(8,128)} %param.15) | copy-start | bytes 24580
  84.3 4.5 %copy-start.25 = (f32[128,16]{0,1:T(8,128)S(1)}, f32[128,16]{0,1:T(8,128)}, u32[]{:S(2)}) copy-start(f32[128,16]{0,1:T(8,128)} %param.14) | copy-start | bytes 24580
  (9 other events, 7.4 us)

commit v3 on v2

--- a/solution.py
+++ b/solution.py
@@ -13,7 +13,6 @@
 VMEM = pl.BlockSpec(memory_space=pltpu.VMEM)
 SMEM = pl.BlockSpec(memory_space=pltpu.SMEM)
 HBM = pl.BlockSpec(memory_space=pltpu.HBM)
-ANY = pl.BlockSpec(memory_space=pl.ANY)
 DMA = pltpu.SemaphoreType.DMA
 
 
@@ -21,14 +20,14 @@
     flops, moved = cost
     return lambda specs, *args: pl.pallas_call(
         body,
-        out_shape=[jax.ShapeDtypeStruct(s, t) for s, t, _ in outs],
+        out_shape=[pltpu.HBM(s, t) if w is HBM else jax.ShapeDtypeStruct(s, t) for s, t, w in outs],
         in_specs=list(specs),
         out_specs=[w for _, _, w in outs],
         scratch_shapes=list(scratch),
         input_output_aliases=aliases or {},
         compiler_params=pltpu.CompilerParams(vmem_limit_bytes=limit_mib * 2**20),
         cost_estimate=pl.CostEstimate(flops=flops, bytes_accessed=moved, transcendentals=0),
-    )(*args)
+    )(*(pltpu.with_memory_space_constraint(a, pltpu.HBM) if w is HBM else a for w, a in zip(specs, args)))
 
 
 def start_all(copies):
@@ -45,7 +44,7 @@
 def halves(table):
     high = table.astype(jnp.bfloat16)
     low = (table - high.astype(np.float64)).astype(jnp.bfloat16)
-    return np.concatenate([high, high, low], axis=1)
+    return np.concatenate([high, low], axis=1)
 
 
 def transform_tables(length):
@@ -64,7 +63,9 @@
 def split_dot(table, signal):
     high = signal.astype(jnp.bfloat16)
     low = (signal - high.astype(jnp.float32)).astype(jnp.bfloat16)
-    return jnp.dot(table, jnp.concatenate([high, low, high], axis=0), preferred_element_type=jnp.float32)
+    depth = signal.shape[0]
+    table = jnp.concatenate([table[:, :depth], table], axis=1)
+    return jnp.dot(table, jnp.concatenate([low, high, high], axis=0), preferred_element_type=jnp.float32)
 
 
 def row_iota(shape):
@@ -84,17 +85,21 @@
     return jnp.concatenate([real, jnp.where(first, both, imag)], axis=0)
 
 
-def spread_body(decay_ref, residue_ref, out_ref, sem):
+def spread_body(decay_ref, residue_ref, out_ref, held_ref, in_sem, out_sem):
     modes, blocks = decay_ref.shape[0], out_ref.shape[0]
-    copies = [pltpu.make_async_copy(decay_ref, out_ref.at[k, pl.ds(0, modes)], sem.at[0, k]) for k in range(blocks)]
-    copies += [pltpu.make_async_copy(residue_ref, out_ref.at[k, pl.ds(modes, modes)], sem.at[1, k]) for k in range(blocks)]
-    wait_all(start_all(copies))
+    wait_all(
+        start_all([
+            pltpu.make_async_copy(ref, held_ref.at[pl.ds(k * modes, modes)], in_sem.at[k])
+            for k, ref in enumerate((decay_ref, residue_ref))
+        ])
+    )
+    wait_all(start_all([pltpu.make_async_copy(held_ref, out_ref.at[k], out_sem.at[k]) for k in range(blocks)]))
 
 
 def product_body(
     gate_ref, key_ref, value_ref, cot_ref, fwd_ref, inv_ref,
     x_ref, b_ref, xs_ref, bs_ref, gk_ref, sk_ref,
-    in_ref, fwd_v, inv_v, spec_ref, in_sem, table_sem, out_sem,
+    in_ref, fwd_v, inv_v, spec_ref, turn_ref, in_sem, table_sem, out_sem,
 ):
     width = 2 * LANES
     count = x_ref.shape[1] // width
@@ -135,7 +140,8 @@
         ])
         if block == 0:
             tables[1].wait()
-        gk_ref[:, lanes] = split_dot(inv_v[...], spectral_product(xs, bs, True))
+        turn_ref[:, lanes] = split_dot(inv_v[...], spectral_product(xs, bs, True))
+        stores += start_all([pltpu.make_async_copy(turn_ref.at[:, lanes], gk_ref.at[:, lanes], out_sem.at[block, 2])])
     wait_all(stores)
 
 
@@ -200,46 +206,48 @@
     wait_all(copies)
 
 
-def slope_body(par_ref, x_ref, b_ref, gk_ref, out_ref, suma_ref, sumb_ref, turn_ref, sem):
+def slope_body(par_ref, x_ref, b_ref, gk_hbm, out_ref, gk_ref, suma_ref, sumb_ref, turn_ref, sem, gk_sem):
     blocks, modes = par_ref.shape[0], par_ref.shape[1] // 2
     positions = x_ref.shape[0]
     tiles = positions // ROWS
-    half = modes // 2
     groups = suma_ref.shape[0] // LANES
     owners = out_ref.shape[0]
-
-    def step(block, carry):
+    fetch = pltpu.make_async_copy(gk_hbm, gk_ref, gk_sem)
+    fetch.start()
+
+    def reader(ref, block, weight=None):
         lanes = pl.ds(pl.multiple_of(block * LANES, LANES), LANES)
         phase = row_iota((ROWS, LANES)).astype(jnp.float32)
 
-        def late(tile):
-            return (positions - 1.0 - tile * ROWS - phase) * x_ref[pl.ds(tile * ROWS, ROWS), lanes]
-
-        def early(ref):
-            return lambda tile: (tile * float(ROWS) + phase) * ref[pl.ds(tile * ROWS, ROWS), lanes]
-
-        for part in range(2):
-            decay = par_ref[block, part * half : (part + 1) * half, :]
-            (up,), (down, plain, slope) = moments(
-                decay,
-                [(late, tiles)],
-                [
-                    (early(b_ref), tiles),
-                    (lambda tile: gk_ref[pl.ds(tile * ROWS, ROWS), lanes], tiles),
-                    (early(gk_ref), tiles),
-                ],
-            )
-            start = pl.multiple_of(block * 2 * modes, 2 * modes) + part * half
-            suma_ref[pl.ds(start, half), :] = down
-            suma_ref[pl.ds(start + modes, half), :] = up
-            sumb_ref[pl.ds(start, half), :] = plain
-            sumb_ref[pl.ds(start + modes, half), :] = slope
+        def read(tile):
+            value = ref[pl.ds(tile * ROWS, ROWS), lanes]
+            return value if weight is None else weight(tile * float(ROWS) + phase) * value
+
+        return read, tiles
+
+    def keep(ref, block, first, second):
+        start = pl.multiple_of(block * 2 * modes, 2 * modes)
+        ref[pl.ds(start, modes), :] = first
+        ref[pl.ds(start + modes, modes), :] = second
+
+    def outer(block, carry):
+        late = reader(x_ref, block, lambda t: positions - 1.0 - t)
+        (up,), (down,) = moments(par_ref[block, :modes, :], [late], [reader(b_ref, block, lambda t: t)])
+        keep(suma_ref, block, down, up)
         return carry
 
+    def inner(block, carry):
+        pair = [reader(gk_ref, block), reader(gk_ref, block, lambda t: t)]
+        _, (plain, slope) = moments(par_ref[block, :modes, :], [], pair)
+        keep(sumb_ref, block, plain, slope)
+        return carry
+
     copies = []
-    for group in range(groups):
-        lax.fori_loop(group * blocks // groups, (group + 1) * blocks // groups, step, 0)
-        for kind, ref in enumerate((suma_ref, sumb_ref)):
+    for kind, (step, ref) in enumerate(((outer, suma_ref), (inner, sumb_ref))):
+        if kind == 1:
+            fetch.wait()
+        for group in range(groups):
+            lax.fori_loop(group * blocks // groups, (group + 1) * blocks // groups, step, 0)
             slot = kind * groups + group
             turn_ref[slot] = turned(ref, group, owners)
             copies += start_all([pltpu.make_async_copy(turn_ref.at[slot], out_ref.at[:, groups + slot], sem.at[slot])])
@@ -253,9 +261,9 @@
 
 
 def local_body(
-    par_ref, skip_ref, x_ref, b_ref, xs_ref, bs_ref, fwd_ref, inv_ref,
-    pre_ref, gp_ref, token_ref,
-    k_ref, fwd_v, inv_v, spec_ref, table_sem, in_sem,
+    par_ref, x_ref, b_ref, skip_hbm, xs_ref, bs_ref, fwd_ref, inv_ref,
+    pre_ref, gp_ref,
+    skip_ref, k_ref, fwd_v, inv_v, spec_ref, turn_ref, table_sem, in_sem, out_sem,
 ):
     modes = par_ref.shape[1] // 2
     width = 2 * LANES
@@ -264,8 +272,9 @@
     tables = start_all([
         pltpu.make_async_copy(fwd_ref, fwd_v, table_sem.at[0]),
         pltpu.make_async_copy(inv_ref, inv_v, table_sem.at[1]),
+        pltpu.make_async_copy(skip_hbm, skip_ref, table_sem.at[2]),
     ])
-    fetch = []
+    fetch, stores = [], []
     for pair in range(count):
         lanes = pl.ds(pair * width, width)
         fetch.append(
@@ -274,30 +283,38 @@
                 for k, ref in enumerate((xs_ref, bs_ref))
             ])
         )
-    token_ref[...] = jnp.zeros(token_ref.shape, jnp.float32)
+
+    def impulse(block, carry):
+        phase = row_iota((ROWS, LANES)).astype(jnp.float32)
+        lanes = pl.ds(pl.multiple_of(block * LANES, LANES), LANES)
+        decay, residue = par_ref[block, :modes, :], par_ref[block, modes:, :]
+        weight = residue * jnp.sqrt(decay)
+        rates = [jnp.broadcast_to(decay[m : m + 1], (ROWS, LANES)) for m in range(modes)]
+        step8 = [jnp.exp(-float(ROWS) * rate) for rate in rates]
+        terms = [weight[m : m + 1] * jnp.exp(-rates[m] * phase) for m in range(modes)]
+        for tile in range(tiles):
+            k_ref[pl.ds(tile * ROWS, ROWS), lanes] = tree(terms)
+            if tile < tiles - 1:
+                terms = [t * s for t, s in zip(terms, step8)]
+        return carry
+
+    lax.fori_loop(0, 2 * count, impulse, 0)
     for pair in range(count):
-        phase = row_iota((ROWS, LANES)).astype(jnp.float32)
-        for side in range(2):
-            block = 2 * pair + side
-            decay, residue = par_ref[block, :modes, :], par_ref[block, modes:, :]
-            weight = residue * jnp.sqrt(decay)
-            rates = [jnp.broadcast_to(decay[m : m + 1], (ROWS, LANES)) for m in range(modes)]
-            step8 = [jnp.exp(-float(ROWS) * rate) for rate in rates]
-            terms = [weight[m : m + 1] * jnp.exp(-rates[m] * phase) for m in range(modes)]
-            for tile in range(tiles):
-                k_ref[pair % 2, pl.ds(tile * ROWS, ROWS), side * LANES : (side + 1) * LANES] = tree(terms)
-                if tile < tiles - 1:
-                    terms = [t * s for t, s in zip(terms, step8)]
         lanes = pl.ds(pair * width, width)
-        skip = jnp.concatenate([skip_ref[pl.ds(2 * pair, 1), :], skip_ref[pl.ds(2 * pair + 1, 1), :]], axis=1)
         if pair == 0:
             wait_all(tables)
-        ks = split_dot(fwd_v[...], k_ref[pair % 2])
+        skip = jnp.concatenate([skip_ref[pl.ds(2 * pair, 1), :], skip_ref[pl.ds(2 * pair + 1, 1), :]], axis=1)
+        ks = split_dot(fwd_v[...], k_ref[:, lanes])
         wait_all(fetch[pair])
         conv = split_dot(inv_v[...], spectral_product(ks, spec_ref[0, :, lanes], False))
-        pre_ref[:, lanes] = conv + skip * x_ref[:, lanes]
+        turn_ref[0, :, lanes] = conv + skip * x_ref[:, lanes]
         corr = split_dot(inv_v[...], spectral_product(ks, spec_ref[1, :, lanes], True))
-        gp_ref[:, lanes] = corr + skip * b_ref[:, lanes]
+        turn_ref[1, :, lanes] = corr + skip * b_ref[:, lanes]
+        stores += start_all([
+            pltpu.make_async_copy(turn_ref.at[k, :, lanes], ref.at[:, lanes], out_sem.at[pair, k])
+            for k, ref in enumerate((pre_ref, gp_ref))
+        ])
+    wait_all(stores)
 
 
 def lane_is_first(shape, modes):
@@ -331,7 +348,7 @@
     wait_all(copies)
 
 
-def slope_sum_body(r_ref, own_ref, acc_ref, rate_ref, token_ref, out_ref, pack_ref, sem, *, modes):
+def slope_sum_body(r_ref, own_ref, acc_ref, rate_ref, done_ref, out_ref, pack_ref, sem, *, modes):
     chunks, groups, rows = r_ref.shape[0], rate_ref.shape[0], r_ref.shape[2]
     first = lane_is_first((rows, LANES), modes)
     span = 2 * modes
@@ -372,22 +389,31 @@
 
 
 def out_body(
-    par_ref, r_ref, pre_ref, gp_ref, gate_hbm, key_hbm, value_hbm, cot_hbm,
-    mixed_ref, ggate_ref, gkey_ref, gvalue_ref,
-    hb_ref, gate_ref, key_ref, value_ref, cot_ref, sem,
+    par_ref, r_ref, pre_hbm, gp_hbm, gate_hbm, key_hbm, value_hbm, cot_hbm,
+    mixed_hbm, ggate_hbm, gkey_hbm, gvalue_hbm,
+    hb_ref, wide_ref, in_ref, out_ref, wide_sem, in_sem, out_sem,
 ):
     blocks, modes = par_ref.shape[0], par_ref.shape[1] // 2
     groups = hb_ref.shape[0] // LANES
     pack = 2 * ROWS
-    copies = start_all([
-        pltpu.make_async_copy(source, target, sem.at[k])
-        for k, (source, target) in enumerate(
-            zip((gate_hbm, key_hbm, value_hbm, cot_hbm), (gate_ref, key_ref, value_ref, cot_ref))
+    width = 2 * LANES
+    fetch = []
+    for pair in range(blocks // 2):
+        lanes = pl.ds(pair * width, width)
+        fetch.append(
+            start_all(
+                [
+                    pltpu.make_async_copy(ref.at[:, lanes], wide_ref.at[k, :, lanes], wide_sem.at[pair, k])
+                    for k, ref in enumerate((pre_hbm, gp_hbm))
+                ]
+                + [
+                    pltpu.make_async_copy(ref.at[:, lanes], in_ref.at[k, :, lanes], in_sem.at[pair, k])
+                    for k, ref in enumerate((gate_hbm, cot_hbm, value_hbm, key_hbm))
+                ]
+            )
         )
-    ])
     for group in range(groups):
         hb_ref[pl.ds(group * LANES, LANES), :] = r_ref[:, group].reshape(LANES, LANES).T
-    wait_all(copies)
 
     def step(block, carry):
         lanes = pl.ds(pl.multiple_of(block * LANES, LANES), LANES)
@@ -399,30 +425,40 @@
         last = weight * hb_ref[pl.ds(start + modes, modes), :]
         rates = [jnp.broadcast_to(decay[m : m + 1], (ROWS, LANES)) for m in range(modes)]
         step8 = [jnp.exp(-float(ROWS) * rate) for rate in rates]
+        count = in_ref.shape[1] // pack
+
+        def finish(kind, place, extra):
+            rows = pl.ds(place * pack, pack)
+            total = wide_ref[kind, rows, lanes] + extra
+            for k in (2 * kind, 2 * kind + 1):
+                out_ref[k, rows, lanes] = (in_ref[k, rows, lanes].astype(jnp.float32) * total).astype(jnp.bfloat16)
+
         terms = [first[m : m + 1] * jnp.exp(-rates[m] * (phase + 1.0)) for m in range(modes)]
-        count = pre_ref.shape[0] // pack
         for place in range(count):
             lower = tree(terms)
             terms = [t * s for t, s in zip(terms, step8)]
             upper = tree(terms)
             terms = [t * s for t, s in zip(terms, step8)]
-            rows = pl.ds(place * pack, pack)
-            pre = pre_ref[rows, lanes] + jnp.concatenate([lower, upper], axis=0)
-            mixed_ref[rows, lanes] = (gate_ref[rows, lanes].astype(jnp.float32) * pre).astype(jnp.bfloat16)
-            ggate_ref[rows, lanes] = (cot_ref[rows, lanes].astype(jnp.float32) * pre).astype(jnp.bfloat16)
+            finish(0, place, jnp.concatenate([lower, upper], axis=0))
         terms = [last[m : m + 1] * jnp.exp(-rates[m] * (ROWS - phase)) for m in range(modes)]
         for place in reversed(range(count)):
             upper = tree(terms)
             terms = [t * s for t, s in zip(terms, step8)]
             lower = tree(terms)
             terms = [t * s for t, s in zip(terms, step8)]
-            rows = pl.ds(place * pack, pack)
-            grad = gp_ref[rows, lanes] + jnp.concatenate([lower, upper], axis=0)
-            gkey_ref[rows, lanes] = (grad * value_ref[rows, lanes].astype(jnp.float32)).astype(jnp.bfloat16)
-            gvalue_ref[rows, lanes] = (grad * key_ref[rows, lanes].astype(jnp.float32)).astype(jnp.bfloat16)
+            finish(1, place, jnp.concatenate([lower, upper], axis=0))
         return carry
 
-    lax.fori_loop(0, blocks, step, 0)
+    stores = []
+    for pair in range(blocks // 2):
+        lanes = pl.ds(pair * width, width)
+        wait_all(fetch[pair])
+        lax.fori_loop(2 * pair, 2 * pair + 2, step, 0)
+        stores += start_all([
+            pltpu.make_async_copy(out_ref.at[k, :, lanes], ref.at[:, lanes], out_sem.at[pair, k])
+            for k, ref in enumerate((mixed_hbm, ggate_hbm, gkey_hbm, gvalue_hbm))
+        ])
+    wait_all(stores)
 
 
 def on_device(gate_in, key_in, value_in, cotangent, skip, residue, decay):
@@ -437,15 +473,15 @@
     forward, inverse = (jnp.asarray(t) for t in transform_tables(length))
     whole = (length, channels)
     size = length * channels
-    dense = pltpu.VMEM(whole, bf16)
+    wide = pltpu.VMEM(whole, f32)
     tables = [pltpu.VMEM(forward.shape, bf16), pltpu.VMEM(inverse.shape, bf16)]
     spectra = pltpu.VMEM((2, 2 * length, channels), f32)
     pairs = channels // (2 * LANES)
     sums = pltpu.VMEM((groups * LANES, LANES), f32)
     tile = (share, LANES)
 
-    (sent,) = call(spread_body, [((blocks, 2 * modes, LANES), f32, HBM)], 4, (0, 10**5), [DMA((2, blocks))])(
-        [ANY] * 2, decay.T, residue.T
+    (sent,) = call(spread_body, [((blocks, 2 * modes, LANES), f32, HBM)], 4, (0, 10**5), [pltpu.VMEM((2 * modes, LANES), f32), DMA((2,)), DMA((blocks,))])(
+        [HBM] * 2, decay.T, residue.T
     )
     params = lax.all_to_all(sent, "ch", 0, 0, tiled=True)
 
@@ -453,11 +489,11 @@
         product_body,
         [(whole, f32, VMEM)] * 2
         + [((2 * length, channels), f32, HBM)] * 2
-        + [(whole, f32, VMEM), ((blocks, LANES), f32, VMEM)],
+        + [(whole, f32, HBM), ((blocks, LANES), f32, VMEM)],
         24,
         (18 * length * size, 36 * size),
-        [pltpu.VMEM((4, *whole), bf16), *tables, spectra, DMA((pairs, 4)), DMA((2,)), DMA((pairs, 2))],
-    )([ANY] * 6, gate_in, key_in, value_in, cotangent, forward, inverse)
+        [pltpu.VMEM((4, *whole), bf16), *tables, spectra, wide, DMA((pairs, 4)), DMA((2,)), DMA((pairs, 3))],
+    )([HBM] * 6, gate_in, key_in, value_in, cotangent, forward, inverse)
 
     states, rates = call(
         state_body,
@@ -473,8 +509,8 @@
         [((owners, 3 * groups, *tile), f32, HBM)],
         8,
         (128 * size, 12 * size),
-        [sums, sums, pltpu.VMEM((2 * groups, owners, *tile), f32), DMA((2 * groups,))],
-    )([VMEM] * 4, params, x, b, gk)
+        [wide, sums, sums, pltpu.VMEM((2 * groups, owners, *tile), f32), DMA((2 * groups,)), DMA],
+    )([VMEM] * 3 + [HBM], params, x, b, gk)
 
     bundle, heads, acc, grad_skip = call(
         functools.partial(scan_body, modes=modes, length=length),
@@ -491,13 +527,14 @@
     )([VMEM, VMEM, HBM], states, rates, slopes)
     arrived = lax.all_to_all(bundle, "ctx", 0, 0, tiled=True)
 
-    pre, gp, token = call(
+    pre, gp = call(
         local_body,
-        [(whole, f32, VMEM)] * 2 + [((ROWS, LANES), f32, VMEM)],
+        [(whole, f32, HBM)] * 2,
         24,
         (18 * length * size, 36 * size),
-        [pltpu.VMEM((2, length, 2 * LANES), f32), *tables, spectra, DMA((2,)), DMA((pairs, 2))],
-    )([VMEM] * 4 + [ANY] * 4, params, skip.reshape(blocks, LANES), x, b, xs, bs, forward, inverse)
+        [pltpu.VMEM((blocks, LANES), f32), wide, *tables, spectra]
+        + [pltpu.VMEM((2, *whole), f32), DMA((3,)), DMA((pairs, 2)), DMA((pairs, 2))],
+    )([VMEM] * 3 + [HBM] * 5, params, x, b, skip.reshape(blocks, LANES), xs, bs, forward, inverse)
 
     packed = (owners, blocks, share * 2 * modes // LANES, LANES)
     (grads,) = call(
@@ -506,16 +543,17 @@
         8,
         (10**5, 10**6),
         [pltpu.VMEM(packed[1:], f32), DMA((owners,))],
-    )([VMEM] * 4 + [ANY], arrived, heads, acc, rates, token)
+    )([VMEM] * 4 + [HBM], arrived, heads, acc, rates, pre)
     grads = lax.all_to_all(grads.reshape(owners * blocks, *packed[2:]), ("ctx", "ch"), 0, 0, tiled=True)
 
     mixed, grad_gate, grad_key, grad_value = call(
         out_body,
-        [(whole, bf16, VMEM)] * 4,
+        [(whole, bf16, HBM)] * 4,
         16,
         (64 * size, 20 * size),
-        [sums, dense, dense, dense, dense, DMA((4,))],
-    )([VMEM] * 4 + [ANY] * 4, params, arrived, pre, gp, gate_in, key_in, value_in, cotangent)
+        [sums, pltpu.VMEM((2, *whole), f32), pltpu.VMEM((4, *whole), bf16), pltpu.VMEM((4, *whole), bf16)]
+        + [DMA((pairs, 2)), DMA((pairs, 4)), DMA((pairs, 4))],
+    )([VMEM] * 2 + [HBM] * 6, params, arrived, pre, gp, gate_in, key_in, value_in, cotangent)
 
     grad_residue, grad_log_decay = call(
         final_body, [((modes, filters), f32, VMEM)] * 2, 8, (10**5, 10**6), [pltpu.VMEM((LANES, LANES), f32)]

time: 90.8 us -> 71 us (0.78)
  local copies, waits for them, and re-layouts: 27.6 us -> 0.01 us
  waiting for transfers between devices: 0.01 us -> 5.16 us
  Pallas kernels: 31.1 us -> 35.4 us
    unnamed x58 -> x4, local copies, waits for them, and re-layouts: 27.6 us -> 0.01 us
    all_to_all x1, waiting for transfers between devices: 0.01 us -> 4.32 us  [on_device(): lax.all_to_all(grads.reshape(owners * blocks, *packed[2:]), ('ctx', 'ch')...]
    pallas_call x9, Pallas kernels: 31.1 us -> 35.4 us  [call(): pl.pallas_call(body, out_shape=[pltpu.HBM(s, t) if w is HBM else jax.Shap...]
    all_to_all x1, starting transfers between devices: 10.4 us -> 9.33 us  [on_device(): lax.all_to_all(grads.reshape(owners * blocks, *packed[2:]), ('ctx', 'ch')...]
  transfers between devices with their start and end apart: 4 -> 4, of which waited for: 0 -> 3; matrix products, arithmetic and copies ran while one was open for 0% -> 0% of each run, Pallas kernels for 27% -> 39%
where the time goes in v3:
time: 71 us; the launch traced here: 70.5 us
  Pallas kernels  35.4 us (50%)
  starting transfers between devices  29.2 us (41%)
  waiting for transfers between devices  5.16 us (7%)
  between operations  0.73 us (1%)
    pallas_call x9, Pallas kernels, call(): pl.pallas_call(body, out_shape=[pltpu.HBM(s, t) if w is HBM else jax.Shap...  35.4 us
    all_to_all x1, starting transfers between devices, on_device(): lax.all_to_all(grads.reshape(owners * blocks, *packed[2:]), ('ctx', 'ch')...  9.33 us
    all_to_all x1, starting transfers between devices, on_device(): params = lax.all_to_all(sent, 'ch', 0, 0, tiled=True)  7.49 us
    all_to_all x1, starting transfers between devices, on_device(): states = lax.all_to_all(states, 'ctx', 0, 0, tiled=True)  6.78 us
    all_to_all x1, starting transfers between devices, on_device(): arrived = lax.all_to_all(bundle, 'ctx', 0, 0, tiled=True)  5.59 us
    all_to_all x1, waiting for transfers between devices, on_device(): lax.all_to_all(grads.reshape(owners * blocks, *packed[2:]), ('ctx', 'ch')...  4.32 us
  transfers between devices with their start and end apart: 4, of which 3 were waited for; matrix products, arithmetic and copies ran while one was open for 0% of the time, Pallas kernels for 39%

profile of v3, /device:TPU:1, one launch (start us, length us, event | category | flops | bytes accessed | tf_op | source)
XLA Modules:
  0.0 70.5 jit_solution(8233221351059978108)
XLA Ops:
  0.6 1.4 %shard_map.144 = f32[8,32,128]{2,1,0:T(8,128)} custom-call(f32[16,128]{1,0:T(8,128)} %bitcast.10, f32[16,128]{1,0:T(8,128)} %bitcast.12), custom_call_target="tpu_custom_call" | custom-call | bytes 100000 | tf_op jit(solution)/shard_map/pallas_call | solution.py:21
  2.1 7.5 %all-to-all-start = ((f32[8,32,128]{2,1,0:T(8,128)}), f32[8,32,128]{2,1,0:T(8,128)S(1)}, u32[]{:S(2)}, u32[]{:S(2)}) async-start(f32[8,32,128]{2,1,0:T(8,128)} %shard_map.144), calls=%async_computation | async-start | bytes 262144 | tf_op jit(solution)/shard_map/all_to_all | solution.py:486
  9.6 7.5 %shard_map.145 = (f32[256,1024]{1,0:T(8,128)S(1)}, f32[256,1024]{1,0:T(8,128)S(1)}, f32[512,1024]{1,0:T(8,128)}, f32[512,1024]{1,0:T(8,128)}, f32[256,1024]{1,0:T(8,128)}, /*index=5*/f32[8,128]{1,0:T(8,128)S(1)}) custom-call(bf16[256,1024]{1,0:T(8,128)(2,1)} %gate_hbm.1, bf16[256,1024]{1,0:T(8,128)(2,1)} %key_hbm.1, bf16[256,1024]{1,0:T(8,128)(2,1)} %value_hbm.1, ...), custom_call_target="tpu_custom_call" | custom-call | flops 1207959552 | bytes 9437184 | tf_op jit(solution)/shard_map/pallas_call | solution.py:21
  17.1 0.0 all-to-all-done.par_ref
  17.1 3.5 %shard_map.146 = (f32[16,3,8,128]{3,2,1,0:T(8,128)}, f32[2,8,128]{2,1,0:T(8,128)S(1)}) custom-call(s32[1]{0:T(128)} %bitcast.2.index_ref, f32[8,32,128]{2,1,0:T(8,128)S(1)} %all-to-all-done.par_ref, f32[256,1024]{1,0:T(8,128)S(1)} %get-tuple-element.27.x_ref, f32[256,1024]{1,0:T(8,128)S(1)} %get-tuple-element.28.b_ref, f32[8,128]{1,0:T(8,128)S(1)} %get-tuple-element.29.sk_ref), custom_call_target="tpu_custom_call" | custom-call | flops 16777216 | bytes 2097152 | tf_op jit(solution)/shard_map/pallas_call | solution.py:21
  20.6 6.8 %all-to-all-start.1 = ((f32[16,3,8,128]{3,2,1,0:T(8,128)}), f32[16,3,8,128]{3,2,1,0:T(8,128)S(1)}, u32[]{:S(2)}, u32[]{:S(2)}) async-start(f32[16,3,8,128]{3,2,1,0:T(8,128)} %get-tuple-element.30), calls=%async_computation.1 | async-start | bytes 393216 | tf_op jit(solution)/shard_map/all_to_all | solution.py:505
  27.4 6.5 %shard_map.147.slopes_ref = f32[16,6,8,128]{3,2,1,0:T(8,128)} custom-call(f32[8,32,128]{2,1,0:T(8,128)S(1)} %all-to-all-done.par_ref, f32[256,1024]{1,0:T(8,128)S(1)} %get-tuple-element.27.x_ref, f32[256,1024]{1,0:T(8,128)S(1)} %get-tuple-element.28.b_ref, f32[256,1024]{1,0:T(8,128)} %get-tuple-element.32.gk_hbm), custom_call_target="tpu_custom_call" | custom-call | flops 33554432 | bytes 3145728 | tf_op jit(solution)/shard_map/pallas_call | solution.py:21
  33.9 0.2 all-to-all-done.1.s_ref
  34.1 1.3 %shard_map.148 = (f32[16,6,8,128]{3,2,1,0:T(8,128)}, f32[2,16,8,128]{3,2,1,0:T(8,128)S(1)}, f32[2,8,128]{2,1,0:T(8,128)S(1)}, f32[8,128]{1,0:T(8,128)}) custom-call(f32[16,3,8,128]{3,2,1,0:T(8,128)S(1)} %all-to-all-done.1.s_ref, f32[2,8,128]{2,1,0:T(8,128)S(1)} %get-tuple-element.31.rate_ref, ...), custom_call_target="tpu_custom_call", output_to_operand_aliasing={{0}: (2, {})} | custom-call | flops 100000 | bytes 1000000 | tf_op jit(solution)/shard_map/pallas_call | solution.py:21
  35.4 5.6 %all-to-all-start.2 = ((f32[16,6,8,128]{3,2,1,0:T(8,128)}), f32[16,6,8,128]{3,2,1,0:T(8,128)S(1)}, u32[]{:S(2)}, u32[]{:S(2)}) async-start(f32[16,6,8,128]{3,2,1,0:T(8,128)} %get-tuple-element.33), calls=%async_computation.2 | async-start | bytes 786432 | tf_op jit(solution)/shard_map/all_to_all | solution.py:528
  41.0 7.7 %shard_map.149 = (f32[256,1024]{1,0:T(8,128)}, f32[256,1024]{1,0:T(8,128)}) custom-call(f32[8,32,128]{2,1,0:T(8,128)S(1)} %all-to-all-done.par_ref, f32[256,1024]{1,0:T(8,128)S(1)} %get-tuple-element.27.x_ref, f32[256,1024]{1,0:T(8,128)S(1)} %get-tuple-element.28.b_ref, f32[8,128]{1,0:T(8,128)} %bitcast.15, f32[512,1024]{1,0:T(8,128)} %get-tuple-element.34.xs_ref, ...), custom_call_target="tpu_custom_call" | custom-call | flops 1207959552 | bytes 9437184 | tf_op jit(solution)/shard_map/pallas_call | solution.py:21
  48.7 0.7 all-to-all-done.2.r_ref
  49.4 1.0 %shard_map.151 = f32[16,8,2,128]{3,2,1,0:T(2,128)} custom-call(f32[16,6,8,128]{3,2,1,0:T(8,128)S(1)} %all-to-all-done.2.r_ref, f32[2,16,8,128]{3,2,1,0:T(8,128)S(1)} %get-tuple-element.43.own_ref, f32[2,8,128]{2,1,0:T(8,128)S(1)} %get-tuple-element.44.acc_ref, f32[2,8,128]{2,1,0:T(8,128)S(1)} %get-tuple-element.31.rate_ref, ...), custom_call_target="tpu_custom_call" | custom-call | flops 100000 | bytes 1000000 | tf_op jit(solution)/shard_map/pallas_call | solution.py:21
  50.4 9.3 %all-to-all-start.3 = ((f32[128,2,128]{2,1,0:T(2,128)}), f32[128,2,128]{2,1,0:T(2,128)S(1)}, u32[]{:S(2)}, u32[]{:S(2)}) async-start(f32[128,2,128]{2,1,0:T(2,128)} %bitcast.14), calls=%async_computation.3 | async-start | bytes 262144 | tf_op jit(solution)/shard_map/all_to_all | solution.py:547
  59.7 0.0 copy-start
  59.7 0.0 copy-start.1
  59.7 5.6 %shard_map.150 = (bf16[256,1024]{1,0:T(8,128)(2,1)}, bf16[256,1024]{1,0:T(8,128)(2,1)}, bf16[256,1024]{1,0:T(8,128)(2,1)}, bf16[256,1024]{1,0:T(8,128)(2,1)}) custom-call(f32[8,32,128]{2,1,0:T(8,128)S(1)} %all-to-all-done.par_ref, f32[16,6,8,128]{3,2,1,0:T(8,128)S(1)} %all-to-all-done.2.r_ref, f32[256,1024]{1,0:T(8,128)} %get-tuple-element.36.pre_hbm.done_ref, ...), custom_call_target="tpu_custom_call" | custom-call | flops 16777216 | bytes 5242880 | tf_op jit(solution)/shard_map/pallas_call | solution.py:21
  65.4 4.3 %all-to-all-done.3 = f32[128,2,128]{2,1,0:T(2,128)S(1)} async-done(((f32[128,2,128]{2,1,0:T(2,128)}), f32[128,2,128]{2,1,0:T(2,128)S(1)}, u32[]{:S(2)}, u32[]{:S(2)}) %all-to-all-start.3) | async-done | bytes 131104 | tf_op jit(solution)/shard_map/all_to_all | solution.py:547
  69.7 0.0 copy-done
  69.7 0.0 copy-done.1
  69.7 0.8 %shard_map.152 = (f32[16,128]{1,0:T(8,128)}, f32[16,128]{1,0:T(8,128)}) custom-call(f32[16,8,2,128]{3,2,1,0:T(2,128)S(1)} %bitcast.9, f32[16,128]{1,0:T(8,128)S(1)} %bitcast.13, f32[16,128]{1,0:T(8,128)S(1)} %bitcast.11), custom_call_target="tpu_custom_call" | custom-call | flops 100000 | bytes 1000000 | tf_op jit(solution)/shard_map/pallas_call | solution.py:21
Async XLA Ops:
  2.1 15.0 %all-to-all-start = ((f32[8,32,128]{2,1,0:T(8,128)}), f32[8,32,128]{2,1,0:T(8,128)S(1)}, u32[]{:S(2)}, u32[]{:S(2)}) async-start(f32[8,32,128]{2,1,0:T(8,128)} %shard_map.144), calls=%async_computation | async-start | bytes 262144 | tf_op jit(solution)/shard_map/all_to_all | solution.py:486
  20.6 13.5 %all-to-all-start.1 = ((f32[16,3,8,128]{3,2,1,0:T(8,128)}), f32[16,3,8,128]{3,2,1,0:T(8,128)S(1)}, u32[]{:S(2)}, u32[]{:S(2)}) async-start(f32[16,3,8,128]{3,2,1,0:T(8,128)} %get-tuple-element.30), calls=%async_computation.1 | async-start | bytes 393216 | tf_op jit(solution)/shard_map/all_to_all | solution.py:505
  35.4 14.0 %all-to-all-start.2 = ((f32[16,6,8,128]{3,2,1,0:T(8,128)}), f32[16,6,8,128]{3,2,1,0:T(8,128)S(1)}, u32[]{:S(2)}, u32[]{:S(2)}) async-start(f32[16,6,8,128]{3,2,1,0:T(8,128)} %get-tuple-element.33), calls=%async_computation.2 | async-start | bytes 786432 | tf_op jit(solution)/shard_map/all_to_all | solution.py:528
  50.4 19.3 %all-to-all-start.3 = ((f32[128,2,128]{2,1,0:T(2,128)}), f32[128,2,128]{2,1,0:T(2,128)S(1)}, u32[]{:S(2)}, u32[]{:S(2)}) async-start(f32[128,2,128]{2,1,0:T(2,128)} %bitcast.14), calls=%async_computation.3 | async-start | bytes 262144 | tf_op jit(solution)/shard_map/all_to_all | solution.py:547
  59.7 10.0 %copy-start = (f32[128,16]{0,1:T(8,128)S(1)}, f32[128,16]{0,1:T(8,128)}, u32[]{:S(2)}) copy-start(f32[128,16]{0,1:T(8,128)} %param.15) | copy-start | bytes 24580
  59.7 10.0 %copy-start.1 = (f32[128,16]{0,1:T(8,128)S(1)}, f32[128,16]{0,1:T(8,128)}, u32[]{:S(2)}) copy-start(f32[128,16]{0,1:T(8,128)} %param.14) | copy-start | bytes 24580

commit v4 on v3

v4 whole, which is shorter than its diff:
```python
import functools

import jax
import jax.numpy as jnp
from jax import lax
from jax.experimental import pallas as pl
from jax.experimental.pallas import tpu as pltpu
from jax.sharding import PartitionSpec as P

LANES = 128
ROWS = 8
SPAN = 16
VMEM = pl.BlockSpec(memory_space=pltpu.VMEM)
SMEM = pl.BlockSpec(memory_space=pltpu.SMEM)
HBM = pl.BlockSpec(memory_space=pltpu.HBM)
DMA = pltpu.SemaphoreType.DMA


def call(body, outs, limit_mib, cost, scratch=(), aliases=None):
    flops, moved = cost
    return lambda specs, *args: pl.pallas_call(
        body,
        out_shape=[pltpu.HBM(s, t) if w is HBM else jax.ShapeDtypeStruct(s, t) for s, t, w in outs],
        in_specs=list(specs),
        out_specs=[w for _, _, w in outs],
        scratch_shapes=list(scratch),
        input_output_aliases=aliases or {},
        compiler_params=pltpu.CompilerParams(vmem_limit_bytes=limit_mib * 2**20),
        cost_estimate=pl.CostEstimate(flops=flops, bytes_accessed=moved, transcendentals=0),
    )(*(pltpu.with_memory_space_constraint(a, pltpu.HBM) if w is HBM else a for w, a in zip(specs, args)))


def start_all(copies):
    for copy in copies:
        copy.start()
    return copies


def wait_all(copies):
    for copy in copies:
        copy.wait()


def spread_body(decay_ref, residue_ref, out_ref, held_ref, in_sem, out_sem):
    modes, blocks = decay_ref.shape[0], out_ref.shape[0]
    wait_all(
        start_all([
            pltpu.make_async_copy(ref, held_ref.at[pl.ds(k * modes, modes)], in_sem.at[k])
            for k, ref in enumerate((decay_ref, residue_ref))
        ])
    )
    wait_all(start_all([pltpu.make_async_copy(held_ref, out_ref.at[k], out_sem.at[k]) for k in range(blocks)]))


def tree(values):
    while len(values) > 1:
        odd = values[-1:] if len(values) % 2 else []
        values = [a + b for a, b in zip(values[::2], values[1::2])] + odd
    return values[0]


def turned(scratch_ref, group, owners):
    return scratch_ref[pl.ds(group * LANES, LANES), :].T.reshape(owners, LANES // owners, LANES)


def by_mode(ref, row, blocks):
    return ref[pl.ds(row, blocks, stride=ref.shape[0] // blocks), :]


def product_body(
    gate_hbm, key_hbm, value_hbm, cot_hbm,
    x_ref, b_ref, sk_ref,
    in_ref, sem,
):
    length, channels = gate_hbm.shape
    blocks = channels // LANES
    pieces = sem.shape[0]
    depth = length // pieces
    fetch = [
        start_all([
            pltpu.make_async_copy(ref.at[pl.ds(p * depth, depth)], in_ref.at[k, pl.ds(p * depth, depth)], sem.at[p, k])
            for k, ref in enumerate((gate_hbm, key_hbm, value_hbm, cot_hbm))
        ])
        for p in range(pieces)
    ]

    def step(place, sums):
        rows = pl.ds(pl.multiple_of(place * SPAN, SPAN), SPAN)
        after = []
        for block in range(blocks):
            lanes = pl.ds(block * LANES, LANES)
            gate, key, value, cot = (in_ref[k, rows, lanes].astype(jnp.float32) for k in range(4))
            x, b = key * value, cot * gate
            for part in range(SPAN // ROWS):
                target = pl.ds((place * SPAN + part * ROWS) * blocks + block, ROWS, stride=blocks)
                x_ref[target, :] = x[part * ROWS : (part + 1) * ROWS]
                b_ref[target, :] = b[part * ROWS : (part + 1) * ROWS]
            both = x * b
            after.append(sums[block] + tree([both[k * ROWS : (k + 1) * ROWS] for k in range(SPAN // ROWS)]))
        return tuple(after)

    sums = tuple(jnp.zeros((ROWS, LANES), jnp.float32) for _ in range(blocks))
    for p in range(pieces):
        wait_all(fetch[p])
        sums = lax.fori_loop(p * depth // SPAN, (p + 1) * depth // SPAN, step, sums)
    for block in range(blocks):
        sk_ref[pl.ds(block, 1), :] = jnp.sum(sums[block], axis=0, keepdims=True)


def state_body(
    index_ref, par_ref, x_ref, b_ref, sk_ref,
    out_ref, hs_hbm, bs_hbm, rate_ref,
    sums_ref, rates_ref, turn_ref, hs_ref, bs_ref, sem, snap_sem,
):
    owners, share = out_ref.shape[0], out_ref.shape[2]
    groups = sums_ref.shape[0] // LANES
    blocks = sk_ref.shape[0]
    modes = par_ref.shape[0] // blocks // 2
    spans = hs_ref.shape[0]
    pieces = snap_sem.shape[1]
    part = spans // pieces
    for owner in range(owners):
        turn_ref[groups, owner, :blocks] = sk_ref[...]
    copies = start_all([pltpu.make_async_copy(turn_ref.at[groups], out_ref.at[:, groups], sem.at[groups])])
    for group in range(groups):
        for block in range(group * blocks // groups, (group + 1) * blocks // groups):
            decay = par_ref[pl.ds(block * 2 * modes, modes), :]
            rates_ref[pl.ds(block * 2 * modes, 2 * modes), :] = jnp.concatenate([decay, decay], axis=0)
        rates_ref[pl.ds(group * LANES, LANES), :] = rates_ref[pl.ds(group * LANES, LANES), :].T
        rate_ref[group] = rates_ref[pl.ds(pl.multiple_of(group * LANES + index_ref[0] * share, share), share), :]
    factor = [jnp.exp(-by_mode(par_ref, m, blocks)) for m in range(modes)]

    def step(span, carry):
        ups, downs = carry
        mirror = spans - 1 - span
        for m in range(modes):
            hs_ref[span, pl.ds(m * blocks, blocks), :] = ups[m]
            bs_ref[mirror + 1, pl.ds(m * blocks, blocks), :] = downs[m]
        for r in range(SPAN):
            x = x_ref[pl.ds(pl.multiple_of((span * SPAN + r) * blocks, blocks), blocks), :]
            b = b_ref[pl.ds(pl.multiple_of((mirror * SPAN + SPAN - 1 - r) * blocks, blocks), blocks), :]
            ups = tuple(f * u + x for f, u in zip(factor, ups))
            downs = tuple(f * d + b for f, d in zip(factor, downs))
        return ups, downs

    zero = tuple(jnp.zeros((blocks, LANES), jnp.float32) for _ in range(modes))
    ups, downs = zero, zero
    for p in range(pieces):
        ups, downs = lax.fori_loop(p * part, (p + 1) * part, step, (ups, downs))
        here, there = pl.ds(p * part, part), pl.ds((pieces - 1 - p) * part + 1, part)
        copies += start_all([
            pltpu.make_async_copy(hs_ref.at[here], hs_hbm.at[here], snap_sem.at[0, p]),
            pltpu.make_async_copy(bs_ref.at[there], bs_hbm.at[there], snap_sem.at[1, p]),
        ])
    for m in range(modes):
        bs_ref[0, pl.ds(m * blocks, blocks), :] = downs[m]
        sums_ref[pl.ds(m, blocks, stride=2 * modes), :] = ups[m]
        sums_ref[pl.ds(modes + m, blocks, stride=2 * modes), :] = downs[m]
    copies += start_all([pltpu.make_async_copy(bs_ref.at[0], bs_hbm.at[0], sem.at[groups + 1])])
    for group in range(groups):
        turn_ref[group] = turned(sums_ref, group, owners)
        copies += start_all([pltpu.make_async_copy(turn_ref.at[group], out_ref.at[:, group], sem.at[group])])
    wait_all(copies)


def slope_body(
    par_ref, x_ref, b_ref, hs_hbm, bs_hbm,
    out_ref,
    hs_ref, bs_ref, lag_ref, run_ref, suma_ref, sumb_ref, turn_ref, sem, snap_sem,
):
    owners = out_ref.shape[0]
    groups = suma_ref.shape[0] // LANES
    spans = hs_ref.shape[0]
    blocks = x_ref.shape[0] // (spans * SPAN)
    modes = par_ref.shape[0] // blocks // 2
    pieces = snap_sem.shape[1]
    part = spans // pieces
    fetch = []
    for p in range(pieces):
        here = pl.ds(p * part, part)
        there = pl.ds(p * part + (1 if p else 0), part + (0 if p else 1))
        fetch.append(
            start_all([
                pltpu.make_async_copy(hs_hbm.at[here], hs_ref.at[here], snap_sem.at[0, p]),
                pltpu.make_async_copy(bs_hbm.at[there], bs_ref.at[there], snap_sem.at[1, p]),
            ])
        )
    zero = jnp.zeros((blocks, LANES), jnp.float32)
    SLOPE, SUM0, SUM1, DOWN, POWER, FACTOR, FAR = range(7)
    for m in range(modes):
        rate = by_mode(par_ref, m, blocks)
        rows = pl.ds(m * blocks, blocks)
        for kind in (SLOPE, SUM0, SUM1, DOWN):
            run_ref[kind, rows, :] = zero
        run_ref[POWER, rows, :] = zero + 1.0
        run_ref[FACTOR, rows, :] = jnp.exp(-rate)
        run_ref[FAR, rows, :] = jnp.exp(-float(SPAN) * rate)
    for u in range(SPAN):
        lag_ref[pl.ds(u * blocks, blocks), :] = zero

    def step(span, carry):
        def at(ref, r):
            return ref[pl.ds(pl.multiple_of((span * SPAN + r) * blocks, blocks), blocks), :]

        x = [at(x_ref, r) for r in range(SPAN)]
        b = [at(b_ref, r) for r in range(SPAN)]
        for u in range(SPAN):
            rows = pl.ds(u * blocks, blocks)
            total = lag_ref[rows, :]
            for r in range(SPAN - u):
                total = total + b[r + u] * x[r]
            lag_ref[rows, :] = total
        late = [x[r] * (SPAN - 1.0 - r) for r in range(SPAN - 1)]
        early = [b[r] * float(r) for r in range(SPAN - 1, 0, -1)]
        begin = (span * SPAN).astype(jnp.float32)
        for m in range(modes):
            rows = pl.ds(m * blocks, blocks)
            factor, far = run_ref[FACTOR, rows, :], run_ref[FAR, rows, :]
            up, down = late[0], early[0]
            for k in range(1, SPAN - 1):
                up = factor * up + late[k]
                down = factor * down + early[k]
            up, down = factor * up, factor * down
            head = hs_ref[span, rows, :]
            own = bs_ref[span, rows, :] - far * bs_ref[span + 1, rows, :]
            slope, power = run_ref[SLOPE, rows, :], run_ref[POWER, rows, :]
            run_ref[SUM0, rows, :] = run_ref[SUM0, rows, :] + head * own
            run_ref[SUM1, rows, :] = run_ref[SUM1, rows, :] + (slope * own + head * (own + down))
            run_ref[DOWN, rows, :] = run_ref[DOWN, rows, :] + power * (begin * own + down)
            run_ref[POWER, rows, :] = power * far
            run_ref[SLOPE, rows, :] = far * (slope + float(SPAN) * head) + up
        return carry

    for p in range(pieces):
        wait_all(fetch[p])
        lax.fori_loop(p * part, (p + 1) * part, step, 0)
    lags = [lag_ref[pl.ds(u * blocks, blocks), :] for u in range(SPAN)]
    for m in range(modes):
        rows = pl.ds(m * blocks, blocks)
        factor = run_ref[FACTOR, rows, :]
        plain, slope = lags[SPAN - 1], lags[SPAN - 1] * (SPAN - 1.0)
        for u in range(SPAN - 2, -1, -1):
            plain = factor * plain + lags[u]
            slope = factor * slope + lags[u] * float(u)
        low, high = pl.ds(m, blocks, stride=2 * modes), pl.ds(modes + m, blocks, stride=2 * modes)
        suma_ref[low, :] = run_ref[DOWN, rows, :]
        suma_ref[high, :] = run_ref[SLOPE, rows, :]
        sumb_ref[low, :] = factor * run_ref[SUM0, rows, :] + plain
        sumb_ref[high, :] = factor * run_ref[SUM1, rows, :] + slope
    copies = []
    for kind, ref in enumerate((suma_ref, sumb_ref)):
        for group in range(groups):
            slot = kind * groups + group
            turn_ref[slot] = turned(ref, group, owners)
            copies += start_all([pltpu.make_async_copy(turn_ref.at[slot], out_ref.at[:, groups + slot], sem.at[slot])])
    wait_all(copies)


def local_body(par_ref, x_ref, b_ref, skip_hbm, y_hbm, z_hbm, skip_ref, out_ref, skip_sem, sem):
    fetch = pltpu.make_async_copy(skip_hbm, skip_ref, skip_sem)
    fetch.start()
    blocks = skip_ref.shape[0]
    modes = par_ref.shape[0] // blocks // 2
    spans = x_ref.shape[0] // blocks // SPAN
    pieces = sem.shape[1]
    part = spans // pieces
    factors, terms = [], []
    for m in range(modes):
        rate = by_mode(par_ref, m, blocks)
        factors.append(jnp.exp(-rate))
        terms.append(by_mode(par_ref, modes + m, blocks) * jnp.sqrt(rate))
    kernel = []
    for u in range(SPAN):
        kernel.append(tree(terms))
        terms = [t * f for t, f in zip(terms, factors)]
    fetch.wait()
    kernel[0] = kernel[0] + skip_ref[...]

    def step(span, carry):
        def at(r):
            return pl.ds(pl.multiple_of((span * SPAN + r) * blocks, blocks), blocks)

        x = [x_ref[at(r), :] for r in range(SPAN)]
        for r in range(SPAN):
            out_ref[0, at(r), :] = tree([kernel[u] * x[r - u] for u in range(r + 1)])
        b = [b_ref[at(r), :] for r in range(SPAN)]
        for r in range(SPAN):
            out_ref[1, at(r), :] = tree([kernel[u] * b[r + u] for u in range(SPAN - r)])
        return carry

    copies = []
    for p in range(pieces):
        lax.fori_loop(p * part, (p + 1) * part, step, 0)
        rows = pl.ds(p * part * SPAN * blocks, part * SPAN * blocks)
        copies += start_all([
            pltpu.make_async_copy(out_ref.at[k, rows], ref.at[rows], sem.at[k, p]) for k, ref in enumerate((y_hbm, z_hbm))
        ])
    wait_all(copies)


def lane_is_first(shape, modes):
    return lax.broadcasted_iota(jnp.int32, shape, 1) % (2 * modes) < modes


def scan_body(s_ref, rate_ref, slopes_ref, out_ref, heads_ref, acc_ref, skip_ref, sem, *, modes, length):
    chunks, groups, rows = s_ref.shape[0], rate_ref.shape[0], s_ref.shape[2]
    first = lane_is_first((rows, LANES), modes)
    zero = jnp.zeros((rows, LANES), jnp.float32)
    copies = []
    for group in range(groups):
        alpha = jnp.exp(-float(length) * rate_ref[group])
        before, lead, total0, total1 = zero, zero, zero, zero
        heads = []
        for k in range(chunks):
            value = s_ref[k, group]
            later = pltpu.roll(value, LANES - modes, 1)
            heads.append(before)
            total0 += before * later
            total1 += (lead + before) * later
            lead = alpha * (lead + float(length) * before)
            before = alpha * before + value
        after = zero
        for k in reversed(range(chunks)):
            heads_ref[group, k] = jnp.where(first, heads[k], after)
            after = alpha * after + s_ref[k, group]
        copies += start_all([pltpu.make_async_copy(heads_ref.at[group], out_ref.at[:, group], sem.at[group])])
        acc_ref[group] = jnp.where(first, total0, pltpu.roll(total1, modes, 1))
    skip_ref[...] = tree([s_ref[k, groups, : skip_ref.shape[0]] for k in range(chunks)])
    wait_all(copies)


def slope_sum_body(r_ref, own_ref, acc_ref, rate_ref, done_ref, out_ref, pack_ref, sem, *, modes):
    chunks, groups, rows = r_ref.shape[0], rate_ref.shape[0], r_ref.shape[2]
    first = lane_is_first((rows, LANES), modes)
    span = 2 * modes
    fold = LANES // span
    row = lax.broadcasted_iota(jnp.int32, (rows, LANES), 0) % fold
    column = lax.broadcasted_iota(jnp.int32, (rows, LANES), 1) // span
    for group in range(groups):
        cross = tree([own_ref[group, k] * r_ref[k, groups + group] for k in range(chunks)])
        inner = tree([r_ref[k, 2 * groups + group] for k in range(chunks)])
        cross = jnp.where(first, 0.0, cross + pltpu.roll(cross, modes, 1))
        total = inner + jnp.exp(-rate_ref[group]) * (acc_ref[group] + cross)
        packed = total
        for shift in range(1, fold):
            moved = pltpu.roll(total, LANES - shift * span, 1)
            moved = jnp.where(row >= shift, pltpu.roll(moved, shift, 0), pltpu.roll(moved, rows - fold + shift, 0))
            packed = jnp.where((row - column + fold) % fold == shift, moved, packed)
        for block in range(fold):
            for r in range(rows // fold):
                pack_ref[group * fold + block, pl.ds(r, 1), :] = packed[r * fold + block : r * fold + block + 1]
    wait_all(start_all([pltpu.make_async_copy(pack_ref, out_ref.at[k], sem.at[k]) for k in range(out_ref.shape[0])]))


def final_body(g_ref, residue_ref, decay_ref, gres_ref, gdec_ref, spread_ref):
    modes = residue_ref.shape[0]
    owners, blocks, rows = g_ref.shape[0], g_ref.shape[1], g_ref.shape[2]
    span = 2 * modes
    fold = LANES // span
    total = tree([g_ref[:, block] for block in range(blocks)]).reshape(owners * rows, LANES)
    for k in range(fold):
        moved = total if k == 0 else pltpu.roll(total, LANES - k * span, 1)
        spread_ref[pl.ds(k, owners * rows, stride=fold), :] = moved
    sums = spread_ref[...].T
    plain, slope = sums[:modes], sums[modes:span]
    decay = decay_ref[...]
    root = jnp.sqrt(decay)
    gres_ref[...] = root * plain
    gdec_ref[...] = residue_ref[...] * root * (0.5 * plain - decay * slope)


def out_body(
    par_ref, r_ref, y_hbm, z_hbm, hs_hbm, bs_hbm, gate_hbm, key_hbm, value_hbm, cot_hbm,
    mixed_hbm, ggate_hbm, gkey_hbm, gvalue_hbm,
    hb_ref, run_ref, loc_ref, snap_ref, in_ref, out_ref, loc_sem, in_sem, out_sem,
):
    length, channels = gate_hbm.shape
    blocks = channels // LANES
    modes = par_ref.shape[0] // blocks // 2
    groups = hb_ref.shape[0] // LANES
    spans = length // SPAN
    pieces = loc_sem.shape[0]
    part = spans // pieces
    depth = part * SPAN
    fetch = []
    for p in range(pieces):
        mirror = pieces - 1 - p
        copies = []
        for kind, (place, local, snaps, shift, near) in enumerate((
            (p, y_hbm, hs_hbm, 0, (gate_hbm, cot_hbm)),
            (mirror, z_hbm, bs_hbm, 1, (value_hbm, key_hbm)),
        )):
            rows = pl.ds(place * depth * blocks, depth * blocks)
            copies.append(pltpu.make_async_copy(local.at[rows], loc_ref.at[kind, rows], loc_sem.at[p, 2 * kind]))
            source, target = pl.ds(place * part + shift, part), pl.ds(place * part, part)
            copies.append(
                pltpu.make_async_copy(snaps.at[source], snap_ref.at[kind, target], loc_sem.at[p, 2 * kind + 1])
            )
            rows = pl.ds(place * depth, depth)
            for k, ref in enumerate(near):
                slot = 2 * kind + k
                copies.append(pltpu.make_async_copy(ref.at[rows], in_ref.at[slot, rows], in_sem.at[p, slot]))
        fetch.append(start_all(copies))
    for group in range(groups):
        hb_ref[pl.ds(group * LANES, LANES), :] = r_ref[:, group].reshape(LANES, LANES).T
    FACTOR, FAR, WEIGHT, HEAD, TAIL = range(5)
    for m in range(modes):
        rows = pl.ds(m * blocks, blocks)
        rate = by_mode(par_ref, m, blocks)
        factor = jnp.exp(-rate)
        run_ref[FACTOR, rows, :] = factor
        run_ref[FAR, rows, :] = jnp.exp(-float(SPAN) * rate)
        run_ref[WEIGHT, rows, :] = by_mode(par_ref, modes + m, blocks) * jnp.sqrt(rate) * factor
        run_ref[HEAD, rows, :] = by_mode(hb_ref, m, blocks)
        run_ref[TAIL, rows, :] = by_mode(hb_ref, modes + m, blocks)

    def finish(kind, span, run):
        terms, factors = [], []
        for m in range(modes):
            rows = pl.ds(m * blocks, blocks)
            state = run_ref[run, rows, :]
            terms.append(run_ref[WEIGHT, rows, :] * (snap_ref[kind, span, rows, :] + state))
            run_ref[run, rows, :] = state * run_ref[FAR, rows, :]
            factors.append(run_ref[FACTOR, rows, :])
        for k in range(SPAN):
            r = k if kind == 0 else SPAN - 1 - k
            rows = pl.ds(pl.multiple_of((span * SPAN + r) * blocks, blocks), blocks)
            loc_ref[kind, rows, :] = loc_ref[kind, rows, :] + tree(terms)
            if k < SPAN - 1:
                terms = [t * f for t, f in zip(terms, factors)]
        rows = pl.ds(pl.multiple_of(span * SPAN, SPAN), SPAN)
        for block in range(blocks):
            lanes = pl.ds(block * LANES, LANES)
            total = jnp.concatenate(
                [
                    loc_ref[kind, pl.ds((span * SPAN + half * ROWS) * blocks + block, ROWS, stride=blocks), :]
                    for half in range(SPAN // ROWS)
                ],
                axis=0,
            )
            for slot in (2 * kind, 2 * kind + 1):
                value = in_ref[slot, rows, lanes].astype(jnp.float32) * total
                out_ref[slot, rows, lanes] = value.astype(jnp.bfloat16)

    def step(span, carry):
        finish(0, span, HEAD)
        finish(1, spans - 1 - span, TAIL)
        return carry

    stores = []
    for p in range(pieces):
        wait_all(fetch[p])
        lax.fori_loop(p * part, (p + 1) * part, step, 0)
        for slot, ref in enumerate((mixed_hbm, ggate_hbm, gkey_hbm, gvalue_hbm)):
            rows = pl.ds((p if slot < 2 else pieces - 1 - p) * depth, depth)
            stores += start_all([pltpu.make_async_copy(out_ref.at[slot, rows], ref.at[rows], out_sem.at[p, slot])])
    wait_all(stores)


def on_device(gate_in, key_in, value_in, cotangent, skip, residue, decay):
    f32, bf16 = jnp.float32, jnp.bfloat16
    owners = lax.axis_size("ctx")
    blocks = lax.axis_size("ch")
    length, channels = gate_in.shape
    filters, modes = residue.shape
    share = filters // owners
    groups = blocks * 2 * modes // LANES
    spans = length // SPAN
    pieces = 4
    place = lax.axis_index("ctx").astype(jnp.int32).reshape(1)
    whole = (length, channels)
    signal = (length * blocks, LANES)
    heads_at, tails_at = (spans, modes * blocks, LANES), (spans + 1, modes * blocks, LANES)
    size = length * channels
    sums = pltpu.VMEM((groups * LANES, LANES), f32)
    dense = pltpu.VMEM((4, *whole), bf16)
    tile = (share, LANES)

    (sent,) = call(
        spread_body,
        [((blocks, 2 * modes, LANES), f32, HBM)],
        4,
        (0, 10**5),
        [pltpu.VMEM((2 * modes, LANES), f32), DMA((2,)), DMA((blocks,))],
    )([HBM] * 2, decay.T, residue.T)
    params = lax.all_to_all(sent, "ch", 0, 0, tiled=True).reshape(blocks * 2 * modes, LANES)

    x, b, sk = call(
        product_body,
        [(signal, f32, VMEM)] * 2 + [((blocks, LANES), f32, VMEM)],
        16,
        (4 * size, 16 * size),
        [dense, DMA((pieces, 4))],
    )([HBM] * 4, gate_in, key_in, value_in, cotangent)

    states, head_states, tail_states, rates = call(
        state_body,
        [
            ((owners, groups + 1, *tile), f32, HBM),
            (heads_at, f32, HBM),
            (tails_at, f32, HBM),
            ((groups, *tile), f32, VMEM),
        ],
        16,
        (64 * size, 16 * size),
        [sums, sums, pltpu.VMEM((groups + 1, owners, *tile), f32), pltpu.VMEM(heads_at, f32), pltpu.VMEM(tails_at, f32)]
        + [DMA((groups + 2,)), DMA((2, pieces))],
    )([SMEM] + [VMEM] * 4, place, params, x, b, sk)
    states = lax.all_to_all(states, "ctx", 0, 0, tiled=True)

    (slopes,) = call(
        slope_body,
        [((owners, 3 * groups, *tile), f32, HBM)],
        16,
        (100 * size, 16 * size),
        [pltpu.VMEM(heads_at, f32), pltpu.VMEM(tails_at, f32), pltpu.VMEM((SPAN * blocks, LANES), f32)]
        + [pltpu.VMEM((7, modes * blocks, LANES), f32), sums, sums, pltpu.VMEM((2 * groups, owners, *tile), f32)]
        + [DMA((2 * groups,)), DMA((2, pieces))],
    )([VMEM] * 3 + [HBM] * 2, params, x, b, head_states, tail_states)

    bundle, heads, acc, grad_skip = call(
        functools.partial(scan_body, modes=modes, length=length),
        [
            ((owners, 3 * groups, *tile), f32, HBM),
            ((groups, owners, *tile), f32, VMEM),
            ((groups, *tile), f32, VMEM),
            ((blocks, LANES), f32, VMEM),
        ],
        8,
        (10**5, 10**6),
        [DMA((groups,))],
        {2: 0},
    )([VMEM, VMEM, HBM], states, rates, slopes)
    arrived = lax.all_to_all(bundle, "ctx", 0, 0, tiled=True)

    y, z = call(
        local_body,
        [(signal, f32, HBM)] * 2,
        16,
        (40 * size, 16 * size),
        [pltpu.VMEM((blocks, LANES), f32), pltpu.VMEM((2, *signal), f32), DMA, DMA((2, pieces))],
    )([VMEM] * 3 + [HBM], params, x, b, skip.reshape(blocks, LANES))

    packed = (owners, blocks, share * 2 * modes // LANES, LANES)
    (grads,) = call(
        functools.partial(slope_sum_body, modes=modes),
        [(packed, f32, HBM)],
        8,
        (10**5, 10**6),
        [pltpu.VMEM(packed[1:], f32), DMA((owners,))],
    )([VMEM] * 4 + [HBM], arrived, heads, acc, rates, y)
    grads = lax.all_to_all(grads.reshape(owners * blocks, *packed[2:]), ("ctx", "ch"), 0, 0, tiled=True)

    mixed, grad_gate, grad_key, grad_value = call(
        out_body,
        [(whole, bf16, HBM)] * 4,
        24,
        (64 * size, 32 * size),
        [sums, pltpu.VMEM((5, modes * blocks, LANES), f32), pltpu.VMEM((2, *signal), f32)]
        + [pltpu.VMEM((2, *heads_at), f32), dense, dense, DMA((pieces, 4)), DMA((pieces, 4)), DMA((pieces, 4))],
    )([VMEM] * 2 + [HBM] * 8, params, arrived, y, z, head_states, tail_states, gate_in, key_in, value_in, cotangent)

    grad_residue, grad_log_decay = call(
        final_body, [((modes, filters), f32, VMEM)] * 2, 8, (10**5, 10**6), [pltpu.VMEM((LANES, LANES), f32)]
    )([VMEM] * 3, grads.reshape(packed), residue.T, decay.T)
    return (mixed, grad_gate, grad_key, grad_value, grad_skip.reshape(channels), grad_residue.T, grad_log_decay.T)


def solution(mesh):
    rows = P("ctx", "ch")
    return jax.shard_map(
        on_device,
        mesh=mesh,
        in_specs=(rows, rows, rows, rows, P("ch"), P("ch", None), P("ch", None)),
        out_specs=(rows, rows, rows, rows, P("ch"), P("ch", None), P("ch", None)),
        check_vma=False,
    )
```

time: 71 us -> 66.4 us (0.935)
  Pallas kernels: 35.4 us -> 24.6 us
  waiting for transfers between devices: 5.16 us -> 15.2 us
  starting transfers between devices: 29.2 us -> 25.2 us
    pallas_call x9, Pallas kernels: 35.4 us -> 24.6 us  [call(): pl.pallas_call(body, out_shape=[pltpu.HBM(s, t) if w is HBM else jax.Shap...]
    all_to_all x1, waiting for transfers between devices: 0.68 us -> 5.67 us  [on_device(): arrived = lax.all_to_all(bundle, 'ctx', 0, 0, tiled=True)]
    all_to_all x1, waiting for transfers between devices: 0.01 us -> 4.91 us  [on_device(): lax.all_to_all(sent, 'ch', 0, 0, tiled=True)]
    all_to_all x1, starting transfers between devices: 9.33 us -> 4.58 us  [on_device(): lax.all_to_all(grads.reshape(owners * blocks, *packed[2:]), ('ctx', 'ch')...]
    all_to_all x1, starting transfers between devices: 6.78 us -> 7.56 us  [on_device(): states = lax.all_to_all(states, 'ctx', 0, 0, tiled=True)]
  transfers between devices with their start and end apart: 4 -> 4, of which waited for: 3 -> 4; matrix products, arithmetic and copies ran while one was open for 0% -> 0% of each run, Pallas kernels for 39% -> 25%
where the time goes in v4:
time: 66.4 us; the launch traced here: 65.8 us
  starting transfers between devices  25.2 us (38%)
  Pallas kernels  24.6 us (37%)
  waiting for transfers between devices  15.2 us (23%)
  between operations  0.72 us (1%)
    pallas_call x9, Pallas kernels, call(): pl.pallas_call(body, out_shape=[pltpu.HBM(s, t) if w is HBM else jax.Shap...  24.6 us
    all_to_all x1, starting transfers between devices, on_device(): states = lax.all_to_all(states, 'ctx', 0, 0, tiled=True)  7.56 us
    all_to_all x1, starting transfers between devices, on_device(): lax.all_to_all(sent, 'ch', 0, 0, tiled=True)  7.49 us
    all_to_all x1, waiting for transfers between devices, on_device(): arrived = lax.all_to_all(bundle, 'ctx', 0, 0, tiled=True)  5.67 us
    all_to_all x1, starting transfers between devices, on_device(): arrived = lax.all_to_all(bundle, 'ctx', 0, 0, tiled=True)  5.6 us
    all_to_all x1, waiting for transfers between devices, on_device(): lax.all_to_all(sent, 'ch', 0, 0, tiled=True)  4.91 us
    all_to_all x1, starting transfers between devices, on_device(): lax.all_to_all(grads.reshape(owners * blocks, *packed[2:]), ('ctx', 'ch')...  4.58 us
    all_to_all x1, waiting for transfers between devices, on_device(): lax.all_to_all(grads.reshape(owners * blocks, *packed[2:]), ('ctx', 'ch')...  4.53 us
  transfers between devices with their start and end apart: 4, of which 4 were waited for; matrix products, arithmetic and copies ran while one was open for 0% of the time, Pallas kernels for 25%

profile of v4, /device:TPU:1, one launch (start us, length us, event | category | flops | bytes accessed | tf_op | source)
XLA Modules:
  0.0 65.8 jit_solution(1857374821941593671)
XLA Ops:
  0.6 1.4 %shard_map.126 = f32[8,32,128]{2,1,0:T(8,128)} custom-call(f32[16,128]{1,0:T(8,128)} %bitcast.15, f32[16,128]{1,0:T(8,128)} %bitcast.17), custom_call_target="tpu_custom_call" | custom-call | bytes 100000 | tf_op jit(solution)/shard_map/pallas_call | solution.py:21
  2.1 7.5 %all-to-all-start = ((f32[8,32,128]{2,1,0:T(8,128)}), f32[8,32,128]{2,1,0:T(8,128)S(1)}, u32[]{:S(2)}, u32[]{:S(2)}) async-start(f32[8,32,128]{2,1,0:T(8,128)} %shard_map.126), calls=%async_computation | async-start | bytes 262144 | tf_op jit(solution)/shard_map/all_to_all | solution.py:486
  9.6 1.8 %shard_map.127 = (f32[2048,128]{1,0:T(8,128)S(1)}, f32[2048,128]{1,0:T(8,128)S(1)}, f32[8,128]{1,0:T(8,128)S(1)}) custom-call(bf16[256,1024]{1,0:T(8,128)(2,1)} %gate_hbm.3, bf16[256,1024]{1,0:T(8,128)(2,1)} %key_hbm.3, bf16[256,1024]{1,0:T(8,128)(2,1)} %value_hbm.3, bf16[256,1024]{1,0:T(8,128)(2,1)} %cot_hbm.3), custom_call_target="tpu_custom_call" | custom-call | flops 1048576 | bytes 4194304 | tf_op jit(solution)/shard_map/pallas_call | solution.py:21
  11.4 4.9 %all-to-all-done = f32[8,32,128]{2,1,0:T(8,128)S(1)} async-done(((f32[8,32,128]{2,1,0:T(8,128)}), f32[8,32,128]{2,1,0:T(8,128)S(1)}, u32[]{:S(2)}, u32[]{:S(2)}) %all-to-all-start) | async-done | bytes 131104 | tf_op jit(solution)/shard_map/all_to_all | solution.py:486
  16.3 3.4 %shard_map.128 = (f32[16,3,8,128]{3,2,1,0:T(8,128)}, f32[16,128,128]{2,1,0:T(8,128)}, f32[17,128,128]{2,1,0:T(8,128)}, f32[2,8,128]{2,1,0:T(8,128)S(1)}) custom-call(s32[1]{0:T(128)} %bitcast.3.index_ref, f32[256,128]{1,0:T(8,128)S(1)} %bitcast.10, f32[2048,128]{1,0:T(8,128)S(1)} %get-tuple-element.26.x_ref, f32[2048,128]{1,0:T(8,128)S(1)} %get-tuple-element.27.b_ref, ...), custom_call_target="tpu_custom_call" | custom-call | flops 16777216 | bytes 4194304 | tf_op jit(solution)/shard_map/pallas_call | solution.py:21
  19.7 7.6 %all-to-all-start.1 = ((f32[16,3,8,128]{3,2,1,0:T(8,128)}), f32[16,3,8,128]{3,2,1,0:T(8,128)S(1)}, u32[]{:S(2)}, u32[]{:S(2)}) async-start(f32[16,3,8,128]{3,2,1,0:T(8,128)} %get-tuple-element.29), calls=%async_computation.1 | async-start | bytes 393216 | tf_op jit(solution)/shard_map/all_to_all | solution.py:509
  27.3 6.5 %shard_map.129.slopes_ref = f32[16,6,8,128]{3,2,1,0:T(8,128)} custom-call(f32[256,128]{1,0:T(8,128)S(1)} %bitcast.11, f32[2048,128]{1,0:T(8,128)S(1)} %get-tuple-element.26.x_ref, f32[2048,128]{1,0:T(8,128)S(1)} %get-tuple-element.27.b_ref, f32[16,128,128]{2,1,0:T(8,128)} %get-tuple-element.31.hs_hbm, f32[17,128,128]{2,1,0:T(8,128)} %get-tuple-element.32.bs_hbm), custom_call_target="tpu_custom_call" | custom-call | flops 26214400 | bytes 4194304 | tf_op jit(solution)/shard_map/pallas_call | solution.py:21
  33.8 0.1 all-to-all-done.1.s_ref
  34.0 1.3 %shard_map.130 = (f32[16,6,8,128]{3,2,1,0:T(8,128)}, f32[2,16,8,128]{3,2,1,0:T(8,128)S(1)}, f32[2,8,128]{2,1,0:T(8,128)S(1)}, f32[8,128]{1,0:T(8,128)}) custom-call(f32[16,3,8,128]{3,2,1,0:T(8,128)S(1)} %all-to-all-done.1.s_ref, f32[2,8,128]{2,1,0:T(8,128)S(1)} %get-tuple-element.30.rate_ref, ...), custom_call_target="tpu_custom_call", output_to_operand_aliasing={{0}: (2, {})} | custom-call | flops 100000 | bytes 1000000 | tf_op jit(solution)/shard_map/pallas_call | solution.py:21
  35.3 5.6 %all-to-all-start.2 = ((f32[16,6,8,128]{3,2,1,0:T(8,128)}), f32[16,6,8,128]{3,2,1,0:T(8,128)S(1)}, u32[]{:S(2)}, u32[]{:S(2)}) async-start(f32[16,6,8,128]{3,2,1,0:T(8,128)} %get-tuple-element.33), calls=%async_computation.2 | async-start | bytes 786432 | tf_op jit(solution)/shard_map/all_to_all | solution.py:534
  40.9 2.7 %shard_map.131 = (f32[2048,128]{1,0:T(8,128)}, f32[2048,128]{1,0:T(8,128)}) custom-call(f32[256,128]{1,0:T(8,128)S(1)} %bitcast.12, f32[2048,128]{1,0:T(8,128)S(1)} %get-tuple-element.26.x_ref, f32[2048,128]{1,0:T(8,128)S(1)} %get-tuple-element.27.b_ref, f32[8,128]{1,0:T(8,128)} %bitcast.20), custom_call_target="tpu_custom_call" | custom-call | flops 10485760 | bytes 4194304 | tf_op jit(solution)/shard_map/pallas_call | solution.py:21
  43.6 5.7 %all-to-all-done.2.r_ref = f32[16,6,8,128]{3,2,1,0:T(8,128)S(1)} async-done(((f32[16,6,8,128]{3,2,1,0:T(8,128)}), f32[16,6,8,128]{3,2,1,0:T(8,128)S(1)}, u32[]{:S(2)}, u32[]{:S(2)}) %all-to-all-start.2) | async-done | bytes 393248 | tf_op jit(solution)/shard_map/all_to_all | solution.py:534
  49.3 1.0 %shard_map.133 = f32[16,8,2,128]{3,2,1,0:T(2,128)} custom-call(f32[16,6,8,128]{3,2,1,0:T(8,128)S(1)} %all-to-all-done.2.r_ref, f32[2,16,8,128]{3,2,1,0:T(8,128)S(1)} %get-tuple-element.41.own_ref, f32[2,8,128]{2,1,0:T(8,128)S(1)} %get-tuple-element.42.acc_ref, f32[2,8,128]{2,1,0:T(8,128)S(1)} %get-tuple-element.30.rate_ref, ...), custom_call_target="tpu_custom_call" | custom-call | flops 100000 | bytes 1000000 | tf_op jit(solution)/shard_map/pallas_call | solution.py:21
  50.3 4.6 %all-to-all-start.3 = ((f32[128,2,128]{2,1,0:T(2,128)}), f32[128,2,128]{2,1,0:T(2,128)S(1)}, u32[]{:S(2)}, u32[]{:S(2)}) async-start(f32[128,2,128]{2,1,0:T(2,128)} %bitcast.19), calls=%async_computation.3 | async-start | bytes 262144 | tf_op jit(solution)/shard_map/all_to_all | solution.py:552
  54.9 0.0 copy-start
  54.9 0.0 copy-start.1
  54.9 5.6 %shard_map.132 = (bf16[256,1024]{1,0:T(8,128)(2,1)}, bf16[256,1024]{1,0:T(8,128)(2,1)}, bf16[256,1024]{1,0:T(8,128)(2,1)}, bf16[256,1024]{1,0:T(8,128)(2,1)}) custom-call(f32[256,128]{1,0:T(8,128)S(1)} %bitcast.13, f32[16,6,8,128]{3,2,1,0:T(8,128)S(1)} %all-to-all-done.2.r_ref, f32[2048,128]{1,0:T(8,128)} %get-tuple-element.34.y_hbm.done_ref, ...), custom_call_target="tpu_custom_call" | custom-call | flops 16777216 | bytes 8388608 | tf_op jit(solution)/shard_map/pallas_call | solution.py:21
  60.5 4.5 %all-to-all-done.3 = f32[128,2,128]{2,1,0:T(2,128)S(1)} async-done(((f32[128,2,128]{2,1,0:T(2,128)}), f32[128,2,128]{2,1,0:T(2,128)S(1)}, u32[]{:S(2)}, u32[]{:S(2)}) %all-to-all-start.3) | async-done | bytes 131104 | tf_op jit(solution)/shard_map/all_to_all | solution.py:552
  65.0 0.0 copy-done
  65.0 0.0 copy-done.1
  65.0 0.8 %shard_map.134 = (f32[16,128]{1,0:T(8,128)}, f32[16,128]{1,0:T(8,128)}) custom-call(f32[16,8,2,128]{3,2,1,0:T(2,128)S(1)} %bitcast.14, f32[16,128]{1,0:T(8,128)S(1)} %bitcast.18, f32[16,128]{1,0:T(8,128)S(1)} %bitcast.16), custom_call_target="tpu_custom_call" | custom-call | flops 100000 | bytes 1000000 | tf_op jit(solution)/shard_map/pallas_call | solution.py:21
Async XLA Ops:
  2.1 14.3 %all-to-all-start = ((f32[8,32,128]{2,1,0:T(8,128)}), f32[8,32,128]{2,1,0:T(8,128)S(1)}, u32[]{:S(2)}, u32[]{:S(2)}) async-start(f32[8,32,128]{2,1,0:T(8,128)} %shard_map.126), calls=%async_computation | async-start | bytes 262144 | tf_op jit(solution)/shard_map/all_to_all | solution.py:486
  19.7 14.2 %all-to-all-start.1 = ((f32[16,3,8,128]{3,2,1,0:T(8,128)}), f32[16,3,8,128]{3,2,1,0:T(8,128)S(1)}, u32[]{:S(2)}, u32[]{:S(2)}) async-start(f32[16,3,8,128]{3,2,1,0:T(8,128)} %get-tuple-element.29), calls=%async_computation.1 | async-start | bytes 393216 | tf_op jit(solution)/shard_map/all_to_all | solution.py:509
  35.3 14.0 %all-to-all-start.2 = ((f32[16,6,8,128]{3,2,1,0:T(8,128)}), f32[16,6,8,128]{3,2,1,0:T(8,128)S(1)}, u32[]{:S(2)}, u32[]{:S(2)}) async-start(f32[16,6,8,128]{3,2,1,0:T(8,128)} %get-tuple-element.33), calls=%async_computation.2 | async-start | bytes 786432 | tf_op jit(solution)/shard_map/all_to_all | solution.py:534
  50.3 14.7 %all-to-all-start.3 = ((f32[128,2,128]{2,1,0:T(2,128)}), f32[128,2,128]{2,1,0:T(2,128)S(1)}, u32[]{:S(2)}, u32[]{:S(2)}) async-start(f32[128,2,128]{2,1,0:T(2,128)} %bitcast.19), calls=%async_computation.3 | async-start | bytes 262144 | tf_op jit(solution)/shard_map/all_to_all | solution.py:552
  54.9 10.1 %copy-start = (f32[128,16]{0,1:T(8,128)S(1)}, f32[128,16]{0,1:T(8,128)}, u32[]{:S(2)}) copy-start(f32[128,16]{0,1:T(8,128)} %param.13) | copy-start | bytes 24580
  54.9 10.1 %copy-start.1 = (f32[128,16]{0,1:T(8,128)S(1)}, f32[128,16]{0,1:T(8,128)}, u32[]{:S(2)}) copy-start(f32[128,16]{0,1:T(8,128)} %param.12) | copy-start | bytes 24580

commit v5 on v4

--- a/solution.py
+++ b/solution.py
@@ -67,9 +67,13 @@
     return ref[pl.ds(row, blocks, stride=ref.shape[0] // blocks), :]
 
 
+def position(span, offset, blocks):
+    return pl.ds(pl.multiple_of((span * SPAN + offset) * blocks, blocks), blocks)
+
+
 def product_body(
     gate_hbm, key_hbm, value_hbm, cot_hbm,
-    x_ref, b_ref, sk_ref,
+    x_ref, b_ref, sk_ref, lag_ref,
     in_ref, sem,
 ):
     length, channels = gate_hbm.shape
@@ -83,6 +87,7 @@
         ])
         for p in range(pieces)
     ]
+    lag_ref[...] = jnp.zeros(lag_ref.shape, jnp.float32)
 
     def step(place, sums):
         rows = pl.ds(pl.multiple_of(place * SPAN, SPAN), SPAN)
@@ -99,20 +104,29 @@
             after.append(sums[block] + tree([both[k * ROWS : (k + 1) * ROWS] for k in range(SPAN // ROWS)]))
         return tuple(after)
 
+    def lags(span, carry):
+        x = [x_ref[position(span, r, blocks), :] for r in range(SPAN)]
+        b = [b_ref[position(span, r, blocks), :] for r in range(SPAN)]
+        for u in range(SPAN):
+            rows = pl.ds(u * blocks, blocks)
+            lag_ref[rows, :] = lag_ref[rows, :] + tree([b[r + u] * x[r] for r in range(SPAN - u)])
+        return carry
+
     sums = tuple(jnp.zeros((ROWS, LANES), jnp.float32) for _ in range(blocks))
     for p in range(pieces):
         wait_all(fetch[p])
         sums = lax.fori_loop(p * depth // SPAN, (p + 1) * depth // SPAN, step, sums)
+        lax.fori_loop(p * depth // SPAN, (p + 1) * depth // SPAN, lags, 0)
     for block in range(blocks):
         sk_ref[pl.ds(block, 1), :] = jnp.sum(sums[block], axis=0, keepdims=True)
 
 
 def state_body(
-    index_ref, par_ref, x_ref, b_ref, sk_ref,
-    out_ref, hs_hbm, bs_hbm, rate_ref,
-    sums_ref, rates_ref, turn_ref, hs_ref, bs_ref, sem, snap_sem,
+    par_ref, x_ref, b_ref, sk_ref,
+    out_ref, hs_hbm, bs_hbm,
+    sums_ref, turn_ref, hs_ref, bs_ref, sem, snap_sem,
 ):
-    owners, share = out_ref.shape[0], out_ref.shape[2]
+    owners = out_ref.shape[0]
     groups = sums_ref.shape[0] // LANES
     blocks = sk_ref.shape[0]
     modes = par_ref.shape[0] // blocks // 2
@@ -122,12 +136,6 @@
     for owner in range(owners):
         turn_ref[groups, owner, :blocks] = sk_ref[...]
     copies = start_all([pltpu.make_async_copy(turn_ref.at[groups], out_ref.at[:, groups], sem.at[groups])])
-    for group in range(groups):
-        for block in range(group * blocks // groups, (group + 1) * blocks // groups):
-            decay = par_ref[pl.ds(block * 2 * modes, modes), :]
-            rates_ref[pl.ds(block * 2 * modes, 2 * modes), :] = jnp.concatenate([decay, decay], axis=0)
-        rates_ref[pl.ds(group * LANES, LANES), :] = rates_ref[pl.ds(group * LANES, LANES), :].T
-        rate_ref[group] = rates_ref[pl.ds(pl.multiple_of(group * LANES + index_ref[0] * share, share), share), :]
     factor = [jnp.exp(-by_mode(par_ref, m, blocks)) for m in range(modes)]
 
     def step(span, carry):
@@ -164,27 +172,21 @@
 
 
 def slope_body(
-    par_ref, x_ref, b_ref, hs_hbm, bs_hbm,
-    out_ref,
-    hs_ref, bs_ref, lag_ref, run_ref, suma_ref, sumb_ref, turn_ref, sem, snap_sem,
+    index_ref, par_ref, x_ref, b_ref, lag_ref, hs_hbm, bs_hbm,
+    out_ref, rate_ref,
+    hs_ref, bs_ref, up_ref, down_ref, run_ref, sums_ref, turn_ref, rates_ref, sem, snap_sem,
 ):
     owners = out_ref.shape[0]
-    groups = suma_ref.shape[0] // LANES
+    kinds = sums_ref.shape[0]
+    groups = sums_ref.shape[1] // LANES
     spans = hs_ref.shape[0]
-    blocks = x_ref.shape[0] // (spans * SPAN)
+    blocks = lag_ref.shape[0] // SPAN
     modes = par_ref.shape[0] // blocks // 2
-    pieces = snap_sem.shape[1]
-    part = spans // pieces
-    fetch = []
-    for p in range(pieces):
-        here = pl.ds(p * part, part)
-        there = pl.ds(p * part + (1 if p else 0), part + (0 if p else 1))
-        fetch.append(
-            start_all([
-                pltpu.make_async_copy(hs_hbm.at[here], hs_ref.at[here], snap_sem.at[0, p]),
-                pltpu.make_async_copy(bs_hbm.at[there], bs_ref.at[there], snap_sem.at[1, p]),
-            ])
-        )
+    fetch = start_all([
+        pltpu.make_async_copy(hs_hbm, hs_ref, snap_sem.at[0]),
+        pltpu.make_async_copy(bs_hbm, bs_ref, snap_sem.at[1]),
+    ])
+    share = rate_ref.shape[1]
     zero = jnp.zeros((blocks, LANES), jnp.float32)
     SLOPE, SUM0, SUM1, DOWN, POWER, FACTOR, FAR = range(7)
     for m in range(modes):
@@ -195,32 +197,47 @@
         run_ref[POWER, rows, :] = zero + 1.0
         run_ref[FACTOR, rows, :] = jnp.exp(-rate)
         run_ref[FAR, rows, :] = jnp.exp(-float(SPAN) * rate)
-    for u in range(SPAN):
-        lag_ref[pl.ds(u * blocks, blocks), :] = zero
-
-    def step(span, carry):
-        def at(ref, r):
-            return ref[pl.ds(pl.multiple_of((span * SPAN + r) * blocks, blocks), blocks), :]
-
-        x = [at(x_ref, r) for r in range(SPAN)]
-        b = [at(b_ref, r) for r in range(SPAN)]
-        for u in range(SPAN):
-            rows = pl.ds(u * blocks, blocks)
-            total = lag_ref[rows, :]
-            for r in range(SPAN - u):
-                total = total + b[r + u] * x[r]
-            lag_ref[rows, :] = total
-        late = [x[r] * (SPAN - 1.0 - r) for r in range(SPAN - 1)]
-        early = [b[r] * float(r) for r in range(SPAN - 1, 0, -1)]
+
+    def send(kind, first, second):
+        for m in range(modes):
+            sums_ref[kind, pl.ds(m, blocks, stride=2 * modes), :] = first(m)
+            sums_ref[kind, pl.ds(modes + m, blocks, stride=2 * modes), :] = second(m)
+        sent = []
+        for group in range(groups):
+            slot = kind * groups + group
+            turned = sums_ref[kind, pl.ds(group * LANES, LANES), :].T
+            turn_ref[slot] = turned.reshape(owners, LANES // owners, LANES)
+            sent += start_all([pltpu.make_async_copy(turn_ref.at[slot], out_ref.at[:, groups + slot], sem.at[slot])])
+        return sent
+
+    def at(m):
+        return pl.ds(m * blocks, blocks)
+
+    for group in range(groups):
+        for block in range(group * blocks // groups, (group + 1) * blocks // groups):
+            decay = par_ref[pl.ds(block * 2 * modes, modes), :]
+            rates_ref[pl.ds(block * 2 * modes, 2 * modes), :] = jnp.concatenate([decay, decay], axis=0)
+        rates_ref[pl.ds(group * LANES, LANES), :] = rates_ref[pl.ds(group * LANES, LANES), :].T
+        rate_ref[group] = rates_ref[pl.ds(pl.multiple_of(group * LANES + index_ref[0] * share, share), share), :]
+
+    def near(span, carry):
+        late = [x_ref[position(span, r, blocks), :] * (SPAN - 1.0 - r) for r in range(SPAN - 1)]
+        early = [b_ref[position(span, r, blocks), :] * float(r) for r in range(SPAN - 1, 0, -1)]
+        factors = [run_ref[FACTOR, at(m), :] for m in range(modes)]
+        for ref, terms in ((up_ref, late), (down_ref, early)):
+            sums = [terms[0]] * modes
+            for term in terms[1:]:
+                sums = [f * s + term for f, s in zip(factors, sums)]
+            for m in range(modes):
+                ref[span, at(m), :] = factors[m] * sums[m]
+        return carry
+
+    def across(span, carry):
         begin = (span * SPAN).astype(jnp.float32)
         for m in range(modes):
-            rows = pl.ds(m * blocks, blocks)
-            factor, far = run_ref[FACTOR, rows, :], run_ref[FAR, rows, :]
-            up, down = late[0], early[0]
-            for k in range(1, SPAN - 1):
-                up = factor * up + late[k]
-                down = factor * down + early[k]
-            up, down = factor * up, factor * down
+            rows = at(m)
+            far = run_ref[FAR, rows, :]
+            up, down = up_ref[span, rows, :], down_ref[span, rows, :]
             head = hs_ref[span, rows, :]
             own = bs_ref[span, rows, :] - far * bs_ref[span + 1, rows, :]
             slope, power = run_ref[SLOPE, rows, :], run_ref[POWER, rows, :]
@@ -231,28 +248,23 @@
             run_ref[SLOPE, rows, :] = far * (slope + float(SPAN) * head) + up
         return carry
 
-    for p in range(pieces):
-        wait_all(fetch[p])
-        lax.fori_loop(p * part, (p + 1) * part, step, 0)
+    lax.fori_loop(0, spans, near, 0)
+    wait_all(fetch)
+    lax.fori_loop(0, spans, across, 0)
+    copies = send(0, lambda m: run_ref[DOWN, at(m), :], lambda m: run_ref[SLOPE, at(m), :])
     lags = [lag_ref[pl.ds(u * blocks, blocks), :] for u in range(SPAN)]
-    for m in range(modes):
-        rows = pl.ds(m * blocks, blocks)
-        factor = run_ref[FACTOR, rows, :]
-        plain, slope = lags[SPAN - 1], lags[SPAN - 1] * (SPAN - 1.0)
-        for u in range(SPAN - 2, -1, -1):
-            plain = factor * plain + lags[u]
-            slope = factor * slope + lags[u] * float(u)
-        low, high = pl.ds(m, blocks, stride=2 * modes), pl.ds(modes + m, blocks, stride=2 * modes)
-        suma_ref[low, :] = run_ref[DOWN, rows, :]
-        suma_ref[high, :] = run_ref[SLOPE, rows, :]
-        sumb_ref[low, :] = factor * run_ref[SUM0, rows, :] + plain
-        sumb_ref[high, :] = factor * run_ref[SUM1, rows, :] + slope
-    copies = []
-    for kind, ref in enumerate((suma_ref, sumb_ref)):
-        for group in range(groups):
-            slot = kind * groups + group
-            turn_ref[slot] = turned(ref, group, owners)
-            copies += start_all([pltpu.make_async_copy(turn_ref.at[slot], out_ref.at[:, groups + slot], sem.at[slot])])
+    factors = [run_ref[FACTOR, at(m), :] for m in range(modes)]
+    plain = [lags[SPAN - 1]] * modes
+    slope = [lags[SPAN - 1] * (SPAN - 1.0)] * modes
+    for u in range(SPAN - 2, -1, -1):
+        sloped = lags[u] * float(u)
+        plain = [f * p + lags[u] for f, p in zip(factors, plain)]
+        slope = [f * p + sloped for f, p in zip(factors, slope)]
+    copies += send(
+        1,
+        lambda m: factors[m] * run_ref[SUM0, at(m), :] + plain[m],
+        lambda m: factors[m] * run_ref[SUM1, at(m), :] + slope[m],
+    )
     wait_all(copies)
 
 
@@ -485,38 +497,33 @@
     )([HBM] * 2, decay.T, residue.T)
     params = lax.all_to_all(sent, "ch", 0, 0, tiled=True).reshape(blocks * 2 * modes, LANES)
 
-    x, b, sk = call(
+    x, b, sk, lag = call(
         product_body,
-        [(signal, f32, VMEM)] * 2 + [((blocks, LANES), f32, VMEM)],
+        [(signal, f32, VMEM)] * 2 + [((blocks, LANES), f32, VMEM), ((SPAN * blocks, LANES), f32, VMEM)],
         16,
-        (4 * size, 16 * size),
+        (8 * size, 16 * size),
         [dense, DMA((pieces, 4))],
     )([HBM] * 4, gate_in, key_in, value_in, cotangent)
 
-    states, head_states, tail_states, rates = call(
+    states, head_states, tail_states = call(
         state_body,
-        [
-            ((owners, groups + 1, *tile), f32, HBM),
-            (heads_at, f32, HBM),
-            (tails_at, f32, HBM),
-            ((groups, *tile), f32, VMEM),
-        ],
+        [((owners, groups + 1, *tile), f32, HBM), (heads_at, f32, HBM), (tails_at, f32, HBM)],
         16,
         (64 * size, 16 * size),
-        [sums, sums, pltpu.VMEM((groups + 1, owners, *tile), f32), pltpu.VMEM(heads_at, f32), pltpu.VMEM(tails_at, f32)]
+        [sums, pltpu.VMEM((groups + 1, owners, *tile), f32), pltpu.VMEM(heads_at, f32), pltpu.VMEM(tails_at, f32)]
         + [DMA((groups + 2,)), DMA((2, pieces))],
-    )([SMEM] + [VMEM] * 4, place, params, x, b, sk)
+    )([VMEM] * 4, params, x, b, sk)
     states = lax.all_to_all(states, "ctx", 0, 0, tiled=True)
 
-    (slopes,) = call(
+    slopes, rates = call(
         slope_body,
-        [((owners, 3 * groups, *tile), f32, HBM)],
+        [((owners, 3 * groups, *tile), f32, HBM), ((groups, *tile), f32, VMEM)],
         16,
         (100 * size, 16 * size),
-        [pltpu.VMEM(heads_at, f32), pltpu.VMEM(tails_at, f32), pltpu.VMEM((SPAN * blocks, LANES), f32)]
-        + [pltpu.VMEM((7, modes * blocks, LANES), f32), sums, sums, pltpu.VMEM((2 * groups, owners, *tile), f32)]
-        + [DMA((2 * groups,)), DMA((2, pieces))],
-    )([VMEM] * 3 + [HBM] * 2, params, x, b, head_states, tail_states)
+        [pltpu.VMEM(heads_at, f32), pltpu.VMEM(tails_at, f32), pltpu.VMEM(heads_at, f32), pltpu.VMEM(heads_at, f32)]
+        + [pltpu.VMEM((7, modes * blocks, LANES), f32), pltpu.VMEM((2, groups * LANES, LANES), f32)]
+        + [pltpu.VMEM((2 * groups, owners, *tile), f32), sums, DMA((2 * groups,)), DMA((2,))],
+    )([SMEM] + [VMEM] * 4 + [HBM] * 2, place, params, x, b, lag, head_states, tail_states)
 
     bundle, heads, acc, grad_skip = call(
         functools.partial(scan_body, modes=modes, length=length),

time: 66.4 us -> 64.9 us (0.977)
  waiting for transfers between devices: 15.2 us -> 16.7 us
  Pallas kernels: 24.6 us -> 23.2 us
  starting transfers between devices: 25.2 us -> 23.8 us
    all_to_all x1, waiting for transfers between devices: 0.14 us -> 2.03 us  [on_device(): states = lax.all_to_all(states, 'ctx', 0, 0, tiled=True)]
    all_to_all x1, starting transfers between devices: 5.6 us -> 4.15 us  [on_device(): arrived = lax.all_to_all(bundle, 'ctx', 0, 0, tiled=True)]
    pallas_call x9, Pallas kernels: 24.6 us -> 23.2 us  [call(): pl.pallas_call(body, out_shape=[pltpu.HBM(s, t) if w is HBM else jax.Shap...]
  transfers between devices with their start and end apart: 4 -> 4, of which waited for: 4 -> 4; matrix products, arithmetic and copies ran while one was open for 0% -> 0% of each run, Pallas kernels for 25% -> 24%
where the time goes in v5:
time: 64.9 us; the launch traced here: 64.4 us
  starting transfers between devices  23.8 us (37%)
  Pallas kernels  23.2 us (36%)
  waiting for transfers between devices  16.7 us (26%)
  between operations  0.72 us (1%)
    pallas_call x9, Pallas kernels, call(): pl.pallas_call(body, out_shape=[pltpu.HBM(s, t) if w is HBM else jax.Shap...  23.2 us
    all_to_all x1, starting transfers between devices, on_device(): states = lax.all_to_all(states, 'ctx', 0, 0, tiled=True)  7.56 us
    all_to_all x1, starting transfers between devices, on_device(): lax.all_to_all(sent, 'ch', 0, 0, tiled=True)  7.49 us
    all_to_all x1, waiting for transfers between devices, on_device(): arrived = lax.all_to_all(bundle, 'ctx', 0, 0, tiled=True)  5.74 us
    all_to_all x1, starting transfers between devices, on_device(): lax.all_to_all(grads.reshape(owners * blocks, *packed[2:]), ('ctx', 'ch')...  4.58 us
    all_to_all x1, waiting for transfers between devices, on_device(): lax.all_to_all(grads.reshape(owners * blocks, *packed[2:]), ('ctx', 'ch')...  4.53 us
    all_to_all x1, waiting for transfers between devices, on_device(): lax.all_to_all(sent, 'ch', 0, 0, tiled=True)  4.37 us
    all_to_all x1, starting transfers between devices, on_device(): arrived = lax.all_to_all(bundle, 'ctx', 0, 0, tiled=True)  4.15 us
  transfers between devices with their start and end apart: 4, of which 4 were waited for; matrix products, arithmetic and copies ran while one was open for 0% of the time, Pallas kernels for 24%

profile of v5, /device:TPU:1, one launch (start us, length us, event | category | flops | bytes accessed | tf_op | source)
XLA Modules:
  0.0 64.4 jit_solution(16618317593904597594)
XLA Ops:
  0.6 1.4 %shard_map.126 = f32[8,32,128]{2,1,0:T(8,128)} custom-call(f32[16,128]{1,0:T(8,128)} %bitcast.15, f32[16,128]{1,0:T(8,128)} %bitcast.17), custom_call_target="tpu_custom_call" | custom-call | bytes 100000 | tf_op jit(solution)/shard_map/pallas_call | solution.py:21
  2.1 7.5 %all-to-all-start = ((f32[8,32,128]{2,1,0:T(8,128)}), f32[8,32,128]{2,1,0:T(8,128)S(1)}, u32[]{:S(2)}, u32[]{:S(2)}) async-start(f32[8,32,128]{2,1,0:T(8,128)} %shard_map.126), calls=%async_computation | async-start | bytes 262144 | tf_op jit(solution)/shard_map/all_to_all | solution.py:498
  9.6 2.4 %shard_map.127 = (f32[2048,128]{1,0:T(8,128)S(1)}, f32[2048,128]{1,0:T(8,128)S(1)}, f32[8,128]{1,0:T(8,128)S(1)}, f32[128,128]{1,0:T(8,128)S(1)}) custom-call(bf16[256,1024]{1,0:T(8,128)(2,1)} %gate_hbm.3, bf16[256,1024]{1,0:T(8,128)(2,1)} %key_hbm.3, bf16[256,1024]{1,0:T(8,128)(2,1)} %value_hbm.3, bf16[256,1024]{1,0:T(8,128)(2,1)} %cot_hbm.3), custom_call_target="tpu_custom_call" | custom-call | flops 2097152 | bytes 4194304 | tf_op jit(solution)/shard_map/pallas_call | solution.py:21
  12.0 4.4 %all-to-all-done = f32[8,32,128]{2,1,0:T(8,128)S(1)} async-done(((f32[8,32,128]{2,1,0:T(8,128)}), f32[8,32,128]{2,1,0:T(8,128)S(1)}, u32[]{:S(2)}, u32[]{:S(2)}) %all-to-all-start) | async-done | bytes 131104 | tf_op jit(solution)/shard_map/all_to_all | solution.py:498
  16.3 3.3 %shard_map.128 = (f32[16,3,8,128]{3,2,1,0:T(8,128)}, f32[16,128,128]{2,1,0:T(8,128)}, f32[17,128,128]{2,1,0:T(8,128)}) custom-call(f32[256,128]{1,0:T(8,128)S(1)} %bitcast.10, f32[2048,128]{1,0:T(8,128)S(1)} %get-tuple-element.28.x_ref, f32[2048,128]{1,0:T(8,128)S(1)} %get-tuple-element.29.b_ref, f32[8,128]{1,0:T(8,128)S(1)} %get-tuple-element.30.sk_ref), custom_call_target="tpu_custom_call" | custom-call | flops 16777216 | bytes 4194304 | tf_op jit(solution)/shard_map/pallas_call | solution.py:21
  19.7 7.6 %all-to-all-start.1 = ((f32[16,3,8,128]{3,2,1,0:T(8,128)}), f32[16,3,8,128]{3,2,1,0:T(8,128)S(1)}, u32[]{:S(2)}, u32[]{:S(2)}) async-start(f32[16,3,8,128]{3,2,1,0:T(8,128)} %get-tuple-element.31), calls=%async_computation.1 | async-start | bytes 393216 | tf_op jit(solution)/shard_map/all_to_all | solution.py:516
  27.2 4.6 %shard_map.129 = (f32[16,6,8,128]{3,2,1,0:T(8,128)}, f32[2,8,128]{2,1,0:T(8,128)S(1)}) custom-call(s32[1]{0:T(128)} %bitcast.3.index_ref, f32[256,128]{1,0:T(8,128)S(1)} %bitcast.11, f32[2048,128]{1,0:T(8,128)S(1)} %get-tuple-element.28.x_ref, f32[2048,128]{1,0:T(8,128)S(1)} %get-tuple-element.29.b_ref, f32[128,128]{1,0:T(8,128)S(1)} %get-tuple-element.32.lag_ref, ...), custom_call_target="tpu_custom_call" | custom-call | flops 26214400 | bytes 4194304 | tf_op jit(solution)/shard_map/pallas_call | solution.py:21
  31.9 2.0 %all-to-all-done.1.s_ref = f32[16,3,8,128]{3,2,1,0:T(8,128)S(1)} async-done(((f32[16,3,8,128]{3,2,1,0:T(8,128)}), f32[16,3,8,128]{3,2,1,0:T(8,128)S(1)}, u32[]{:S(2)}, u32[]{:S(2)}) %all-to-all-start.1) | async-done | bytes 196640 | tf_op jit(solution)/shard_map/all_to_all | solution.py:516
  33.9 1.3 %shard_map.130 = (f32[16,6,8,128]{3,2,1,0:T(8,128)}, f32[2,16,8,128]{3,2,1,0:T(8,128)S(1)}, f32[2,8,128]{2,1,0:T(8,128)S(1)}, f32[8,128]{1,0:T(8,128)}) custom-call(f32[16,3,8,128]{3,2,1,0:T(8,128)S(1)} %all-to-all-done.1.s_ref, f32[2,8,128]{2,1,0:T(8,128)S(1)} %get-tuple-element.35.rate_ref, ...), custom_call_target="tpu_custom_call", output_to_operand_aliasing={{0}: (2, {})} | custom-call | flops 100000 | bytes 1000000 | tf_op jit(solution)/shard_map/pallas_call | solution.py:21
  35.3 4.1 %all-to-all-start.2 = ((f32[16,6,8,128]{3,2,1,0:T(8,128)}), f32[16,6,8,128]{3,2,1,0:T(8,128)S(1)}, u32[]{:S(2)}, u32[]{:S(2)}) async-start(f32[16,6,8,128]{3,2,1,0:T(8,128)} %get-tuple-element.37), calls=%async_computation.2 | async-start | bytes 786432 | tf_op jit(solution)/shard_map/all_to_all | solution.py:541
  39.4 2.7 %shard_map.131 = (f32[2048,128]{1,0:T(8,128)}, f32[2048,128]{1,0:T(8,128)}) custom-call(f32[256,128]{1,0:T(8,128)S(1)} %bitcast.12, f32[2048,128]{1,0:T(8,128)S(1)} %get-tuple-element.28.x_ref, f32[2048,128]{1,0:T(8,128)S(1)} %get-tuple-element.29.b_ref, f32[8,128]{1,0:T(8,128)} %bitcast.20), custom_call_target="tpu_custom_call" | custom-call | flops 10485760 | bytes 4194304 | tf_op jit(solution)/shard_map/pallas_call | solution.py:21
  42.1 5.7 %all-to-all-done.2.r_ref = f32[16,6,8,128]{3,2,1,0:T(8,128)S(1)} async-done(((f32[16,6,8,128]{3,2,1,0:T(8,128)}), f32[16,6,8,128]{3,2,1,0:T(8,128)S(1)}, u32[]{:S(2)}, u32[]{:S(2)}) %all-to-all-start.2) | async-done | bytes 393248 | tf_op jit(solution)/shard_map/all_to_all | solution.py:541
  47.9 1.0 %shard_map.133 = f32[16,8,2,128]{3,2,1,0:T(2,128)} custom-call(f32[16,6,8,128]{3,2,1,0:T(8,128)S(1)} %all-to-all-done.2.r_ref, f32[2,16,8,128]{3,2,1,0:T(8,128)S(1)} %get-tuple-element.45.own_ref, f32[2,8,128]{2,1,0:T(8,128)S(1)} %get-tuple-element.46.acc_ref, f32[2,8,128]{2,1,0:T(8,128)S(1)} %get-tuple-element.35.rate_ref, ...), custom_call_target="tpu_custom_call" | custom-call | flops 100000 | bytes 1000000 | tf_op jit(solution)/shard_map/pallas_call | solution.py:21
  48.9 4.6 %all-to-all-start.3 = ((f32[128,2,128]{2,1,0:T(2,128)}), f32[128,2,128]{2,1,0:T(2,128)S(1)}, u32[]{:S(2)}, u32[]{:S(2)}) async-start(f32[128,2,128]{2,1,0:T(2,128)} %bitcast.19), calls=%async_computation.3 | async-start | bytes 262144 | tf_op jit(solution)/shard_map/all_to_all | solution.py:559
  53.4 0.0 copy-start
  53.5 0.0 copy-start.1
  53.5 5.6 %shard_map.132 = (bf16[256,1024]{1,0:T(8,128)(2,1)}, bf16[256,1024]{1,0:T(8,128)(2,1)}, bf16[256,1024]{1,0:T(8,128)(2,1)}, bf16[256,1024]{1,0:T(8,128)(2,1)}) custom-call(f32[256,128]{1,0:T(8,128)S(1)} %bitcast.13, f32[16,6,8,128]{3,2,1,0:T(8,128)S(1)} %all-to-all-done.2.r_ref, f32[2048,128]{1,0:T(8,128)} %get-tuple-element.38.y_hbm.done_ref, ...), custom_call_target="tpu_custom_call" | custom-call | flops 16777216 | bytes 8388608 | tf_op jit(solution)/shard_map/pallas_call | solution.py:21
  59.1 4.5 %all-to-all-done.3 = f32[128,2,128]{2,1,0:T(2,128)S(1)} async-done(((f32[128,2,128]{2,1,0:T(2,128)}), f32[128,2,128]{2,1,0:T(2,128)S(1)}, u32[]{:S(2)}, u32[]{:S(2)}) %all-to-all-start.3) | async-done | bytes 131104 | tf_op jit(solution)/shard_map/all_to_all | solution.py:559
  63.6 0.0 copy-done
  63.6 0.0 copy-done.1
  63.6 0.8 %shard_map.134 = (f32[16,128]{1,0:T(8,128)}, f32[16,128]{1,0:T(8,128)}) custom-call(f32[16,8,2,128]{3,2,1,0:T(2,128)S(1)} %bitcast.14, f32[16,128]{1,0:T(8,128)S(1)} %bitcast.18, f32[16,128]{1,0:T(8,128)S(1)} %bitcast.16), custom_call_target="tpu_custom_call" | custom-call | flops 100000 | bytes 1000000 | tf_op jit(solution)/shard_map/pallas_call | solution.py:21
Async XLA Ops:
  2.1 14.3 %all-to-all-start = ((f32[8,32,128]{2,1,0:T(8,128)}), f32[8,32,128]{2,1,0:T(8,128)S(1)}, u32[]{:S(2)}, u32[]{:S(2)}) async-start(f32[8,32,128]{2,1,0:T(8,128)} %shard_map.126), calls=%async_computation | async-start | bytes 262144 | tf_op jit(solution)/shard_map/all_to_all | solution.py:498
  19.7 14.2 %all-to-all-start.1 = ((f32[16,3,8,128]{3,2,1,0:T(8,128)}), f32[16,3,8,128]{3,2,1,0:T(8,128)S(1)}, u32[]{:S(2)}, u32[]{:S(2)}) async-start(f32[16,3,8,128]{3,2,1,0:T(8,128)} %get-tuple-element.31), calls=%async_computation.1 | async-start | bytes 393216 | tf_op jit(solution)/shard_map/all_to_all | solution.py:516
  35.3 12.6 %all-to-all-start.2 = ((f32[16,6,8,128]{3,2,1,0:T(8,128)}), f32[16,6,8,128]{3,2,1,0:T(8,128)S(1)}, u32[]{:S(2)}, u32[]{:S(2)}) async-start(f32[16,6,8,128]{3,2,1,0:T(8,128)} %get-tuple-element.37), calls=%async_computation.2 | async-start | bytes 786432 | tf_op jit(solution)/shard_map/all_to_all | solution.py:541
  48.9 14.7 %all-to-all-start.3 = ((f32[128,2,128]{2,1,0:T(2,128)}), f32[128,2,128]{2,1,0:T(2,128)S(1)}, u32[]{:S(2)}, u32[]{:S(2)}) async-start(f32[128,2,128]{2,1,0:T(2,128)} %bitcast.19), calls=%async_computation.3 | async-start | bytes 262144 | tf_op jit(solution)/shard_map/all_to_all | solution.py:559
  53.4 10.1 %copy-start = (f32[128,16]{0,1:T(8,128)S(1)}, f32[128,16]{0,1:T(8,128)}, u32[]{:S(2)}) copy-start(f32[128,16]{0,1:T(8,128)} %param.13) | copy-start | bytes 24580
  53.5 10.1 %copy-start.1 = (f32[128,16]{0,1:T(8,128)S(1)}, f32[128,16]{0,1:T(8,128)}, u32[]{:S(2)}) copy-start(f32[128,16]{0,1:T(8,128)} %param.12) | copy-start | bytes 24580

commit v6 on v5

--- a/solution.py
+++ b/solution.py
@@ -121,9 +121,15 @@
         sk_ref[pl.ds(block, 1), :] = jnp.sum(sums[block], axis=0, keepdims=True)
 
 
+def part_slices(core, turned_ref, keep_ref, send_ref):
+    for chip in range(keep_ref.shape[0]):
+        keep_ref[chip] = turned_ref[2 * chip + core]
+        send_ref[chip] = turned_ref[2 * chip + 1 - core]
+
+
 def state_body(
-    par_ref, x_ref, b_ref, sk_ref,
-    out_ref, hs_hbm, bs_hbm,
+    core_ref, par_ref, x_ref, b_ref, sk_ref,
+    out_ref, hs_hbm, bs_hbm, keep_ref, send_ref, edge_ref,
     sums_ref, turn_ref, hs_ref, bs_ref, sem, snap_sem,
 ):
     owners = out_ref.shape[0]
@@ -162,23 +168,25 @@
         ])
     for m in range(modes):
         bs_ref[0, pl.ds(m * blocks, blocks), :] = downs[m]
+        edge_ref[pl.ds(m * blocks, blocks), :] = jnp.where(core_ref[0] == 0, ups[m], downs[m])
         sums_ref[pl.ds(m, blocks, stride=2 * modes), :] = ups[m]
         sums_ref[pl.ds(modes + m, blocks, stride=2 * modes), :] = downs[m]
     copies += start_all([pltpu.make_async_copy(bs_ref.at[0], bs_hbm.at[0], sem.at[groups + 1])])
     for group in range(groups):
         turn_ref[group] = turned(sums_ref, group, owners)
         copies += start_all([pltpu.make_async_copy(turn_ref.at[group], out_ref.at[:, group], sem.at[group])])
+    for group in range(groups):
+        part_slices(core_ref[0], turn_ref.at[group], keep_ref.at[group], send_ref.at[group])
     wait_all(copies)
 
 
 def slope_body(
-    index_ref, par_ref, x_ref, b_ref, lag_ref, hs_hbm, bs_hbm,
-    out_ref, rate_ref,
-    hs_ref, bs_ref, up_ref, down_ref, run_ref, sums_ref, turn_ref, rates_ref, sem, snap_sem,
+    index_ref, core_ref, par_ref, x_ref, b_ref, lag_ref, hs_hbm, bs_hbm,
+    rate_ref, side_rate_ref, keep_a_ref, send_a_ref, keep_b_ref, send_b_ref,
+    hs_ref, bs_ref, up_ref, down_ref, run_ref, sums_ref, turn_ref, rates_ref, snap_sem,
 ):
-    owners = out_ref.shape[0]
-    kinds = sums_ref.shape[0]
-    groups = sums_ref.shape[1] // LANES
+    owners = turn_ref.shape[0]
+    groups = sums_ref.shape[0] // LANES
     spans = hs_ref.shape[0]
     blocks = lag_ref.shape[0] // SPAN
     modes = par_ref.shape[0] // blocks // 2
@@ -198,17 +206,13 @@
         run_ref[FACTOR, rows, :] = jnp.exp(-rate)
         run_ref[FAR, rows, :] = jnp.exp(-float(SPAN) * rate)
 
-    def send(kind, first, second):
+    def part(first, second, keep_ref, send_ref):
         for m in range(modes):
-            sums_ref[kind, pl.ds(m, blocks, stride=2 * modes), :] = first(m)
-            sums_ref[kind, pl.ds(modes + m, blocks, stride=2 * modes), :] = second(m)
-        sent = []
+            sums_ref[pl.ds(m, blocks, stride=2 * modes), :] = first(m)
+            sums_ref[pl.ds(modes + m, blocks, stride=2 * modes), :] = second(m)
         for group in range(groups):
-            slot = kind * groups + group
-            turned = sums_ref[kind, pl.ds(group * LANES, LANES), :].T
-            turn_ref[slot] = turned.reshape(owners, LANES // owners, LANES)
-            sent += start_all([pltpu.make_async_copy(turn_ref.at[slot], out_ref.at[:, groups + slot], sem.at[slot])])
-        return sent
+            turn_ref[...] = turned(sums_ref, group, owners)
+            part_slices(core_ref[0], turn_ref, keep_ref.at[group], send_ref.at[group])
 
     def at(m):
         return pl.ds(m * blocks, blocks)
@@ -219,6 +223,9 @@
             rates_ref[pl.ds(block * 2 * modes, 2 * modes), :] = jnp.concatenate([decay, decay], axis=0)
         rates_ref[pl.ds(group * LANES, LANES), :] = rates_ref[pl.ds(group * LANES, LANES), :].T
         rate_ref[group] = rates_ref[pl.ds(pl.multiple_of(group * LANES + index_ref[0] * share, share), share), :]
+        for chip in range(side_rate_ref.shape[1]):
+            start = group * LANES + (2 * chip + core_ref[0]) * share
+            side_rate_ref[group, chip] = rates_ref[pl.ds(pl.multiple_of(start, share), share), :]
 
     def near(span, carry):
         late = [x_ref[position(span, r, blocks), :] * (SPAN - 1.0 - r) for r in range(SPAN - 1)]
@@ -251,7 +258,7 @@
     lax.fori_loop(0, spans, near, 0)
     wait_all(fetch)
     lax.fori_loop(0, spans, across, 0)
-    copies = send(0, lambda m: run_ref[DOWN, at(m), :], lambda m: run_ref[SLOPE, at(m), :])
+    part(lambda m: run_ref[DOWN, at(m), :], lambda m: run_ref[SLOPE, at(m), :], keep_a_ref, send_a_ref)
     lags = [lag_ref[pl.ds(u * blocks, blocks), :] for u in range(SPAN)]
     factors = [run_ref[FACTOR, at(m), :] for m in range(modes)]
     plain = [lags[SPAN - 1]] * modes
@@ -260,11 +267,47 @@
         sloped = lags[u] * float(u)
         plain = [f * p + lags[u] for f, p in zip(factors, plain)]
         slope = [f * p + sloped for f, p in zip(factors, slope)]
-    copies += send(
-        1,
+    part(
         lambda m: factors[m] * run_ref[SUM0, at(m), :] + plain[m],
         lambda m: factors[m] * run_ref[SUM1, at(m), :] + slope[m],
+        keep_b_ref,
+        send_b_ref,
     )
+
+
+def pair_body(
+    core_ref, a_ref, a_other_ref, b_ref, b_other_ref, s_ref, s_other_ref, rate_ref,
+    out_hbm, held_ref, sem,
+    *, modes, length,
+):
+    groups, chips, rows = s_ref.shape[0], s_ref.shape[1], s_ref.shape[2]
+    first = lane_is_first((rows, LANES), modes)
+    low = core_ref[0] == 0
+
+    def turn(value):
+        return jnp.where(first, pltpu.roll(value, LANES - modes, 1), pltpu.roll(value, modes, 1))
+
+    copies = []
+    for group in range(groups):
+        for chip in range(chips):
+            def both(own_ref, other_ref):
+                own, other = own_ref[group, chip], other_ref[group, chip]
+                return jnp.where(low, own, other), jnp.where(low, other, own)
+
+            (a0, a1), (b0, b1), (s0, s1) = both(a_ref, a_other_ref), both(b_ref, b_other_ref), both(s_ref, s_other_ref)
+            rate = rate_ref[group, chip]
+            far, factor = jnp.exp(-float(length) * rate), jnp.exp(-rate)
+            later = turn(s1)
+            held_ref[0, group, chip] = jnp.where(
+                first, a0 + far * (a1 + float(length) * later), far * (a0 + float(length) * turn(s0)) + a1
+            )
+            cross = s0 * later
+            slope = pltpu.roll(cross + s0 * a1, modes, 1) + a0 * s1
+            held_ref[1, group, chip] = b0 + b1 + factor * jnp.where(first, cross, slope)
+        copies += start_all([
+            pltpu.make_async_copy(held_ref.at[k, group], out_hbm.at[:, (k + 1) * groups + group], sem.at[k, group])
+            for k in range(2)
+        ])
     wait_all(copies)
 
 
@@ -320,28 +363,30 @@
     zero = jnp.zeros((rows, LANES), jnp.float32)
     copies = []
     for group in range(groups):
-        alpha = jnp.exp(-float(length) * rate_ref[group])
+        near = jnp.exp(-float(length) * rate_ref[group])
+        alpha = near * near
+        pairs = [(s_ref[k, group], s_ref[k + 1, group]) for k in range(0, chunks, 2)]
+        pairs = [jnp.where(first, near * early + late, early + near * late) for early, late in pairs]
         before, lead, total0, total1 = zero, zero, zero, zero
         heads = []
-        for k in range(chunks):
-            value = s_ref[k, group]
+        for value in pairs:
             later = pltpu.roll(value, LANES - modes, 1)
             heads.append(before)
             total0 += before * later
             total1 += (lead + before) * later
-            lead = alpha * (lead + float(length) * before)
+            lead = alpha * (lead + 2.0 * length * before)
             before = alpha * before + value
         after = zero
-        for k in reversed(range(chunks)):
+        for k in reversed(range(len(pairs))):
             heads_ref[group, k] = jnp.where(first, heads[k], after)
-            after = alpha * after + s_ref[k, group]
+            after = alpha * after + pairs[k]
         copies += start_all([pltpu.make_async_copy(heads_ref.at[group], out_ref.at[:, group], sem.at[group])])
         acc_ref[group] = jnp.where(first, total0, pltpu.roll(total1, modes, 1))
     skip_ref[...] = tree([s_ref[k, groups, : skip_ref.shape[0]] for k in range(chunks)])
     wait_all(copies)
 
 
-def slope_sum_body(r_ref, own_ref, acc_ref, rate_ref, done_ref, out_ref, pack_ref, sem, *, modes):
+def slope_sum_body(r_ref, own_ref, acc_ref, rate_ref, done_ref, out_ref, ends_ref, pack_ref, sem, *, modes):
     chunks, groups, rows = r_ref.shape[0], rate_ref.shape[0], r_ref.shape[2]
     first = lane_is_first((rows, LANES), modes)
     span = 2 * modes
@@ -361,7 +406,10 @@
         for block in range(fold):
             for r in range(rows // fold):
                 pack_ref[group * fold + block, pl.ds(r, 1), :] = packed[r * fold + block : r * fold + block + 1]
-    wait_all(start_all([pltpu.make_async_copy(pack_ref, out_ref.at[k], sem.at[k]) for k in range(out_ref.shape[0])]))
+    copies = start_all([pltpu.make_async_copy(pack_ref, out_ref.at[k], sem.at[k]) for k in range(out_ref.shape[0])])
+    for group in range(groups):
+        ends_ref[group] = r_ref[:, group]
+    wait_all(copies)
 
 
 def final_body(g_ref, residue_ref, decay_ref, gres_ref, gdec_ref, spread_ref):
@@ -382,9 +430,9 @@
 
 
 def out_body(
-    par_ref, r_ref, y_hbm, z_hbm, hs_hbm, bs_hbm, gate_hbm, key_hbm, value_hbm, cot_hbm,
-    mixed_hbm, ggate_hbm, gkey_hbm, gvalue_hbm,
-    hb_ref, run_ref, loc_ref, snap_ref, in_ref, out_ref, loc_sem, in_sem, out_sem,
+    core_ref, par_ref, ends_ref, other_ref, edge_ref, skip_ref, y_hbm, z_hbm, hs_hbm, bs_hbm, gate_hbm, key_hbm, value_hbm, cot_hbm,
+    mixed_hbm, ggate_hbm, gkey_hbm, gvalue_hbm, gskip_ref,
+    hb_ref, run_ref, loc_ref, snap_ref, in_ref, out_ref, mix_ref, loc_sem, in_sem, out_sem,
 ):
     length, channels = gate_hbm.shape
     blocks = channels // LANES
@@ -413,8 +461,14 @@
                 slot = 2 * kind + k
                 copies.append(pltpu.make_async_copy(ref.at[rows], in_ref.at[slot, rows], in_sem.at[p, slot]))
         fetch.append(start_all(copies))
-    for group in range(groups):
-        hb_ref[pl.ds(group * LANES, LANES), :] = r_ref[:, group].reshape(LANES, LANES).T
+    gskip_ref[...] = skip_ref[...]
+    low = core_ref[0] == 0
+    for group in range(groups):
+        for chip in range(ends_ref.shape[1]):
+            own, other = ends_ref[group, chip], other_ref[group, chip]
+            mix_ref[2 * chip] = jnp.where(low, own, other)
+            mix_ref[2 * chip + 1] = jnp.where(low, other, own)
+        hb_ref[pl.ds(group * LANES, LANES), :] = mix_ref[...].reshape(LANES, LANES).T
     FACTOR, FAR, WEIGHT, HEAD, TAIL = range(5)
     for m in range(modes):
         rows = pl.ds(m * blocks, blocks)
@@ -423,8 +477,10 @@
         run_ref[FACTOR, rows, :] = factor
         run_ref[FAR, rows, :] = jnp.exp(-float(SPAN) * rate)
         run_ref[WEIGHT, rows, :] = by_mode(par_ref, modes + m, blocks) * jnp.sqrt(rate) * factor
-        run_ref[HEAD, rows, :] = by_mode(hb_ref, m, blocks)
-        run_ref[TAIL, rows, :] = by_mode(hb_ref, modes + m, blocks)
+        head, tail, edge = by_mode(hb_ref, m, blocks), by_mode(hb_ref, modes + m, blocks), edge_ref[rows, :]
+        chunk = jnp.exp(-float(length) * rate)
+        run_ref[HEAD, rows, :] = jnp.where(low, head, chunk * head + edge)
+        run_ref[TAIL, rows, :] = jnp.where(low, chunk * tail + edge, tail)
 
     def finish(kind, span, run):
         terms, factors = [], []
@@ -471,7 +527,9 @@
 
 def on_device(gate_in, key_in, value_in, cotangent, skip, residue, decay):
     f32, bf16 = jnp.float32, jnp.bfloat16
-    owners = lax.axis_size("ctx")
+    chips, cores = lax.axis_size("chip"), lax.axis_size("core")
+    ctx = ("chip", "core")
+    owners = chips * cores
     blocks = lax.axis_size("ch")
     length, channels = gate_in.shape
     filters, modes = residue.shape
@@ -479,7 +537,12 @@
     groups = blocks * 2 * modes // LANES
     spans = length // SPAN
     pieces = 4
-    place = lax.axis_index("ctx").astype(jnp.int32).reshape(1)
+    place = lax.axis_index(ctx).astype(jnp.int32).reshape(1)
+    core = lax.axis_index("core").astype(jnp.int32).reshape(1)
+
+    def change(value):
+        return lax.ppermute(value, "core", [(i, cores - 1 - i) for i in range(cores)])
+
     whole = (length, channels)
     signal = (length * blocks, LANES)
     heads_at, tails_at = (spans, modes * blocks, LANES), (spans + 1, modes * blocks, LANES)
@@ -505,31 +568,41 @@
         [dense, DMA((pieces, 4))],
     )([HBM] * 4, gate_in, key_in, value_in, cotangent)
 
-    states, head_states, tail_states = call(
+    side = (groups, chips, *tile)
+    states, head_states, tail_states, own_s, send_s, edge = call(
         state_body,
-        [((owners, groups + 1, *tile), f32, HBM), (heads_at, f32, HBM), (tails_at, f32, HBM)],
+        [((owners, groups + 1, *tile), f32, HBM), (heads_at, f32, HBM), (tails_at, f32, HBM)]
+        + [(side, f32, VMEM)] * 2
+        + [((modes * blocks, LANES), f32, VMEM)],
         16,
         (64 * size, 16 * size),
         [sums, pltpu.VMEM((groups + 1, owners, *tile), f32), pltpu.VMEM(heads_at, f32), pltpu.VMEM(tails_at, f32)]
         + [DMA((groups + 2,)), DMA((2, pieces))],
-    )([VMEM] * 4, params, x, b, sk)
-    states = lax.all_to_all(states, "ctx", 0, 0, tiled=True)
-
-    slopes, rates = call(
+    )([SMEM] + [VMEM] * 4, core, params, x, b, sk)
+    states = lax.all_to_all(states, ctx, 0, 0, tiled=True)
+
+    rates, side_rates, own_a, send_a, own_b, send_b = call(
         slope_body,
-        [((owners, 3 * groups, *tile), f32, HBM), ((groups, *tile), f32, VMEM)],
+        [((groups, *tile), f32, VMEM)] + [(side, f32, VMEM)] * 5,
         16,
         (100 * size, 16 * size),
         [pltpu.VMEM(heads_at, f32), pltpu.VMEM(tails_at, f32), pltpu.VMEM(heads_at, f32), pltpu.VMEM(heads_at, f32)]
-        + [pltpu.VMEM((7, modes * blocks, LANES), f32), pltpu.VMEM((2, groups * LANES, LANES), f32)]
-        + [pltpu.VMEM((2 * groups, owners, *tile), f32), sums, DMA((2 * groups,)), DMA((2,))],
-    )([SMEM] + [VMEM] * 4 + [HBM] * 2, place, params, x, b, lag, head_states, tail_states)
-
-    bundle, heads, acc, grad_skip = call(
+        + [pltpu.VMEM((7, modes * blocks, LANES), f32), sums, pltpu.VMEM((owners, *tile), f32), sums, DMA((2,))],
+    )([SMEM] * 2 + [VMEM] * 4 + [HBM] * 2, place, core, params, x, b, lag, head_states, tail_states)
+
+    (slopes,) = call(
+        functools.partial(pair_body, modes=modes, length=length),
+        [((chips, 3 * groups, *tile), f32, HBM)],
+        8,
+        (size, size),
+        [pltpu.VMEM((2, *side), f32), DMA((2, groups))],
+    )([SMEM] + [VMEM] * 7, core, own_a, change(send_a), own_b, change(send_b), own_s, change(send_s), side_rates)
+
+    bundle, heads, acc, sum_skip = call(
         functools.partial(scan_body, modes=modes, length=length),
         [
-            ((owners, 3 * groups, *tile), f32, HBM),
-            ((groups, owners, *tile), f32, VMEM),
+            ((chips, 3 * groups, *tile), f32, HBM),
+            (side, f32, VMEM),
             ((groups, *tile), f32, VMEM),
             ((blocks, LANES), f32, VMEM),
         ],
@@ -538,7 +611,7 @@
         [DMA((groups,))],
         {2: 0},
     )([VMEM, VMEM, HBM], states, rates, slopes)
-    arrived = lax.all_to_all(bundle, "ctx", 0, 0, tiled=True)
+    arrived = lax.all_to_all(bundle, "chip", 0, 0, tiled=True)
 
     y, z = call(
         local_body,
@@ -549,23 +622,27 @@
     )([VMEM] * 3 + [HBM], params, x, b, skip.reshape(blocks, LANES))
 
     packed = (owners, blocks, share * 2 * modes // LANES, LANES)
-    (grads,) = call(
+    grads, ends = call(
         functools.partial(slope_sum_body, modes=modes),
-        [(packed, f32, HBM)],
+        [(packed, f32, HBM), (side, f32, VMEM)],
         8,
         (10**5, 10**6),
         [pltpu.VMEM(packed[1:], f32), DMA((owners,))],
     )([VMEM] * 4 + [HBM], arrived, heads, acc, rates, y)
-    grads = lax.all_to_all(grads.reshape(owners * blocks, *packed[2:]), ("ctx", "ch"), 0, 0, tiled=True)
-
-    mixed, grad_gate, grad_key, grad_value = call(
+    grads = lax.all_to_all(grads.reshape(owners * blocks, *packed[2:]), ("chip", "core", "ch"), 0, 0, tiled=True)
+
+    mixed, grad_gate, grad_key, grad_value, grad_skip = call(
         out_body,
-        [(whole, bf16, HBM)] * 4,
+        [(whole, bf16, HBM)] * 4 + [((blocks, LANES), f32, VMEM)],
         24,
         (64 * size, 32 * size),
         [sums, pltpu.VMEM((5, modes * blocks, LANES), f32), pltpu.VMEM((2, *signal), f32)]
-        + [pltpu.VMEM((2, *heads_at), f32), dense, dense, DMA((pieces, 4)), DMA((pieces, 4)), DMA((pieces, 4))],
-    )([VMEM] * 2 + [HBM] * 8, params, arrived, y, z, head_states, tail_states, gate_in, key_in, value_in, cotangent)
+        + [pltpu.VMEM((2, *heads_at), f32), dense, dense, pltpu.VMEM((owners, *tile), f32)]
+        + [DMA((pieces, 4)), DMA((pieces, 4)), DMA((pieces, 4))],
+    )(
+        [SMEM] + [VMEM] * 5 + [HBM] * 8,
+        core, params, ends, change(ends), change(edge), sum_skip, y, z, head_states, tail_states, gate_in, key_in, value_in, cotangent,
+    )
 
     grad_residue, grad_log_decay = call(
         final_body, [((modes, filters), f32, VMEM)] * 2, 8, (10**5, 10**6), [pltpu.VMEM((LANES, LANES), f32)]
@@ -574,11 +651,9 @@
 
 
 def solution(mesh):
-    rows = P("ctx", "ch")
-    return jax.shard_map(
-        on_device,
-        mesh=mesh,
-        in_specs=(rows, rows, rows, rows, P("ch"), P("ch", None), P("ch", None)),
-        out_specs=(rows, rows, rows, rows, P("ch"), P("ch", None), P("ch", None)),
-        check_vma=False,
-    )
+    cores = 2
+    shape = (mesh.shape["ctx"] // cores, cores, mesh.shape["ch"])
+    split = jax.sharding.Mesh(mesh.devices.reshape(shape), ("chip", "core", "ch"))
+    rows = P(("chip", "core"), "ch")
+    specs = (rows, rows, rows, rows, P("ch"), P("ch", None), P("ch", None))
+    return jax.shard_map(on_device, mesh=split, in_specs=specs, out_specs=specs, check_vma=False)

time: 64.9 us -> 63.4 us (0.977)
  waiting for transfers between devices: 16.7 us -> 11.5 us
  starting transfers between devices: 23.8 us -> 27.3 us
    all_to_all x3, waiting for transfers between devices: 12.3 us -> 4.78 us  [the longest x1 3.39 us: on_device(): arrived = lax.all_to_all(bundle, 'chip', 0, 0, tiled=True)]
    ppermute x0 -> x5, waiting for transfers between devices: none -> 2.31 us  [change(): lax.ppermute(value, 'core', [(i, cores - 1 - i) for i in range(cores)])]
    ppermute x0 -> x5, starting transfers between devices: none -> 1.94 us  [change(): lax.ppermute(value, 'core', [(i, cores - 1 - i) for i in range(cores)])]
    all_to_all x3, starting transfers between devices: 16.3 us -> 17.9 us  [the longest x1 7.56 us: on_device(): states = lax.all_to_all(states, ctx, 0, 0, tiled=True)]
    pallas_call x9 -> x10, Pallas kernels: 23.2 us -> 23.3 us  [call(): pl.pallas_call(body, out_shape=[pltpu.HBM(s, t) if w is HBM else jax.Shap...]
  transfers between devices with their start and end apart: 4 -> 9, of which waited for: 4 -> 8; matrix products, arithmetic and copies ran while one was open for 0% -> 0% of each run, Pallas kernels for 24% -> 26%
where the time goes in v6:
time: 63.4 us; the launch traced here: 62.8 us
  starting transfers between devices  27.3 us (43%)
  Pallas kernels  23.3 us (37%)
  waiting for transfers between devices  11.5 us (18%)
  between operations  0.73 us (1%)
    pallas_call x10, Pallas kernels, call(): pl.pallas_call(body, out_shape=[pltpu.HBM(s, t) if w is HBM else jax.Shap...  23.3 us
    all_to_all x1, starting transfers between devices, on_device(): states = lax.all_to_all(states, ctx, 0, 0, tiled=True)  7.56 us
    all_to_all x1, starting transfers between devices, on_device(): lax.all_to_all(sent, 'ch', 0, 0, tiled=True)  7.49 us
    all_to_all x1, starting transfers between devices, on_device(): lax.all_to_all(grads.reshape(owners * blocks, *packed[2:]), ('chip', 'cor...  5.23 us
    all_to_all x1, starting transfers between devices, on_device(): arrived = lax.all_to_all(bundle, 'chip', 0, 0, tiled=True)  5.09 us
    all_to_all x1, waiting for transfers between devices, on_device(): lax.all_to_all(sent, 'ch', 0, 0, tiled=True)  4.37 us
    all_to_all x1, waiting for transfers between devices, on_device(): arrived = lax.all_to_all(bundle, 'chip', 0, 0, tiled=True)  3.39 us
    ppermute x5, waiting for transfers between devices, change(): lax.ppermute(value, 'core', [(i, cores - 1 - i) for i in range(cores)])  2.31 us
  transfers between devices with their start and end apart: 9, of which 8 were waited for; matrix products, arithmetic and copies ran while one was open for 0% of the time, Pallas kernels for 26%

profile of v6, /device:TPU:1, one launch (start us, length us, event | category | flops | bytes accessed | tf_op | source)
XLA Modules:
  0.0 62.8 jit_solution(17497829063047161833)
XLA Ops:
  0.6 1.4 %shard_map.126 = f32[8,32,128]{2,1,0:T(8,128)} custom-call(f32[16,128]{1,0:T(8,128)} %bitcast.16, f32[16,128]{1,0:T(8,128)} %bitcast.18), custom_call_target="tpu_custom_call" | custom-call | bytes 100000 | tf_op jit(solution)/shard_map/pallas_call | solution.py:21
  2.1 7.5 %all-to-all-start = ((f32[8,32,128]{2,1,0:T(8,128)}), f32[8,32,128]{2,1,0:T(8,128)S(1)}, u32[]{:S(2)}, u32[]{:S(2)}) async-start(f32[8,32,128]{2,1,0:T(8,128)} %shard_map.126), calls=%async_computation | async-start | bytes 262144 | tf_op jit(solution)/shard_map/all_to_all | solution.py:561
  9.6 2.4 %shard_map.127 = (f32[2048,128]{1,0:T(8,128)S(1)}, f32[2048,128]{1,0:T(8,128)S(1)}, f32[8,128]{1,0:T(8,128)S(1)}, f32[128,128]{1,0:T(8,128)S(1)}) custom-call(bf16[256,1024]{1,0:T(8,128)(2,1)} %gate_hbm.3, bf16[256,1024]{1,0:T(8,128)(2,1)} %key_hbm.3, bf16[256,1024]{1,0:T(8,128)(2,1)} %value_hbm.3, bf16[256,1024]{1,0:T(8,128)(2,1)} %cot_hbm.3), custom_call_target="tpu_custom_call" | custom-call | flops 2097152 | bytes 4194304 | tf_op jit(solution)/shard_map/pallas_call | solution.py:21
  12.0 4.4 %all-to-all-done = f32[8,32,128]{2,1,0:T(8,128)S(1)} async-done(((f32[8,32,128]{2,1,0:T(8,128)}), f32[8,32,128]{2,1,0:T(8,128)S(1)}, u32[]{:S(2)}, u32[]{:S(2)}) %all-to-all-start) | async-done | bytes 131104 | tf_op jit(solution)/shard_map/all_to_all | solution.py:561
  16.3 3.3 %shard_map.128 = (f32[16,3,8,128]{3,2,1,0:T(8,128)}, f32[16,128,128]{2,1,0:T(8,128)}, f32[17,128,128]{2,1,0:T(8,128)}, f32[2,8,8,128]{3,2,1,0:T(8,128)S(1)}, f32...) custom-call(s32[1]{0:T(128)} %bitcast.core_ref, f32[256,128]{1,0:T(8,128)S(1)} %bitcast.11, ...), custom_call_target="tpu_custom_call" | custom-call | flops 16777216 | bytes 4194304 | tf_op jit(solution)/shard_map/pallas_call | solution.py:21
  19.7 7.6 %all-to-all-start.1 = ((f32[16,3,8,128]{3,2,1,0:T(8,128)}), f32[16,3,8,128]{3,2,1,0:T(8,128)S(1)}, u32[]{:S(2)}, u32[]{:S(2)}) async-start(f32[16,3,8,128]{3,2,1,0:T(8,128)} %get-tuple-element.41), calls=%async_computation.1 | async-start | bytes 393216 | tf_op jit(solution)/shard_map/all_to_all | solution.py:582
  27.2 4.0 %shard_map.129 = (f32[2,8,128]{2,1,0:T(8,128)S(1)}, f32[2,8,8,128]{3,2,1,0:T(8,128)S(1)}, f32[2,8,8,128]{3,2,1,0:T(8,128)S(1)}, f32[2,8,8,128]{3,2,1,0:T(8,128)S...) custom-call(s32[1]{0:T(128)} %bitcast.4.index_ref, s32[1]{0:T(128)} %bitcast.core_ref, ...), custom_call_target="tpu_custom_call" | custom-call | flops 26214400 | bytes 4194304 | tf_op jit(solution)/shard_map/pallas_call | solution.py:21
  31.2 0.2 collective-permute-start
  31.4 0.4 collective-permute-start.1
  31.9 0.6 %collective-permute-done.a_other_ref = f32[2,8,8,128]{3,2,1,0:T(8,128)S(1)} collective-permute-done((f32[2,8,8,128]{3,2,1,0:T(8,128)S(1)}, f32[2,8,8,128]{3,2,1,0:T(8,128)S(1)}, u32[]{:S(2)}, u32[]{:S(2)}) %collective-permute-start) | collective-permute-done | bytes 65568 | tf_op jit(solution)/shard_map/ppermute | solution.py:544
  32.7 0.4 collective-permute-done.2.s_other_ref
  33.1 0.8 %shard_map.130.slopes_ref = f32[8,6,8,128]{3,2,1,0:T(8,128)} custom-call(s32[1]{0:T(128)} %bitcast.core_ref, f32[2,8,8,128]{3,2,1,0:T(8,128)S(1)} %get-tuple-element.46.a_ref, f32[2,8,8,128]{3,2,1,0:T(8,128)S(1)} %collective-permute-done.a_other_ref, f32[2,8,8,128]{3,2,1,0:T(8,128)S(1)} %get-tuple-element.48.b_ref, ...), custom_call_target="tpu_custom_call" | custom-call | flops 262144 | bytes 262144 | tf_op jit(solution)/shard_map/pallas_call | solution.py:21
  33.9 0.7 %shard_map.131 = (f32[8,6,8,128]{3,2,1,0:T(8,128)}, f32[2,8,8,128]{3,2,1,0:T(8,128)S(1)}, f32[2,8,128]{2,1,0:T(8,128)S(1)}, f32[8,128]{1,0:T(8,128)S(1)}) custom-call(f32[16,3,8,128]{3,2,1,0:T(8,128)S(1)} %all-to-all-done.1.s_ref, f32[2,8,128]{2,1,0:T(8,128)S(1)} %get-tuple-element.45.rate_ref, ...), custom_call_target="tpu_custom_call", output_to_operand_aliasing={{0}: (2, {})} | custom-call | flops 100000 | bytes 1000000 | tf_op jit(solution)/shard_map/pallas_call | solution.py:21
  34.7 5.1 %all-to-all-start.2 = ((f32[8,6,8,128]{3,2,1,0:T(8,128)}), f32[8,6,8,128]{3,2,1,0:T(8,128)S(1)}, u32[]{:S(2)}, u32[]{:S(2)}) async-start(f32[8,6,8,128]{3,2,1,0:T(8,128)} %get-tuple-element.53), calls=%async_computation.2 | async-start | bytes 393216 | tf_op jit(solution)/shard_map/all_to_all | solution.py:614
  39.8 2.7 %shard_map.132 = (f32[2048,128]{1,0:T(8,128)}, f32[2048,128]{1,0:T(8,128)}) custom-call(f32[256,128]{1,0:T(8,128)S(1)} %bitcast.13, f32[2048,128]{1,0:T(8,128)S(1)} %get-tuple-element.38.x_ref, f32[2048,128]{1,0:T(8,128)S(1)} %get-tuple-element.39.b_ref, f32[8,128]{1,0:T(8,128)} %bitcast.21), custom_call_target="tpu_custom_call" | custom-call | flops 10485760 | bytes 4194304 | tf_op jit(solution)/shard_map/pallas_call | solution.py:21
  42.5 3.4 %all-to-all-done.2.r_ref = f32[8,6,8,128]{3,2,1,0:T(8,128)S(1)} async-done(((f32[8,6,8,128]{3,2,1,0:T(8,128)}), f32[8,6,8,128]{3,2,1,0:T(8,128)S(1)}, u32[]{:S(2)}, u32[]{:S(2)}) %all-to-all-start.2) | async-done | bytes 196640 | tf_op jit(solution)/shard_map/all_to_all | solution.py:614
  45.9 1.0 %shard_map.133 = (f32[16,8,2,128]{3,2,1,0:T(2,128)}, f32[2,8,8,128]{3,2,1,0:T(8,128)S(1)}) custom-call(f32[8,6,8,128]{3,2,1,0:T(8,128)S(1)} %all-to-all-done.2.r_ref, f32[2,8,8,128]{3,2,1,0:T(8,128)S(1)} %get-tuple-element.54.own_ref, f32[2,8,128]{2,1,0:T(8,128)S(1)} %get-tuple-element.55.acc_ref, f32[2,8,128]{2,1,0:T(8,128)S(1)} %get-tuple-element.45.rate_ref, ...), custom_call_target="tpu_custom_call" | custom-call | flops 100000 | bytes 1000000 | tf_op jit(solution)/shard_map/pallas_call | solution.py:21
  46.8 5.2 %all-to-all-start.3 = ((f32[128,2,128]{2,1,0:T(2,128)}), f32[128,2,128]{2,1,0:T(2,128)S(1)}, u32[]{:S(2)}, u32[]{:S(2)}) async-start(f32[128,2,128]{2,1,0:T(2,128)} %bitcast.20), calls=%async_computation.3 | async-start | bytes 262144 | tf_op jit(solution)/shard_map/all_to_all | solution.py:632
  52.1 1.1 %collective-permute-start.4 = (f32[128,128]{1,0:T(8,128)S(1)}, f32[128,128]{1,0:T(8,128)S(1)}, u32[]{:S(2)}, u32[]{:S(2)}) collective-permute-start(f32[128,128]{1,0:T(8,128)S(1)} %get-tuple-element.58), channel_id=1, source_target_pairs={{0,8},{8,0},{1,9},{9,1},{2,10},{10,2},{3,11},{11,3},{4,12},{12,4},... | collective-permute-start | bytes 196616 | tf_op jit(solution)/shard_map/ppermute | solution.py:544
  53.3 0.8 %collective-permute-done.4.edge_ref = f32[128,128]{1,0:T(8,128)S(1)} collective-permute-done((f32[128,128]{1,0:T(8,128)S(1)}, f32[128,128]{1,0:T(8,128)S(1)}, u32[]{:S(2)}, u32[]{:S(2)}) %collective-permute-start.4) | collective-permute-done | bytes 65568 | tf_op jit(solution)/shard_map/ppermute | solution.py:544
  54.1 0.4 collective-permute-done.3.other_ref
  54.5 6.2 %shard_map.134 = (bf16[256,1024]{1,0:T(8,128)(2,1)}, bf16[256,1024]{1,0:T(8,128)(2,1)}, bf16[256,1024]{1,0:T(8,128)(2,1)}, bf16[256,1024]{1,0:T(8,128)(2,1)}, f32[8,128]{1,0:T(8,128)}) custom-call(s32[1]{0:T(128)} %bitcast.core_ref, f32[256,128]{1,0:T(8,128)S(1)} %bitcast.14, f32[2,8,8,128]{3,2,1,0:T(8,128)S(1)} %get-tuple-element.57.ends_ref, ...), custom_call_target="tpu_custom_call" | custom-call | flops 16777216 | bytes 8388608 | tf_op jit(solution)/shard_map/pallas_call | solution.py:21
  60.7 1.4 %all-to-all-done.3 = f32[128,2,128]{2,1,0:T(2,128)S(1)} async-done(((f32[128,2,128]{2,1,0:T(2,128)}), f32[128,2,128]{2,1,0:T(2,128)S(1)}, u32[]{:S(2)}, u32[]{:S(2)}) %all-to-all-start.3) | async-done | bytes 131104 | tf_op jit(solution)/shard_map/all_to_all | solution.py:632
  62.1 0.8 %shard_map.135 = (f32[16,128]{1,0:T(8,128)}, f32[16,128]{1,0:T(8,128)}) custom-call(f32[16,8,2,128]{3,2,1,0:T(2,128)S(1)} %bitcast.15, f32[16,128]{1,0:T(8,128)S(1)} %bitcast.19, f32[16,128]{1,0:T(8,128)S(1)} %bitcast.17), custom_call_target="tpu_custom_call" | custom-call | flops 100000 | bytes 1000000 | tf_op jit(solution)/shard_map/pallas_call | solution.py:21
  (8 shorter events, 0.4 us)
Async XLA Ops:
  2.1 14.3 %all-to-all-start = ((f32[8,32,128]{2,1,0:T(8,128)}), f32[8,32,128]{2,1,0:T(8,128)S(1)}, u32[]{:S(2)}, u32[]{:S(2)}) async-start(f32[8,32,128]{2,1,0:T(8,128)} %shard_map.126), calls=%async_computation | async-start | bytes 262144 | tf_op jit(solution)/shard_map/all_to_all | solution.py:561
  19.7 14.3 %all-to-all-start.1 = ((f32[16,3,8,128]{3,2,1,0:T(8,128)}), f32[16,3,8,128]{3,2,1,0:T(8,128)S(1)}, u32[]{:S(2)}, u32[]{:S(2)}) async-start(f32[16,3,8,128]{3,2,1,0:T(8,128)} %get-tuple-element.41), calls=%async_computation.1 | async-start | bytes 393216 | tf_op jit(solution)/shard_map/all_to_all | solution.py:582
  31.2 1.3 %collective-permute-start = (f32[2,8,8,128]{3,2,1,0:T(8,128)S(1)}, f32[2,8,8,128]{3,2,1,0:T(8,128)S(1)}, u32[]{:S(2)}, u32[]{:S(2)}) collective-permute-start(f32[2,8,8,128]{3,2,1,0:T(8,128)S(1)} %get-tuple-element.47), channel_id=1, source_target_pairs={{0,8},{8,0},{1,9},{9,1},{2,10},{10,2},{3,11},{11,3},{4,12},{12,4},... | collective-permute-start | bytes 196616 | tf_op jit(solution)/shard_map/ppermute | solution.py:544
  31.4 1.3 %collective-permute-start.1 = (f32[2,8,8,128]{3,2,1,0:T(8,128)S(1)}, f32[2,8,8,128]{3,2,1,0:T(8,128)S(1)}, u32[]{:S(2)}, u32[]{:S(2)}) collective-permute-start(f32[2,8,8,128]{3,2,1,0:T(8,128)S(1)} %get-tuple-element.49), channel_id=1, source_target_pairs={{0,8},{8,0},{1,9},{9,1},{2,10},{10,2},{3,11},{11,3},{4,12},{12,4},... | collective-permute-start | bytes 196616 | tf_op jit(solution)/shard_map/ppermute | solution.py:544
  31.8 1.3 %collective-permute-start.2 = (f32[2,8,8,128]{3,2,1,0:T(8,128)S(1)}, f32[2,8,8,128]{3,2,1,0:T(8,128)S(1)}, u32[]{:S(2)}, u32[]{:S(2)}) collective-permute-start(f32[2,8,8,128]{3,2,1,0:T(8,128)S(1)} %get-tuple-element.51), channel_id=1, source_target_pairs={{0,8},{8,0},{1,9},{9,1},{2,10},{10,2},{3,11},{11,3},{4,12},{12,4},... | collective-permute-start | bytes 196616 | tf_op jit(solution)/shard_map/ppermute | solution.py:544
  34.7 11.2 %all-to-all-start.2 = ((f32[8,6,8,128]{3,2,1,0:T(8,128)}), f32[8,6,8,128]{3,2,1,0:T(8,128)S(1)}, u32[]{:S(2)}, u32[]{:S(2)}) async-start(f32[8,6,8,128]{3,2,1,0:T(8,128)} %get-tuple-element.53), calls=%async_computation.2 | async-start | bytes 393216 | tf_op jit(solution)/shard_map/all_to_all | solution.py:614
  46.8 15.2 %all-to-all-start.3 = ((f32[128,2,128]{2,1,0:T(2,128)}), f32[128,2,128]{2,1,0:T(2,128)S(1)}, u32[]{:S(2)}, u32[]{:S(2)}) async-start(f32[128,2,128]{2,1,0:T(2,128)} %bitcast.20), calls=%async_computation.3 | async-start | bytes 262144 | tf_op jit(solution)/shard_map/all_to_all | solution.py:632
  52.1 2.0 %collective-permute-start.4 = (f32[128,128]{1,0:T(8,128)S(1)}, f32[128,128]{1,0:T(8,128)S(1)}, u32[]{:S(2)}, u32[]{:S(2)}) collective-permute-start(f32[128,128]{1,0:T(8,128)S(1)} %get-tuple-element.58), channel_id=1, source_target_pairs={{0,8},{8,0},{1,9},{9,1},{2,10},{10,2},{3,11},{11,3},{4,12},{12,4},... | collective-permute-start | bytes 196616 | tf_op jit(solution)/shard_map/ppermute | solution.py:544
  53.2 1.3 %collective-permute-start.3 = (f32[2,8,8,128]{3,2,1,0:T(8,128)S(1)}, f32[2,8,8,128]{3,2,1,0:T(8,128)S(1)}, u32[]{:S(2)}, u32[]{:S(2)}) collective-permute-start(f32[2,8,8,128]{3,2,1,0:T(8,128)S(1)} %get-tuple-element.57.ends_ref), channel_id=1, source_target_pairs={{0,8},{8,0},{1,9},{9,1},{2,10},{10,2},{3,11},{11,3},{4,12},{12,4},... | collective-permute-start | bytes 196616 | tf_op jit(solution)/shard_map/ppermute | solution.py:544
  54.5 7.6 %copy-start = (f32[128,16]{0,1:T(8,128)S(1)}, f32[128,16]{0,1:T(8,128)}, u32[]{:S(2)}) copy-start(f32[128,16]{0,1:T(8,128)} %param.13) | copy-start | bytes 24580
  54.5 7.6 %copy-start.1 = (f32[128,16]{0,1:T(8,128)S(1)}, f32[128,16]{0,1:T(8,128)}, u32[]{:S(2)}) copy-start(f32[128,16]{0,1:T(8,128)} %param.12) | copy-start | bytes 24580

commit v7 on v6

--- a/solution.py
+++ b/solution.py
@@ -127,21 +127,12 @@
         send_ref[chip] = turned_ref[2 * chip + 1 - core]
 
 
-def state_body(
-    core_ref, par_ref, x_ref, b_ref, sk_ref,
-    out_ref, hs_hbm, bs_hbm, keep_ref, send_ref, edge_ref,
-    sums_ref, turn_ref, hs_ref, bs_ref, sem, snap_sem,
-):
-    owners = out_ref.shape[0]
-    groups = sums_ref.shape[0] // LANES
+def state_body(par_ref, x_ref, b_ref, sk_ref, total_ref, hs_hbm, bs_hbm, hs_ref, bs_ref, sem, last_sem):
+    spans = hs_ref.shape[0]
     blocks = sk_ref.shape[0]
     modes = par_ref.shape[0] // blocks // 2
-    spans = hs_ref.shape[0]
-    pieces = snap_sem.shape[1]
+    pieces = sem.shape[1]
     part = spans // pieces
-    for owner in range(owners):
-        turn_ref[groups, owner, :blocks] = sk_ref[...]
-    copies = start_all([pltpu.make_async_copy(turn_ref.at[groups], out_ref.at[:, groups], sem.at[groups])])
     factor = [jnp.exp(-by_mode(par_ref, m, blocks)) for m in range(modes)]
 
     def step(span, carry):
@@ -151,38 +142,34 @@
             hs_ref[span, pl.ds(m * blocks, blocks), :] = ups[m]
             bs_ref[mirror + 1, pl.ds(m * blocks, blocks), :] = downs[m]
         for r in range(SPAN):
-            x = x_ref[pl.ds(pl.multiple_of((span * SPAN + r) * blocks, blocks), blocks), :]
-            b = b_ref[pl.ds(pl.multiple_of((mirror * SPAN + SPAN - 1 - r) * blocks, blocks), blocks), :]
+            x = x_ref[position(span, r, blocks), :]
+            b = b_ref[position(mirror, SPAN - 1 - r, blocks), :]
             ups = tuple(f * u + x for f, u in zip(factor, ups))
             downs = tuple(f * d + b for f, d in zip(factor, downs))
         return ups, downs
 
     zero = tuple(jnp.zeros((blocks, LANES), jnp.float32) for _ in range(modes))
     ups, downs = zero, zero
+    copies = []
     for p in range(pieces):
         ups, downs = lax.fori_loop(p * part, (p + 1) * part, step, (ups, downs))
         here, there = pl.ds(p * part, part), pl.ds((pieces - 1 - p) * part + 1, part)
         copies += start_all([
-            pltpu.make_async_copy(hs_ref.at[here], hs_hbm.at[here], snap_sem.at[0, p]),
-            pltpu.make_async_copy(bs_ref.at[there], bs_hbm.at[there], snap_sem.at[1, p]),
+            pltpu.make_async_copy(hs_ref.at[here], hs_hbm.at[here], sem.at[0, p]),
+            pltpu.make_async_copy(bs_ref.at[there], bs_hbm.at[there], sem.at[1, p]),
         ])
     for m in range(modes):
         bs_ref[0, pl.ds(m * blocks, blocks), :] = downs[m]
-        edge_ref[pl.ds(m * blocks, blocks), :] = jnp.where(core_ref[0] == 0, ups[m], downs[m])
-        sums_ref[pl.ds(m, blocks, stride=2 * modes), :] = ups[m]
-        sums_ref[pl.ds(modes + m, blocks, stride=2 * modes), :] = downs[m]
-    copies += start_all([pltpu.make_async_copy(bs_ref.at[0], bs_hbm.at[0], sem.at[groups + 1])])
-    for group in range(groups):
-        turn_ref[group] = turned(sums_ref, group, owners)
-        copies += start_all([pltpu.make_async_copy(turn_ref.at[group], out_ref.at[:, group], sem.at[group])])
-    for group in range(groups):
-        part_slices(core_ref[0], turn_ref.at[group], keep_ref.at[group], send_ref.at[group])
+        total_ref[pl.ds(m * blocks, blocks), :] = ups[m]
+        total_ref[pl.ds((modes + m) * blocks, blocks), :] = downs[m]
+    total_ref[pl.ds(2 * modes * blocks, blocks), :] = sk_ref[...]
+    copies += start_all([pltpu.make_async_copy(bs_ref.at[0], bs_hbm.at[0], last_sem)])
     wait_all(copies)
 
 
 def slope_body(
-    index_ref, core_ref, par_ref, x_ref, b_ref, lag_ref, hs_hbm, bs_hbm,
-    rate_ref, side_rate_ref, keep_a_ref, send_a_ref, keep_b_ref, send_b_ref,
+    index_ref, core_ref, par_ref, x_ref, b_ref, lag_ref, total_ref, joined_ref, hs_hbm, bs_hbm,
+    rate_ref, side_rate_ref, keep_s_ref, send_s_ref, keep_a_ref, send_a_ref, keep_b_ref, send_b_ref,
     hs_ref, bs_ref, up_ref, down_ref, run_ref, sums_ref, turn_ref, rates_ref, snap_sem,
 ):
     owners = turn_ref.shape[0]
@@ -217,6 +204,10 @@
     def at(m):
         return pl.ds(m * blocks, blocks)
 
+    def totals(kind):
+        return lambda m: total_ref[pl.ds((kind * modes + m) * blocks, blocks), :]
+
+    part(totals(0), totals(1), keep_s_ref, send_s_ref)
     for group in range(groups):
         for block in range(group * blocks // groups, (group + 1) * blocks // groups):
             decay = par_ref[pl.ds(block * 2 * modes, modes), :]
@@ -276,7 +267,7 @@
 
 
 def pair_body(
-    core_ref, a_ref, a_other_ref, b_ref, b_other_ref, s_ref, s_other_ref, rate_ref,
+    core_ref, a_ref, a_other_ref, b_ref, b_other_ref, s_ref, s_other_ref, rate_ref, joined_ref,
     out_hbm, held_ref, sem,
     *, modes, length,
 ):
@@ -298,20 +289,54 @@
             rate = rate_ref[group, chip]
             far, factor = jnp.exp(-float(length) * rate), jnp.exp(-rate)
             later = turn(s1)
-            held_ref[0, group, chip] = jnp.where(
+            held_ref[0, group, chip] = jnp.where(first, far * s0 + s1, s0 + far * s1)
+            held_ref[1, group, chip] = jnp.where(
                 first, a0 + far * (a1 + float(length) * later), far * (a0 + float(length) * turn(s0)) + a1
             )
             cross = s0 * later
             slope = pltpu.roll(cross + s0 * a1, modes, 1) + a0 * s1
-            held_ref[1, group, chip] = b0 + b1 + factor * jnp.where(first, cross, slope)
+            held_ref[2, group, chip] = b0 + b1 + factor * jnp.where(first, cross, slope)
         copies += start_all([
-            pltpu.make_async_copy(held_ref.at[k, group], out_hbm.at[:, (k + 1) * groups + group], sem.at[k, group])
-            for k in range(2)
+            pltpu.make_async_copy(held_ref.at[k, group], out_hbm.at[:, k * groups + group], sem.at[k, group])
+            for k in range(3)
         ])
     wait_all(copies)
 
 
-def local_body(par_ref, x_ref, b_ref, skip_hbm, y_hbm, z_hbm, skip_ref, out_ref, skip_sem, sem):
+def join_weights(index, step, rate, length):
+    run = 2**step
+    upper = lax.rem(lax.div(index, run), 2) == 1
+    offset = lax.rem(index, run)
+    chunk = float(length) * rate
+    ahead = jnp.where(upper, offset, run - 1 - offset).astype(jnp.float32)
+    return upper, jnp.exp(-float(run) * chunk), jnp.exp(-ahead * chunk)
+
+
+def join_body(index_ref, par_ref, total_ref, other_ref, *refs, step, length, modes, last):
+    sends_later = lax.rem(lax.div(index_ref[0], 2 ** (step + 1)), 2) == 1
+    held_ref = refs[0] if step else None
+    next_ref, out_ref = refs[-2:]
+    blocks = par_ref.shape[0] // modes // 2
+    for m in range(modes):
+        low, high = pl.ds(m * blocks, blocks), pl.ds((modes + m) * blocks, blocks)
+        upper, far, near = join_weights(index_ref[0], step, by_mode(par_ref, m, blocks), length)
+        x, y, ox, oy = total_ref[low, :], total_ref[high, :], other_ref[low, :], other_ref[high, :]
+        head, tail = jnp.where(upper, near * ox, 0.0), jnp.where(upper, 0.0, near * oy)
+        if held_ref is not None:
+            head, tail = head + held_ref[low, :], tail + held_ref[high, :]
+        out_ref[low, :] = head
+        out_ref[high, :] = tail
+        new_x, new_y = jnp.where(upper, far * ox + x, far * x + ox), jnp.where(upper, far * y + oy, far * oy + y)
+        if last:
+            next_ref[low, :] = jnp.where(sends_later, new_y, new_x)
+        else:
+            next_ref[low, :] = new_x
+            next_ref[high, :] = new_y
+    rest = pl.ds(2 * modes * blocks, blocks)
+    next_ref[pl.ds(next_ref.shape[0] - blocks, blocks), :] = total_ref[rest, :] + other_ref[rest, :]
+
+
+def local_body(par_ref, x_ref, b_ref, joined_ref, skip_hbm, y_hbm, z_hbm, skip_ref, out_ref, skip_sem, sem):
     fetch = pltpu.make_async_copy(skip_hbm, skip_ref, skip_sem)
     fetch.start()
     blocks = skip_ref.shape[0]
@@ -357,47 +382,33 @@
     return lax.broadcasted_iota(jnp.int32, shape, 1) % (2 * modes) < modes
 
 
-def scan_body(s_ref, rate_ref, slopes_ref, out_ref, heads_ref, acc_ref, skip_ref, sem, *, modes, length):
-    chunks, groups, rows = s_ref.shape[0], rate_ref.shape[0], s_ref.shape[2]
+def scan_body(s_ref, rate_ref, done_hbm, out_ref, pack_ref, sem, *, modes, length):
+    chunks, groups, rows = s_ref.shape[0], rate_ref.shape[0], rate_ref.shape[1]
     first = lane_is_first((rows, LANES), modes)
     zero = jnp.zeros((rows, LANES), jnp.float32)
-    copies = []
-    for group in range(groups):
-        near = jnp.exp(-float(length) * rate_ref[group])
-        alpha = near * near
-        pairs = [(s_ref[k, group], s_ref[k + 1, group]) for k in range(0, chunks, 2)]
-        pairs = [jnp.where(first, near * early + late, early + near * late) for early, late in pairs]
-        before, lead, total0, total1 = zero, zero, zero, zero
-        heads = []
-        for value in pairs:
-            later = pltpu.roll(value, LANES - modes, 1)
-            heads.append(before)
-            total0 += before * later
-            total1 += (lead + before) * later
-            lead = alpha * (lead + 2.0 * length * before)
-            before = alpha * before + value
-        after = zero
-        for k in reversed(range(len(pairs))):
-            heads_ref[group, k] = jnp.where(first, heads[k], after)
-            after = alpha * after + pairs[k]
-        copies += start_all([pltpu.make_async_copy(heads_ref.at[group], out_ref.at[:, group], sem.at[group])])
-        acc_ref[group] = jnp.where(first, total0, pltpu.roll(total1, modes, 1))
-    skip_ref[...] = tree([s_ref[k, groups, : skip_ref.shape[0]] for k in range(chunks)])
-    wait_all(copies)
-
-
-def slope_sum_body(r_ref, own_ref, acc_ref, rate_ref, done_ref, out_ref, ends_ref, pack_ref, sem, *, modes):
-    chunks, groups, rows = r_ref.shape[0], rate_ref.shape[0], r_ref.shape[2]
-    first = lane_is_first((rows, LANES), modes)
     span = 2 * modes
     fold = LANES // span
     row = lax.broadcasted_iota(jnp.int32, (rows, LANES), 0) % fold
     column = lax.broadcasted_iota(jnp.int32, (rows, LANES), 1) // span
     for group in range(groups):
-        cross = tree([own_ref[group, k] * r_ref[k, groups + group] for k in range(chunks)])
-        inner = tree([r_ref[k, 2 * groups + group] for k in range(chunks)])
-        cross = jnp.where(first, 0.0, cross + pltpu.roll(cross, modes, 1))
-        total = inner + jnp.exp(-rate_ref[group]) * (acc_ref[group] + cross)
+        alpha = jnp.exp(-float(length) * rate_ref[group])
+        before, lead, total0, total1 = zero, zero, zero, zero
+        heads = []
+        for k in range(chunks):
+            value = s_ref[k, group]
+            later = pltpu.roll(value, LANES - modes, 1)
+            heads.append(before)
+            total0 += before * later
+            total1 += (lead + before) * later
+            lead = alpha * (lead + float(length) * before)
+            before = alpha * before + value
+        after, cross = zero, zero
+        for k in reversed(range(chunks)):
+            cross += jnp.where(first, heads[k], after) * s_ref[k, groups + group]
+            after = alpha * after + s_ref[k, group]
+        inner = tree([s_ref[k, 2 * groups + group] for k in range(chunks)])
+        outer = jnp.where(first, total0, pltpu.roll(total1, modes, 1) + cross + pltpu.roll(cross, modes, 1))
+        total = inner + jnp.exp(-rate_ref[group]) * outer
         packed = total
         for shift in range(1, fold):
             moved = pltpu.roll(total, LANES - shift * span, 1)
@@ -406,10 +417,7 @@
         for block in range(fold):
             for r in range(rows // fold):
                 pack_ref[group * fold + block, pl.ds(r, 1), :] = packed[r * fold + block : r * fold + block + 1]
-    copies = start_all([pltpu.make_async_copy(pack_ref, out_ref.at[k], sem.at[k]) for k in range(out_ref.shape[0])])
-    for group in range(groups):
-        ends_ref[group] = r_ref[:, group]
-    wait_all(copies)
+    wait_all(start_all([pltpu.make_async_copy(pack_ref, out_ref.at[k], sem.at[k]) for k in range(out_ref.shape[0])]))
 
 
 def final_body(g_ref, residue_ref, decay_ref, gres_ref, gdec_ref, spread_ref):
@@ -429,46 +437,24 @@
     gdec_ref[...] = residue_ref[...] * root * (0.5 * plain - decay * slope)
 
 
-def out_body(
-    core_ref, par_ref, ends_ref, other_ref, edge_ref, skip_ref, y_hbm, z_hbm, hs_hbm, bs_hbm, gate_hbm, key_hbm, value_hbm, cot_hbm,
-    mixed_hbm, ggate_hbm, gkey_hbm, gvalue_hbm, gskip_ref,
-    hb_ref, run_ref, loc_ref, snap_ref, in_ref, out_ref, mix_ref, loc_sem, in_sem, out_sem,
+def settle_body(
+    par_ref, held_ref, y_hbm, z_hbm, hs_hbm, bs_hbm,
+    loc_ref,
+    run_ref, snap_ref, sem,
 ):
-    length, channels = gate_hbm.shape
-    blocks = channels // LANES
-    modes = par_ref.shape[0] // blocks // 2
-    groups = hb_ref.shape[0] // LANES
-    spans = length // SPAN
-    pieces = loc_sem.shape[0]
+    spans, blocks = hs_hbm.shape[0], y_hbm.shape[0] // hs_hbm.shape[0] // SPAN
+    modes = hs_hbm.shape[1] // blocks
+    pieces = sem.shape[0]
     part = spans // pieces
-    depth = part * SPAN
     fetch = []
     for p in range(pieces):
-        mirror = pieces - 1 - p
         copies = []
-        for kind, (place, local, snaps, shift, near) in enumerate((
-            (p, y_hbm, hs_hbm, 0, (gate_hbm, cot_hbm)),
-            (mirror, z_hbm, bs_hbm, 1, (value_hbm, key_hbm)),
-        )):
-            rows = pl.ds(place * depth * blocks, depth * blocks)
-            copies.append(pltpu.make_async_copy(local.at[rows], loc_ref.at[kind, rows], loc_sem.at[p, 2 * kind]))
+        for kind, (place, local, snaps, shift) in enumerate(((p, y_hbm, hs_hbm, 0), (pieces - 1 - p, z_hbm, bs_hbm, 1))):
+            rows = pl.ds(place * part * SPAN * blocks, part * SPAN * blocks)
+            copies.append(pltpu.make_async_copy(local.at[rows], loc_ref.at[kind, rows], sem.at[p, 2 * kind]))
             source, target = pl.ds(place * part + shift, part), pl.ds(place * part, part)
-            copies.append(
-                pltpu.make_async_copy(snaps.at[source], snap_ref.at[kind, target], loc_sem.at[p, 2 * kind + 1])
-            )
-            rows = pl.ds(place * depth, depth)
-            for k, ref in enumerate(near):
-                slot = 2 * kind + k
-                copies.append(pltpu.make_async_copy(ref.at[rows], in_ref.at[slot, rows], in_sem.at[p, slot]))
+            copies.append(pltpu.make_async_copy(snaps.at[source], snap_ref.at[kind, target], sem.at[p, 2 * kind + 1]))
         fetch.append(start_all(copies))
-    gskip_ref[...] = skip_ref[...]
-    low = core_ref[0] == 0
-    for group in range(groups):
-        for chip in range(ends_ref.shape[1]):
-            own, other = ends_ref[group, chip], other_ref[group, chip]
-            mix_ref[2 * chip] = jnp.where(low, own, other)
-            mix_ref[2 * chip + 1] = jnp.where(low, other, own)
-        hb_ref[pl.ds(group * LANES, LANES), :] = mix_ref[...].reshape(LANES, LANES).T
     FACTOR, FAR, WEIGHT, HEAD, TAIL = range(5)
     for m in range(modes):
         rows = pl.ds(m * blocks, blocks)
@@ -477,10 +463,8 @@
         run_ref[FACTOR, rows, :] = factor
         run_ref[FAR, rows, :] = jnp.exp(-float(SPAN) * rate)
         run_ref[WEIGHT, rows, :] = by_mode(par_ref, modes + m, blocks) * jnp.sqrt(rate) * factor
-        head, tail, edge = by_mode(hb_ref, m, blocks), by_mode(hb_ref, modes + m, blocks), edge_ref[rows, :]
-        chunk = jnp.exp(-float(length) * rate)
-        run_ref[HEAD, rows, :] = jnp.where(low, head, chunk * head + edge)
-        run_ref[TAIL, rows, :] = jnp.where(low, chunk * tail + edge, tail)
+        run_ref[HEAD, rows, :] = held_ref[rows, :]
+        run_ref[TAIL, rows, :] = held_ref[pl.ds((modes + m) * blocks, blocks), :]
 
     def finish(kind, span, run):
         terms, factors = [], []
@@ -491,36 +475,96 @@
             run_ref[run, rows, :] = state * run_ref[FAR, rows, :]
             factors.append(run_ref[FACTOR, rows, :])
         for k in range(SPAN):
-            r = k if kind == 0 else SPAN - 1 - k
-            rows = pl.ds(pl.multiple_of((span * SPAN + r) * blocks, blocks), blocks)
+            rows = position(span, k if kind == 0 else SPAN - 1 - k, blocks)
             loc_ref[kind, rows, :] = loc_ref[kind, rows, :] + tree(terms)
             if k < SPAN - 1:
                 terms = [t * f for t, f in zip(terms, factors)]
+
+    def both(span, carry):
+        finish(0, span, HEAD)
+        finish(1, spans - 1 - span, TAIL)
+        return carry
+
+    for p in range(pieces):
+        wait_all(fetch[p])
+        lax.fori_loop(p * part, (p + 1) * part, both, 0)
+
+
+def out_body(
+    index_ref, par_ref, loc_ref, total_ref, other_ref, gate_hbm, key_hbm, value_hbm, cot_hbm,
+    mixed_hbm, ggate_hbm, gkey_hbm, gvalue_hbm, gskip_ref,
+    run_ref, sum_ref, in_ref, out_ref, in_sem, out_sem,
+    *, step,
+):
+    length, channels = gate_hbm.shape
+    blocks = channels // LANES
+    modes = par_ref.shape[0] // blocks // 2
+    spans = length // SPAN
+    pieces = in_sem.shape[0]
+    part = spans // pieces
+    depth = part * SPAN
+    fetch = [
+        start_all([
+            pltpu.make_async_copy(ref.at[pl.ds(p * depth, depth)], in_ref.at[k, pl.ds(p * depth, depth)], in_sem.at[p, k])
+            for k, ref in enumerate((gate_hbm, cot_hbm, value_hbm, key_hbm))
+        ])
+        for p in range(pieces)
+    ]
+    rest = pl.ds(modes * blocks, blocks)
+    gskip_ref[...] = total_ref[rest, :] + other_ref[rest, :]
+    FACTOR, FAR, STATE = range(3)
+    for m in range(modes):
+        rows = pl.ds(m * blocks, blocks)
+        rate = by_mode(par_ref, m, blocks)
+        _, _, near = join_weights(index_ref[0], step, rate, length)
+        factor = jnp.exp(-rate)
+        run_ref[FACTOR, rows, :] = factor
+        run_ref[FAR, rows, :] = jnp.exp(-float(SPAN) * rate)
+        weight = by_mode(par_ref, modes + m, blocks) * jnp.sqrt(rate) * factor
+        run_ref[STATE, rows, :] = weight * (near * other_ref[rows, :])
+    later = lax.rem(lax.div(index_ref[0], 2**step), 2) == 1
+    kind, other_kind = jnp.where(later, 0, 1), jnp.where(later, 1, 0)
+
+    def carry_in(span, carry):
+        place = jnp.where(later, span, spans - 1 - span)
+        terms, factors = [], []
+        for m in range(modes):
+            rows = pl.ds(m * blocks, blocks)
+            terms.append(run_ref[STATE, rows, :])
+            run_ref[STATE, rows, :] = terms[-1] * run_ref[FAR, rows, :]
+            factors.append(run_ref[FACTOR, rows, :])
+        for k in range(SPAN):
+            rows = position(place, jnp.where(later, k, SPAN - 1 - k), blocks)
+            sum_ref[kind, rows, :] = loc_ref[kind, rows, :] + tree(terms)
+            sum_ref[other_kind, rows, :] = loc_ref[other_kind, rows, :]
+            if k < SPAN - 1:
+                terms = [t * f for t, f in zip(terms, factors)]
+        return carry
+
+    def finish(span, carry):
         rows = pl.ds(pl.multiple_of(span * SPAN, SPAN), SPAN)
         for block in range(blocks):
             lanes = pl.ds(block * LANES, LANES)
-            total = jnp.concatenate(
-                [
-                    loc_ref[kind, pl.ds((span * SPAN + half * ROWS) * blocks + block, ROWS, stride=blocks), :]
-                    for half in range(SPAN // ROWS)
-                ],
-                axis=0,
-            )
-            for slot in (2 * kind, 2 * kind + 1):
-                value = in_ref[slot, rows, lanes].astype(jnp.float32) * total
-                out_ref[slot, rows, lanes] = value.astype(jnp.bfloat16)
-
-    def step(span, carry):
-        finish(0, span, HEAD)
-        finish(1, spans - 1 - span, TAIL)
+            for side in range(2):
+                total = jnp.concatenate(
+                    [
+                        sum_ref[side, pl.ds((span * SPAN + half * ROWS) * blocks + block, ROWS, stride=blocks), :]
+                        for half in range(SPAN // ROWS)
+                    ],
+                    axis=0,
+                )
+                for slot in (2 * side, 2 * side + 1):
+                    value = in_ref[slot, rows, lanes].astype(jnp.float32) * total
+                    out_ref[slot, rows, lanes] = value.astype(jnp.bfloat16)
         return carry
 
+    lax.fori_loop(0, spans, carry_in, 0)
     stores = []
     for p in range(pieces):
         wait_all(fetch[p])
-        lax.fori_loop(p * part, (p + 1) * part, step, 0)
+        lax.fori_loop(p * part, (p + 1) * part, finish, 0)
+        rows = pl.ds(p * depth, depth)
         for slot, ref in enumerate((mixed_hbm, ggate_hbm, gkey_hbm, gvalue_hbm)):
-            rows = pl.ds((p if slot < 2 else pieces - 1 - p) * depth, depth)
             stores += start_all([pltpu.make_async_copy(out_ref.at[slot, rows], ref.at[rows], out_sem.at[p, slot])])
     wait_all(stores)
 
@@ -569,49 +613,29 @@
     )([HBM] * 4, gate_in, key_in, value_in, cotangent)
 
     side = (groups, chips, *tile)
-    states, head_states, tail_states, own_s, send_s, edge = call(
+    total_at = ((2 * modes + 1) * blocks, LANES)
+    total, head_states, tail_states = call(
         state_body,
-        [((owners, groups + 1, *tile), f32, HBM), (heads_at, f32, HBM), (tails_at, f32, HBM)]
-        + [(side, f32, VMEM)] * 2
-        + [((modes * blocks, LANES), f32, VMEM)],
+        [(total_at, f32, VMEM), (heads_at, f32, HBM), (tails_at, f32, HBM)],
         16,
         (64 * size, 16 * size),
-        [sums, pltpu.VMEM((groups + 1, owners, *tile), f32), pltpu.VMEM(heads_at, f32), pltpu.VMEM(tails_at, f32)]
-        + [DMA((groups + 2,)), DMA((2, pieces))],
-    )([SMEM] + [VMEM] * 4, core, params, x, b, sk)
-    states = lax.all_to_all(states, ctx, 0, 0, tiled=True)
-
-    rates, side_rates, own_a, send_a, own_b, send_b = call(
-        slope_body,
-        [((groups, *tile), f32, VMEM)] + [(side, f32, VMEM)] * 5,
-        16,
-        (100 * size, 16 * size),
-        [pltpu.VMEM(heads_at, f32), pltpu.VMEM(tails_at, f32), pltpu.VMEM(heads_at, f32), pltpu.VMEM(heads_at, f32)]
-        + [pltpu.VMEM((7, modes * blocks, LANES), f32), sums, pltpu.VMEM((owners, *tile), f32), sums, DMA((2,))],
-    )([SMEM] * 2 + [VMEM] * 4 + [HBM] * 2, place, core, params, x, b, lag, head_states, tail_states)
-
-    (slopes,) = call(
-        functools.partial(pair_body, modes=modes, length=length),
-        [((chips, 3 * groups, *tile), f32, HBM)],
-        8,
-        (size, size),
-        [pltpu.VMEM((2, *side), f32), DMA((2, groups))],
-    )([SMEM] + [VMEM] * 7, core, own_a, change(send_a), own_b, change(send_b), own_s, change(send_s), side_rates)
-
-    bundle, heads, acc, sum_skip = call(
-        functools.partial(scan_body, modes=modes, length=length),
-        [
-            ((chips, 3 * groups, *tile), f32, HBM),
-            (side, f32, VMEM),
-            ((groups, *tile), f32, VMEM),
-            ((blocks, LANES), f32, VMEM),
-        ],
-        8,
-        (10**5, 10**6),
-        [DMA((groups,))],
-        {2: 0},
-    )([VMEM, VMEM, HBM], states, rates, slopes)
-    arrived = lax.all_to_all(bundle, "chip", 0, 0, tiled=True)
+        [pltpu.VMEM(heads_at, f32), pltpu.VMEM(tails_at, f32), DMA((2, pieces)), DMA],
+    )([VMEM] * 4, params, x, b, sk)
+
+    totals, held, others = [total], [], []
+    steps = (owners - 1).bit_length()
+    for step in range(steps):
+        others.append(lax.ppermute(totals[-1], ctx, [(i, i ^ 2**step) for i in range(owners)]))
+        if step == steps - 1:
+            break
+        last = step == steps - 2
+        total, *held = call(
+            functools.partial(join_body, step=step, length=length, modes=modes, last=last),
+            [(((modes + 1) * blocks, LANES) if last else total_at, f32, VMEM), ((2 * modes * blocks, LANES), f32, VMEM)],
+            8,
+            (size, size),
+        )([SMEM] + [VMEM] * (3 + len(held)), place, params, totals[-1], others[-1], *held)
+        totals.append(total)
 
     y, z = call(
         local_body,
@@ -619,29 +643,60 @@
         16,
         (40 * size, 16 * size),
         [pltpu.VMEM((blocks, LANES), f32), pltpu.VMEM((2, *signal), f32), DMA, DMA((2, pieces))],
-    )([VMEM] * 3 + [HBM], params, x, b, skip.reshape(blocks, LANES))
+    )([VMEM] * 4 + [HBM], params, x, b, totals[2], skip.reshape(blocks, LANES))
+
+    rates, side_rates, own_s, send_s, own_a, send_a, own_b, send_b = call(
+        slope_body,
+        [((groups, *tile), f32, VMEM)] + [(side, f32, VMEM)] * 7,
+        16,
+        (100 * size, 16 * size),
+        [pltpu.VMEM(heads_at, f32), pltpu.VMEM(tails_at, f32), pltpu.VMEM(heads_at, f32), pltpu.VMEM(heads_at, f32)]
+        + [pltpu.VMEM((7, modes * blocks, LANES), f32), sums, pltpu.VMEM((owners, *tile), f32), sums, DMA((2,))],
+    )(
+        [SMEM] * 2 + [VMEM] * 6 + [HBM] * 2,
+        place, core, params, x, b, lag, totals[0], totals[1], head_states, tail_states,
+    )
+
+    (states,) = call(
+        functools.partial(pair_body, modes=modes, length=length),
+        [((chips, 3 * groups, *tile), f32, HBM)],
+        8,
+        (size, size),
+        [pltpu.VMEM((3, *side), f32), DMA((3, groups))],
+    )(
+        [SMEM] + [VMEM] * 8,
+        core, own_a, change(send_a), own_b, change(send_b), own_s, change(send_s), side_rates, totals[2],
+    )
+    states = lax.all_to_all(states, "chip", 0, 0, tiled=True)
 
     packed = (owners, blocks, share * 2 * modes // LANES, LANES)
-    grads, ends = call(
-        functools.partial(slope_sum_body, modes=modes),
-        [(packed, f32, HBM), (side, f32, VMEM)],
+    (grads,) = call(
+        functools.partial(scan_body, modes=modes, length=cores * length),
+        [(packed, f32, HBM)],
         8,
         (10**5, 10**6),
         [pltpu.VMEM(packed[1:], f32), DMA((owners,))],
-    )([VMEM] * 4 + [HBM], arrived, heads, acc, rates, y)
+    )([VMEM] * 2 + [HBM], states, rates, y)
     grads = lax.all_to_all(grads.reshape(owners * blocks, *packed[2:]), ("chip", "core", "ch"), 0, 0, tiled=True)
 
+    (settled,) = call(
+        settle_body,
+        [((2, *signal), f32, VMEM)],
+        16,
+        (64 * size, 16 * size),
+        [pltpu.VMEM((5, modes * blocks, LANES), f32), pltpu.VMEM((2, *heads_at), f32), DMA((pieces, 4))],
+    )([VMEM] * 2 + [HBM] * 4, params, *held, y, z, head_states, tail_states)
+
     mixed, grad_gate, grad_key, grad_value, grad_skip = call(
-        out_body,
+        functools.partial(out_body, step=steps - 1),
         [(whole, bf16, HBM)] * 4 + [((blocks, LANES), f32, VMEM)],
-        24,
-        (64 * size, 32 * size),
-        [sums, pltpu.VMEM((5, modes * blocks, LANES), f32), pltpu.VMEM((2, *signal), f32)]
-        + [pltpu.VMEM((2, *heads_at), f32), dense, dense, pltpu.VMEM((owners, *tile), f32)]
-        + [DMA((pieces, 4)), DMA((pieces, 4)), DMA((pieces, 4))],
+        16,
+        (32 * size, 16 * size),
+        [pltpu.VMEM((3, modes * blocks, LANES), f32), pltpu.VMEM((2, *signal), f32), dense, dense]
+        + [DMA((pieces, 4)), DMA((pieces, 4))],
     )(
-        [SMEM] + [VMEM] * 5 + [HBM] * 8,
-        core, params, ends, change(ends), change(edge), sum_skip, y, z, head_states, tail_states, gate_in, key_in, value_in, cotangent,
+        [SMEM] + [VMEM] * 4 + [HBM] * 4,
+        place, params, settled, totals[3], others[3], gate_in, key_in, value_in, cotangent,
     )
 
     grad_residue, grad_log_decay = call(

time: 63.4 us -> 61.3 us (0.967)
  waiting for transfers between devices: 11.5 us -> 7.92 us
  Pallas kernels: 23.3 us -> 24.6 us
    ppermute x0 -> x4, starting transfers between devices: none -> 7.62 us  [on_device(): lax.ppermute(totals[-1], ctx, [(i, i ^ 2 ** step) for i in range(owners)])]
    all_to_all x2 -> x1, starting transfers between devices: 12.6 us -> 5.83 us  [on_device(): states = lax.all_to_all(states, 'chip', 0, 0, tiled=True)]
    all_to_all x2 -> x1, waiting for transfers between devices: 3.39 us -> 1.74 us  [on_device(): states = lax.all_to_all(states, 'chip', 0, 0, tiled=True)]
    ppermute x5 -> x3, waiting for transfers between devices: 2.31 us -> 0.8 us  [change(): lax.ppermute(value, 'core', [(i, cores - 1 - i) for i in range(cores)])]
    all_to_all x1, waiting for transfers between devices: 1.4 us -> 0.01 us  [on_device(): lax.all_to_all(grads.reshape(owners * blocks, *packed[2:]), ('chip', 'cor...]
    pallas_call x10 -> x13, Pallas kernels: 23.3 us -> 24.6 us  [call(): pl.pallas_call(body, out_shape=[pltpu.HBM(s, t) if w is HBM else jax.Shap...]
    ppermute x0 -> x4, waiting for transfers between devices: none -> 1 us  [on_device(): lax.ppermute(totals[-1], ctx, [(i, i ^ 2 ** step) for i in range(owners)])]
    ppermute x5 -> x3, starting transfers between devices: 1.94 us -> 1.23 us  [change(): lax.ppermute(value, 'core', [(i, cores - 1 - i) for i in range(cores)])]
  transfers between devices with their start and end apart: 9 -> 10, of which waited for: 8 -> 6; matrix products, arithmetic and copies ran while one was open for 0% -> 0% of each run, Pallas kernels for 26% -> 30%
where the time goes in v7:
time: 61.3 us; the launch traced here: 60.9 us
  starting transfers between devices  27.6 us (45%)
  Pallas kernels  24.6 us (40%)
  waiting for transfers between devices  7.92 us (13%)
  between operations  0.79 us (1%)
    pallas_call x13, Pallas kernels, call(): pl.pallas_call(body, out_shape=[pltpu.HBM(s, t) if w is HBM else jax.Shap...  24.6 us
    ppermute x4, starting transfers between devices, on_device(): lax.ppermute(totals[-1], ctx, [(i, i ^ 2 ** step) for i in range(owners)])  7.62 us
    all_to_all x1, starting transfers between devices, on_device(): lax.all_to_all(sent, 'ch', 0, 0, tiled=True)  7.49 us
    all_to_all x1, starting transfers between devices, on_device(): states = lax.all_to_all(states, 'chip', 0, 0, tiled=True)  5.83 us
    all_to_all x1, starting transfers between devices, on_device(): lax.all_to_all(grads.reshape(owners * blocks, *packed[2:]), ('chip', 'cor...  5.42 us
    all_to_all x1, waiting for transfers between devices, on_device(): lax.all_to_all(sent, 'ch', 0, 0, tiled=True)  4.37 us
    all_to_all x1, waiting for transfers between devices, on_device(): states = lax.all_to_all(states, 'chip', 0, 0, tiled=True)  1.74 us
    ppermute x3, starting transfers between devices, change(): lax.ppermute(value, 'core', [(i, cores - 1 - i) for i in range(cores)])  1.23 us
  transfers between devices with their start and end apart: 10, of which 6 were waited for; matrix products, arithmetic and copies ran while one was open for 0% of the time, Pallas kernels for 30%

profile of v7, /device:TPU:1, one launch (start us, length us, event | category | flops | bytes accessed | tf_op | source)
XLA Modules:
  0.0 60.9 jit_solution(4117210677345000311)
XLA Ops:
  0.6 1.4 %shard_map.126 = f32[8,32,128]{2,1,0:T(8,128)} custom-call(f32[16,128]{1,0:T(8,128)} %bitcast.20, f32[16,128]{1,0:T(8,128)} %bitcast.22), custom_call_target="tpu_custom_call" | custom-call | bytes 100000 | tf_op jit(solution)/shard_map/pallas_call | solution.py:21
  2.1 7.5 %all-to-all-start = ((f32[8,32,128]{2,1,0:T(8,128)}), f32[8,32,128]{2,1,0:T(8,128)S(1)}, u32[]{:S(2)}, u32[]{:S(2)}) async-start(f32[8,32,128]{2,1,0:T(8,128)} %shard_map.126), calls=%async_computation | async-start | bytes 262144 | tf_op jit(solution)/shard_map/all_to_all | solution.py:605
  9.6 2.4 %shard_map.127 = (f32[2048,128]{1,0:T(8,128)S(1)}, f32[2048,128]{1,0:T(8,128)S(1)}, f32[8,128]{1,0:T(8,128)S(1)}, f32[128,128]{1,0:T(8,128)S(1)}) custom-call(bf16[256,1024]{1,0:T(8,128)(2,1)} %gate_hbm.3, bf16[256,1024]{1,0:T(8,128)(2,1)} %key_hbm.3, bf16[256,1024]{1,0:T(8,128)(2,1)} %value_hbm.3, bf16[256,1024]{1,0:T(8,128)(2,1)} %cot_hbm.3), custom_call_target="tpu_custom_call" | custom-call | flops 2097152 | bytes 4194304 | tf_op jit(solution)/shard_map/pallas_call | solution.py:21
  12.0 4.4 %all-to-all-done = f32[8,32,128]{2,1,0:T(8,128)S(1)} async-done(((f32[8,32,128]{2,1,0:T(8,128)}), f32[8,32,128]{2,1,0:T(8,128)S(1)}, u32[]{:S(2)}, u32[]{:S(2)}) %all-to-all-start) | async-done | bytes 131104 | tf_op jit(solution)/shard_map/all_to_all | solution.py:605
  16.3 3.3 %shard_map.128 = (f32[264,128]{1,0:T(8,128)S(1)}, f32[16,128,128]{2,1,0:T(8,128)}, f32[17,128,128]{2,1,0:T(8,128)}) custom-call(f32[256,128]{1,0:T(8,128)S(1)} %bitcast.11, f32[2048,128]{1,0:T(8,128)S(1)} %get-tuple-element.37.x_ref, f32[2048,128]{1,0:T(8,128)S(1)} %get-tuple-element.38.b_ref, f32[8,128]{1,0:T(8,128)S(1)} %get-tuple-element.39.sk_ref), custom_call_target="tpu_custom_call" | custom-call | flops 16777216 | bytes 4194304 | tf_op jit(solution)/shard_map/pallas_call | solution.py:21
  19.6 2.2 %collective-permute-start = (f32[264,128]{1,0:T(8,128)S(1)}, f32[264,128]{1,0:T(8,128)S(1)}, u32[]{:S(2)}, u32[]{:S(2)}) collective-permute-start(f32[264,128]{1,0:T(8,128)S(1)} %get-tuple-element.40.total_ref), channel_id=1, source_target_pairs={{0,8},{8,0},{16,24},{24,16},{32,40},{40,32},{48,56},{56,48},{64,72... | collective-permute-start | bytes 405512 | tf_op jit(solution)/shard_map/ppermute | solution.py:628
  21.8 1.0 %collective-permute-done.other_ref = f32[264,128]{1,0:T(8,128)S(1)} collective-permute-done((f32[264,128]{1,0:T(8,128)S(1)}, f32[264,128]{1,0:T(8,128)S(1)}, u32[]{:S(2)}, u32[]{:S(2)}) %collective-permute-start) | collective-permute-done | bytes 135200 | tf_op jit(solution)/shard_map/ppermute | solution.py:628
  22.9 0.5 collective-permute-start.1
  23.3 4.2 %shard_map.135 = (f32[2,8,128]{2,1,0:T(8,128)S(1)}, f32[2,8,8,128]{3,2,1,0:T(8,128)S(1)}, f32[2,8,8,128]{3,2,1,0:T(8,128)S(1)}, f32[2,8,8,128]{3,2,1,0:T(8,128)S...) custom-call(s32[1]{0:T(128)} %bitcast.index_ref, ...), custom_call_target="tpu_custom_call" | custom-call | flops 26214400 | bytes 4194304 | tf_op jit(solution)/shard_map/pallas_call | solution.py:21
  27.5 0.7 %collective-permute-start.4 = (f32[2,8,8,128]{3,2,1,0:T(8,128)S(1)}, f32[2,8,8,128]{3,2,1,0:T(8,128)S(1)}, u32[]{:S(2)}, u32[]{:S(2)}) collective-permute-start(f32[2,8,8,128]{3,2,1,0:T(8,128)S(1)} %get-tuple-element.58), channel_id=1, source_target_pairs={{0,8},{8,0},{1,9},{9,1},{2,10},{10,2},{3,11},{11,3},{4,12},{12,4},... | collective-permute-start | bytes 196616 | tf_op jit(solution)/shard_map/ppermute | solution.py:588
  28.3 0.4 collective-permute-start.6
  28.8 0.3 collective-permute-done.4.a_other_ref
  29.1 0.4 collective-permute-done.5.b_other_ref
  29.6 0.9 %shard_map.136 = f32[8,6,8,128]{3,2,1,0:T(8,128)} custom-call(s32[1]{0:T(128)} %bitcast.6.core_ref, f32[2,8,8,128]{3,2,1,0:T(8,128)S(1)} %get-tuple-element.57.a_ref, f32[2,8,8,128]{3,2,1,0:T(8,128)S(1)} %collective-permute-done.4.a_other_ref, f32[2,8,8,128]{3,2,1,0:T(8,128)S(1)} %get-tuple-element.59.b_ref, ...), custom_call_target="tpu_custom_call" | custom-call | flops 262144 | bytes 262144 | tf_op jit(solution)/shard_map/pallas_call | solution.py:21
  30.5 5.8 %all-to-all-start.1 = ((f32[8,6,8,128]{3,2,1,0:T(8,128)}), f32[8,6,8,128]{3,2,1,0:T(8,128)S(1)}, u32[]{:S(2)}, u32[]{:S(2)}) async-start(f32[8,6,8,128]{3,2,1,0:T(8,128)} %shard_map.136), calls=%async_computation.1 | async-start | bytes 393216 | tf_op jit(solution)/shard_map/all_to_all | solution.py:670
  36.4 1.5 %collective-permute-start.2 = (f32[264,128]{1,0:T(8,128)S(1)}, f32[264,128]{1,0:T(8,128)S(1)}, u32[]{:S(2)}, u32[]{:S(2)}) collective-permute-start(f32[264,128]{1,0:T(8,128)S(1)} %get-tuple-element.43.total_ref.joined_ref), channel_id=1, source_target_pairs={{0,32},{8,40},{16,48},{24,56},{32,0},{40,8},{48,16},{56,24},{64,96... | collective-permute-start | bytes 405512 | tf_op jit(solution)/shard_map/ppermute | solution.py:628
  37.8 2.7 %shard_map.132 = (f32[2048,128]{1,0:T(8,128)}, f32[2048,128]{1,0:T(8,128)}) custom-call(f32[256,128]{1,0:T(8,128)S(1)} %bitcast.15, f32[2048,128]{1,0:T(8,128)S(1)} %get-tuple-element.37.x_ref, f32[2048,128]{1,0:T(8,128)S(1)} %get-tuple-element.38.b_ref, f32[264,128]{1,0:T(8,128)S(1)} %get-tuple-element.43.total_ref.joined_ref, f32[8,128]{1,0:T(8,128)} %bitcast.25), custom_call_target="tpu_custom_call" | custom-call | flops 10485760 | bytes 4194304 | tf_op jit(solution)/shard_map/pallas_call | solution.py:21
  40.5 1.7 %all-to-all-done.1.s_ref = f32[8,6,8,128]{3,2,1,0:T(8,128)S(1)} async-done(((f32[8,6,8,128]{3,2,1,0:T(8,128)}), f32[8,6,8,128]{3,2,1,0:T(8,128)S(1)}, u32[]{:S(2)}, u32[]{:S(2)}) %all-to-all-start.1) | async-done | bytes 196640 | tf_op jit(solution)/shard_map/all_to_all | solution.py:670
  42.3 1.0 %shard_map.137 = f32[16,8,2,128]{3,2,1,0:T(2,128)} custom-call(f32[8,6,8,128]{3,2,1,0:T(8,128)S(1)} %all-to-all-done.1.s_ref, f32[2,8,128]{2,1,0:T(8,128)S(1)} %get-tuple-element.64.rate_ref, f32[2048,128]{1,0:T(8,128)} %get-tuple-element.46.y_hbm.done_hbm), custom_call_target="tpu_custom_call" | custom-call | flops 100000 | bytes 1000000 | tf_op jit(solution)/shard_map/pallas_call | solution.py:21
  43.3 5.4 %all-to-all-start.2 = ((f32[128,2,128]{2,1,0:T(2,128)}), f32[128,2,128]{2,1,0:T(2,128)S(1)}, u32[]{:S(2)}, u32[]{:S(2)}) async-start(f32[128,2,128]{2,1,0:T(2,128)} %bitcast.24), calls=%async_computation.2 | async-start | bytes 262144 | tf_op jit(solution)/shard_map/all_to_all | solution.py:680
  48.9 3.5 %collective-permute-start.3 = (f32[136,128]{1,0:T(8,128)S(1)}, f32[136,128]{1,0:T(8,128)S(1)}, u32[]{:S(2)}, u32[]{:S(2)}) collective-permute-start(f32[136,128]{1,0:T(8,128)S(1)} %get-tuple-element.50.total_ref), channel_id=1, source_target_pairs={{0,64},{8,72},{16,80},{24,88},{32,96},{40,104},{48,112},{56,120},{... | collective-permute-start | bytes 208904 | tf_op jit(solution)/shard_map/ppermute | solution.py:628
  52.4 3.8 %shard_map.133.loc_ref = f32[2,2048,128]{2,1,0:T(8,128)S(1)} custom-call(f32[256,128]{1,0:T(8,128)S(1)} %bitcast.17, f32[256,128]{1,0:T(8,128)S(1)} %get-tuple-element.45.held_ref, f32[2048,128]{1,0:T(8,128)} %get-tuple-element.46.y_hbm.done_hbm, f32[2048,128]{1,0:T(8,128)} %get-tuple-element.47.z_hbm, f32[16,128,128]{2,1,0:T(8,128)} %get-tuple-element.48.hs_hbm, ...), custom_call_target="tpu_custom_call" | custom-call | flops 16777216 | bytes 4194304 | tf_op jit(solution)/shard_map/pallas_call | solution.py:21
  56.2 3.9 %shard_map.134 = (bf16[256,1024]{1,0:T(8,128)(2,1)}, bf16[256,1024]{1,0:T(8,128)(2,1)}, bf16[256,1024]{1,0:T(8,128)(2,1)}, bf16[256,1024]{1,0:T(8,128)(2,1)}, f32[8,128]{1,0:T(8,128)}) custom-call(s32[1]{0:T(128)} %bitcast.index_ref, f32[256,128]{1,0:T(8,128)S(1)} %bitcast.18, f32[2,2048,128]{2,1,0:T(8,128)S(1)} %shard_map.133.loc_ref, ...), custom_call_target="tpu_custom_call" | custom-call | flops 8388608 | bytes 4194304 | tf_op jit(solution)/shard_map/pallas_call | solution.py:21
  60.1 0.8 %shard_map.138 = (f32[16,128]{1,0:T(8,128)}, f32[16,128]{1,0:T(8,128)}) custom-call(f32[16,8,2,128]{3,2,1,0:T(2,128)S(1)} %bitcast.19, f32[16,128]{1,0:T(8,128)S(1)} %bitcast.23, f32[16,128]{1,0:T(8,128)S(1)} %bitcast.21), custom_call_target="tpu_custom_call" | custom-call | flops 100000 | bytes 1000000 | tf_op jit(solution)/shard_map/pallas_call | solution.py:21
  (13 shorter events, 0.5 us)
Async XLA Ops:
  2.1 14.3 %all-to-all-start = ((f32[8,32,128]{2,1,0:T(8,128)}), f32[8,32,128]{2,1,0:T(8,128)S(1)}, u32[]{:S(2)}, u32[]{:S(2)}) async-start(f32[8,32,128]{2,1,0:T(8,128)} %shard_map.126), calls=%async_computation | async-start | bytes 262144 | tf_op jit(solution)/shard_map/all_to_all | solution.py:605
  19.6 3.2 %collective-permute-start = (f32[264,128]{1,0:T(8,128)S(1)}, f32[264,128]{1,0:T(8,128)S(1)}, u32[]{:S(2)}, u32[]{:S(2)}) collective-permute-start(f32[264,128]{1,0:T(8,128)S(1)} %get-tuple-element.40.total_ref), channel_id=1, source_target_pairs={{0,8},{8,0},{16,24},{24,16},{32,40},{40,32},{48,56},{56,48},{64,72... | collective-permute-start | bytes 405512 | tf_op jit(solution)/shard_map/ppermute | solution.py:628
  22.9 5.9 %collective-permute-start.1 = (f32[264,128]{1,0:T(8,128)S(1)}, f32[264,128]{1,0:T(8,128)S(1)}, u32[]{:S(2)}, u32[]{:S(2)}) collective-permute-start(f32[264,128]{1,0:T(8,128)S(1)} %get-tuple-element.41.total_ref.joined_ref), channel_id=1, source_target_pairs={{0,16},{8,24},{16,0},{24,8},{32,48},{40,56},{48,32},{56,40},{64,80... | collective-permute-start | bytes 405512 | tf_op jit(solution)/shard_map/ppermute | solution.py:628
  27.5 1.6 %collective-permute-start.4 = (f32[2,8,8,128]{3,2,1,0:T(8,128)S(1)}, f32[2,8,8,128]{3,2,1,0:T(8,128)S(1)}, u32[]{:S(2)}, u32[]{:S(2)}) collective-permute-start(f32[2,8,8,128]{3,2,1,0:T(8,128)S(1)} %get-tuple-element.58), channel_id=1, source_target_pairs={{0,8},{8,0},{1,9},{9,1},{2,10},{10,2},{3,11},{11,3},{4,12},{12,4},... | collective-permute-start | bytes 196616 | tf_op jit(solution)/shard_map/ppermute | solution.py:588
  28.2 1.3 %collective-permute-start.5 = (f32[2,8,8,128]{3,2,1,0:T(8,128)S(1)}, f32[2,8,8,128]{3,2,1,0:T(8,128)S(1)}, u32[]{:S(2)}, u32[]{:S(2)}) collective-permute-start(f32[2,8,8,128]{3,2,1,0:T(8,128)S(1)} %get-tuple-element.60), channel_id=1, source_target_pairs={{0,8},{8,0},{1,9},{9,1},{2,10},{10,2},{3,11},{11,3},{4,12},{12,4},... | collective-permute-start | bytes 196616 | tf_op jit(solution)/shard_map/ppermute | solution.py:588
  28.3 1.3 %collective-permute-start.6 = (f32[2,8,8,128]{3,2,1,0:T(8,128)S(1)}, f32[2,8,8,128]{3,2,1,0:T(8,128)S(1)}, u32[]{:S(2)}, u32[]{:S(2)}) collective-permute-start(f32[2,8,8,128]{3,2,1,0:T(8,128)S(1)} %get-tuple-element.62), channel_id=1, source_target_pairs={{0,8},{8,0},{1,9},{9,1},{2,10},{10,2},{3,11},{11,3},{4,12},{12,4},... | collective-permute-start | bytes 196616 | tf_op jit(solution)/shard_map/ppermute | solution.py:588
  30.5 11.7 %all-to-all-start.1 = ((f32[8,6,8,128]{3,2,1,0:T(8,128)}), f32[8,6,8,128]{3,2,1,0:T(8,128)S(1)}, u32[]{:S(2)}, u32[]{:S(2)}) async-start(f32[8,6,8,128]{3,2,1,0:T(8,128)} %shard_map.136), calls=%async_computation.1 | async-start | bytes 393216 | tf_op jit(solution)/shard_map/all_to_all | solution.py:670
  36.4 12.4 %collective-permute-start.2 = (f32[264,128]{1,0:T(8,128)S(1)}, f32[264,128]{1,0:T(8,128)S(1)}, u32[]{:S(2)}, u32[]{:S(2)}) collective-permute-start(f32[264,128]{1,0:T(8,128)S(1)} %get-tuple-element.43.total_ref.joined_ref), channel_id=1, source_target_pairs={{0,32},{8,40},{16,48},{24,56},{32,0},{40,8},{48,16},{56,24},{64,96... | collective-permute-start | bytes 405512 | tf_op jit(solution)/shard_map/ppermute | solution.py:628
  43.3 16.8 %all-to-all-start.2 = ((f32[128,2,128]{2,1,0:T(2,128)}), f32[128,2,128]{2,1,0:T(2,128)S(1)}, u32[]{:S(2)}, u32[]{:S(2)}) async-start(f32[128,2,128]{2,1,0:T(2,128)} %bitcast.24), calls=%async_computation.2 | async-start | bytes 262144 | tf_op jit(solution)/shard_map/all_to_all | solution.py:680
  48.9 7.3 %collective-permute-start.3 = (f32[136,128]{1,0:T(8,128)S(1)}, f32[136,128]{1,0:T(8,128)S(1)}, u32[]{:S(2)}, u32[]{:S(2)}) collective-permute-start(f32[136,128]{1,0:T(8,128)S(1)} %get-tuple-element.50.total_ref), channel_id=1, source_target_pairs={{0,64},{8,72},{16,80},{24,88},{32,96},{40,104},{48,112},{56,120},{... | collective-permute-start | bytes 208904 | tf_op jit(solution)/shard_map/ppermute | solution.py:628
  56.1 4.0 %copy-start = (f32[128,16]{0,1:T(8,128)S(1)}, f32[128,16]{0,1:T(8,128)}, u32[]{:S(2)}) copy-start(f32[128,16]{0,1:T(8,128)} %param.13) | copy-start | bytes 24580
  56.1 4.0 %copy-start.1 = (f32[128,16]{0,1:T(8,128)S(1)}, f32[128,16]{0,1:T(8,128)}, u32[]{:S(2)}) copy-start(f32[128,16]{0,1:T(8,128)} %param.12) | copy-start | bytes 24580

commit v8 on v7

--- a/solution.py
+++ b/solution.py
@@ -127,20 +127,21 @@
         send_ref[chip] = turned_ref[2 * chip + 1 - core]
 
 
-def state_body(par_ref, x_ref, b_ref, sk_ref, total_ref, hs_hbm, bs_hbm, hs_ref, bs_ref, sem, last_sem):
+def state_body(par_ref, x_ref, b_ref, sk_ref, total_ref, hs_hbm, bs_hbm, hs_last_ref, bs_last_ref, hs_ref, bs_ref, sem):
     spans = hs_ref.shape[0]
     blocks = sk_ref.shape[0]
     modes = par_ref.shape[0] // blocks // 2
-    pieces = sem.shape[1]
-    part = spans // pieces
+    part = hs_last_ref.shape[0]
+    pieces = spans // part
     factor = [jnp.exp(-by_mode(par_ref, m, blocks)) for m in range(modes)]
 
-    def step(span, carry):
+    def step(span, carry, last):
         ups, downs = carry
         mirror = spans - 1 - span
+        heads, tails, first = (hs_last_ref, bs_last_ref, spans - part) if last else (hs_ref, bs_ref, 0)
         for m in range(modes):
-            hs_ref[span, pl.ds(m * blocks, blocks), :] = ups[m]
-            bs_ref[mirror + 1, pl.ds(m * blocks, blocks), :] = downs[m]
+            heads[span - first, pl.ds(m * blocks, blocks), :] = ups[m]
+            tails[mirror + 1, pl.ds(m * blocks, blocks), :] = downs[m]
         for r in range(SPAN):
             x = x_ref[position(span, r, blocks), :]
             b = b_ref[position(mirror, SPAN - 1 - r, blocks), :]
@@ -152,24 +153,26 @@
     ups, downs = zero, zero
     copies = []
     for p in range(pieces):
-        ups, downs = lax.fori_loop(p * part, (p + 1) * part, step, (ups, downs))
+        last = p == pieces - 1
+        ups, downs = lax.fori_loop(p * part, (p + 1) * part, functools.partial(step, last=last), (ups, downs))
+        if last:
+            break
         here, there = pl.ds(p * part, part), pl.ds((pieces - 1 - p) * part + 1, part)
         copies += start_all([
             pltpu.make_async_copy(hs_ref.at[here], hs_hbm.at[here], sem.at[0, p]),
             pltpu.make_async_copy(bs_ref.at[there], bs_hbm.at[there], sem.at[1, p]),
         ])
     for m in range(modes):
-        bs_ref[0, pl.ds(m * blocks, blocks), :] = downs[m]
+        bs_last_ref[0, pl.ds(m * blocks, blocks), :] = downs[m]
         total_ref[pl.ds(m * blocks, blocks), :] = ups[m]
         total_ref[pl.ds((modes + m) * blocks, blocks), :] = downs[m]
     total_ref[pl.ds(2 * modes * blocks, blocks), :] = sk_ref[...]
-    copies += start_all([pltpu.make_async_copy(bs_ref.at[0], bs_hbm.at[0], last_sem)])
     wait_all(copies)
 
 
 def slope_body(
-    index_ref, core_ref, par_ref, x_ref, b_ref, lag_ref, total_ref, joined_ref, hs_hbm, bs_hbm,
-    rate_ref, side_rate_ref, keep_s_ref, send_s_ref, keep_a_ref, send_a_ref, keep_b_ref, send_b_ref,
+    index_ref, core_ref, par_ref, x_ref, b_ref, lag_ref, total_ref, joined_ref, hs_in, bs_in, hs_last_ref, bs_last_ref,
+    hs_hbm, bs_hbm, rate_ref, side_rate_ref, keep_s_ref, send_s_ref, keep_a_ref, send_a_ref, keep_b_ref, send_b_ref,
     hs_ref, bs_ref, up_ref, down_ref, run_ref, sums_ref, turn_ref, rates_ref, snap_sem,
 ):
     owners = turn_ref.shape[0]
@@ -177,10 +180,19 @@
     spans = hs_ref.shape[0]
     blocks = lag_ref.shape[0] // SPAN
     modes = par_ref.shape[0] // blocks // 2
+    part_spans = hs_last_ref.shape[0]
+    rest = spans - part_spans
+    heads, tails = pl.ds(0, rest), pl.ds(part_spans + 1, rest)
     fetch = start_all([
-        pltpu.make_async_copy(hs_hbm, hs_ref, snap_sem.at[0]),
-        pltpu.make_async_copy(bs_hbm, bs_ref, snap_sem.at[1]),
+        pltpu.make_async_copy(hs_in.at[heads], hs_ref.at[heads], snap_sem.at[0]),
+        pltpu.make_async_copy(bs_in.at[tails], bs_ref.at[tails], snap_sem.at[1]),
     ])
+    stores = start_all([
+        pltpu.make_async_copy(hs_last_ref, hs_hbm.at[pl.ds(rest, part_spans)], snap_sem.at[2]),
+        pltpu.make_async_copy(bs_last_ref, bs_hbm.at[pl.ds(0, part_spans + 1)], snap_sem.at[3]),
+    ])
+    hs_ref[rest:] = hs_last_ref[...]
+    bs_ref[: part_spans + 1] = bs_last_ref[...]
     share = rate_ref.shape[1]
     zero = jnp.zeros((blocks, LANES), jnp.float32)
     SLOPE, SUM0, SUM1, DOWN, POWER, FACTOR, FAR = range(7)
@@ -264,6 +276,7 @@
         keep_b_ref,
         send_b_ref,
     )
+    wait_all(stores)
 
 
 def pair_body(
@@ -614,12 +627,14 @@
 
     side = (groups, chips, *tile)
     total_at = ((2 * modes + 1) * blocks, LANES)
-    total, head_states, tail_states = call(
+    part = spans // pieces
+    total, head_states, tail_states, last_heads, last_tails = call(
         state_body,
-        [(total_at, f32, VMEM), (heads_at, f32, HBM), (tails_at, f32, HBM)],
+        [(total_at, f32, VMEM), (heads_at, f32, HBM), (tails_at, f32, HBM)]
+        + [((part, *heads_at[1:]), f32, VMEM), ((part + 1, *heads_at[1:]), f32, VMEM)],
         16,
         (64 * size, 16 * size),
-        [pltpu.VMEM(heads_at, f32), pltpu.VMEM(tails_at, f32), DMA((2, pieces)), DMA],
+        [pltpu.VMEM(heads_at, f32), pltpu.VMEM(tails_at, f32), DMA((2, pieces))],
     )([VMEM] * 4, params, x, b, sk)
 
     totals, held, others = [total], [], []
@@ -645,16 +660,17 @@
         [pltpu.VMEM((blocks, LANES), f32), pltpu.VMEM((2, *signal), f32), DMA, DMA((2, pieces))],
     )([VMEM] * 4 + [HBM], params, x, b, totals[2], skip.reshape(blocks, LANES))
 
-    rates, side_rates, own_s, send_s, own_a, send_a, own_b, send_b = call(
+    head_states, tail_states, rates, side_rates, own_s, send_s, own_a, send_a, own_b, send_b = call(
         slope_body,
-        [((groups, *tile), f32, VMEM)] + [(side, f32, VMEM)] * 7,
+        [(heads_at, f32, HBM), (tails_at, f32, HBM), ((groups, *tile), f32, VMEM)] + [(side, f32, VMEM)] * 7,
         16,
         (100 * size, 16 * size),
         [pltpu.VMEM(heads_at, f32), pltpu.VMEM(tails_at, f32), pltpu.VMEM(heads_at, f32), pltpu.VMEM(heads_at, f32)]
-        + [pltpu.VMEM((7, modes * blocks, LANES), f32), sums, pltpu.VMEM((owners, *tile), f32), sums, DMA((2,))],
+        + [pltpu.VMEM((7, modes * blocks, LANES), f32), sums, pltpu.VMEM((owners, *tile), f32), sums, DMA((4,))],
+        {8: 0, 9: 1},
     )(
-        [SMEM] * 2 + [VMEM] * 6 + [HBM] * 2,
-        place, core, params, x, b, lag, totals[0], totals[1], head_states, tail_states,
+        [SMEM] * 2 + [VMEM] * 6 + [HBM] * 2 + [VMEM] * 2,
+        place, core, params, x, b, lag, totals[0], totals[1], head_states, tail_states, last_heads, last_tails,
     )
 
     (states,) = call(

time: 61.3 us -> 60.7 us (level)
  no operation moved by 1% of the time
where the time goes in v8:
time: 60.7 us; the launch traced here: 60.3 us
  starting transfers between devices  27.6 us (45%)
  Pallas kernels  24 us (40%)
  waiting for transfers between devices  7.92 us (13%)
  between operations  0.79 us (1%)
    pallas_call x13, Pallas kernels, call(): pl.pallas_call(body, out_shape=[pltpu.HBM(s, t) if w is HBM else jax.Shap...  24 us
    ppermute x4, starting transfers between devices, on_device(): lax.ppermute(totals[-1], ctx, [(i, i ^ 2 ** step) for i in range(owners)])  7.62 us
    all_to_all x1, starting transfers between devices, on_device(): lax.all_to_all(sent, 'ch', 0, 0, tiled=True)  7.49 us
    all_to_all x1, starting transfers between devices, on_device(): states = lax.all_to_all(states, 'chip', 0, 0, tiled=True)  5.83 us
    all_to_all x1, starting transfers between devices, on_device(): lax.all_to_all(grads.reshape(owners * blocks, *packed[2:]), ('chip', 'cor...  5.42 us
    all_to_all x1, waiting for transfers between devices, on_device(): lax.all_to_all(sent, 'ch', 0, 0, tiled=True)  4.37 us
    all_to_all x1, waiting for transfers between devices, on_device(): states = lax.all_to_all(states, 'chip', 0, 0, tiled=True)  1.74 us
    ppermute x3, starting transfers between devices, change(): lax.ppermute(value, 'core', [(i, cores - 1 - i) for i in range(cores)])  1.23 us
  transfers between devices with their start and end apart: 10, of which 6 were waited for; matrix products, arithmetic and copies ran while one was open for 0% of the time, Pallas kernels for 30%

profile of v8, /device:TPU:1, one launch (start us, length us, event | category | flops | bytes accessed | tf_op | source)
XLA Modules:
  0.0 60.3 jit_solution(12542497126580310966)
XLA Ops:
  0.6 1.4 %shard_map.126 = f32[8,32,128]{2,1,0:T(8,128)} custom-call(f32[16,128]{1,0:T(8,128)} %bitcast.20, f32[16,128]{1,0:T(8,128)} %bitcast.22), custom_call_target="tpu_custom_call" | custom-call | bytes 100000 | tf_op jit(solution)/shard_map/pallas_call | solution.py:21
  2.1 7.5 %all-to-all-start = ((f32[8,32,128]{2,1,0:T(8,128)}), f32[8,32,128]{2,1,0:T(8,128)S(1)}, u32[]{:S(2)}, u32[]{:S(2)}) async-start(f32[8,32,128]{2,1,0:T(8,128)} %shard_map.126), calls=%async_computation | async-start | bytes 262144 | tf_op jit(solution)/shard_map/all_to_all | solution.py:618
  9.6 2.4 %shard_map.127 = (f32[2048,128]{1,0:T(8,128)S(1)}, f32[2048,128]{1,0:T(8,128)S(1)}, f32[8,128]{1,0:T(8,128)S(1)}, f32[128,128]{1,0:T(8,128)S(1)}) custom-call(bf16[256,1024]{1,0:T(8,128)(2,1)} %gate_hbm.3, bf16[256,1024]{1,0:T(8,128)(2,1)} %key_hbm.3, bf16[256,1024]{1,0:T(8,128)(2,1)} %value_hbm.3, bf16[256,1024]{1,0:T(8,128)(2,1)} %cot_hbm.3), custom_call_target="tpu_custom_call" | custom-call | flops 2097152 | bytes 4194304 | tf_op jit(solution)/shard_map/pallas_call | solution.py:21
  12.0 4.4 %all-to-all-done = f32[8,32,128]{2,1,0:T(8,128)S(1)} async-done(((f32[8,32,128]{2,1,0:T(8,128)}), f32[8,32,128]{2,1,0:T(8,128)S(1)}, u32[]{:S(2)}, u32[]{:S(2)}) %all-to-all-start) | async-done | bytes 131104 | tf_op jit(solution)/shard_map/all_to_all | solution.py:618
  16.3 2.6 %shard_map.128 = (f32[264,128]{1,0:T(8,128)S(1)}, f32[16,128,128]{2,1,0:T(8,128)}, f32[17,128,128]{2,1,0:T(8,128)}, f32[4,128,128]{2,1,0:T(8,128)S(1)}, f32[5,128,128]{2,1,0:T(8,128)S(1)}) custom-call(f32[256,128]{1,0:T(8,128)S(1)} %bitcast.11, f32[2048,128]{1,0:T(8,128)S(1)} %get-tuple-element.41.x_ref, f32[2048,128]{1,0:T(8,128)S(1)} %get-tuple-element.42.b_ref, ...), custom_call_target="tpu_custom_call" | custom-call | flops 16777216 | bytes 4194304 | tf_op jit(solution)/shard_map/pallas_call | solution.py:21
  19.0 2.2 %collective-permute-start = (f32[264,128]{1,0:T(8,128)S(1)}, f32[264,128]{1,0:T(8,128)S(1)}, u32[]{:S(2)}, u32[]{:S(2)}) collective-permute-start(f32[264,128]{1,0:T(8,128)S(1)} %get-tuple-element.44.total_ref), channel_id=1, source_target_pairs={{0,8},{8,0},{16,24},{24,16},{32,40},{40,32},{48,56},{56,48},{64,72... | collective-permute-start | bytes 405512 | tf_op jit(solution)/shard_map/ppermute | solution.py:643
  21.2 1.0 %collective-permute-done.other_ref = f32[264,128]{1,0:T(8,128)S(1)} collective-permute-done((f32[264,128]{1,0:T(8,128)S(1)}, f32[264,128]{1,0:T(8,128)S(1)}, u32[]{:S(2)}, u32[]{:S(2)}) %collective-permute-start) | collective-permute-done | bytes 135200 | tf_op jit(solution)/shard_map/ppermute | solution.py:643
  22.2 0.5 collective-permute-start.1
  22.7 4.2 %shard_map.133 = (f32[16,128,128]{2,1,0:T(8,128)}, f32[17,128,128]{2,1,0:T(8,128)}, f32[2,8,128]{2,1,0:T(8,128)S(1)}, f32[2,8,8,128]{3,2,1,0:T(8,128)S(1)}, f32[...) custom-call(s32[1]{0:T(128)} %bitcast.index_ref, ...), custom_call_target="tpu_custom_call", output_to_operand_aliasing={{0}: (8, {}), {1}: (9, {})} | custom-call | flops 26214400 | bytes 4194304 | tf_op jit(solution)/shard_map/pallas_call | solution.py:21
  26.9 0.7 %collective-permute-start.4 = (f32[2,8,8,128]{3,2,1,0:T(8,128)S(1)}, f32[2,8,8,128]{3,2,1,0:T(8,128)S(1)}, u32[]{:S(2)}, u32[]{:S(2)}) collective-permute-start(f32[2,8,8,128]{3,2,1,0:T(8,128)S(1)} %get-tuple-element.66), channel_id=1, source_target_pairs={{0,8},{8,0},{1,9},{9,1},{2,10},{10,2},{3,11},{11,3},{4,12},{12,4},... | collective-permute-start | bytes 196616 | tf_op jit(solution)/shard_map/ppermute | solution.py:601
  27.7 0.4 collective-permute-start.6
  28.2 0.3 collective-permute-done.4.a_other_ref
  28.5 0.4 collective-permute-done.5.b_other_ref
  29.0 0.9 %shard_map.136 = f32[8,6,8,128]{3,2,1,0:T(8,128)} custom-call(s32[1]{0:T(128)} %bitcast.5.core_ref, f32[2,8,8,128]{3,2,1,0:T(8,128)S(1)} %get-tuple-element.65.a_ref, f32[2,8,8,128]{3,2,1,0:T(8,128)S(1)} %collective-permute-done.4.a_other_ref, f32[2,8,8,128]{3,2,1,0:T(8,128)S(1)} %get-tuple-element.67.b_ref, ...), custom_call_target="tpu_custom_call" | custom-call | flops 262144 | bytes 262144 | tf_op jit(solution)/shard_map/pallas_call | solution.py:21
  29.9 5.8 %all-to-all-start.1 = ((f32[8,6,8,128]{3,2,1,0:T(8,128)}), f32[8,6,8,128]{3,2,1,0:T(8,128)S(1)}, u32[]{:S(2)}, u32[]{:S(2)}) async-start(f32[8,6,8,128]{3,2,1,0:T(8,128)} %shard_map.136), calls=%async_computation.1 | async-start | bytes 393216 | tf_op jit(solution)/shard_map/all_to_all | solution.py:686
  35.8 1.5 %collective-permute-start.2 = (f32[264,128]{1,0:T(8,128)S(1)}, f32[264,128]{1,0:T(8,128)S(1)}, u32[]{:S(2)}, u32[]{:S(2)}) collective-permute-start(f32[264,128]{1,0:T(8,128)S(1)} %get-tuple-element.47.total_ref.joined_ref), channel_id=1, source_target_pairs={{0,32},{8,40},{16,48},{24,56},{32,0},{40,8},{48,16},{56,24},{64,96... | collective-permute-start | bytes 405512 | tf_op jit(solution)/shard_map/ppermute | solution.py:643
  37.2 2.7 %shard_map.132 = (f32[2048,128]{1,0:T(8,128)}, f32[2048,128]{1,0:T(8,128)}) custom-call(f32[256,128]{1,0:T(8,128)S(1)} %bitcast.15, f32[2048,128]{1,0:T(8,128)S(1)} %get-tuple-element.41.x_ref, f32[2048,128]{1,0:T(8,128)S(1)} %get-tuple-element.42.b_ref, f32[264,128]{1,0:T(8,128)S(1)} %get-tuple-element.47.total_ref.joined_ref, f32[8,128]{1,0:T(8,128)} %bitcast.25), custom_call_target="tpu_custom_call" | custom-call | flops 10485760 | bytes 4194304 | tf_op jit(solution)/shard_map/pallas_call | solution.py:21
  39.9 1.7 %all-to-all-done.1.s_ref = f32[8,6,8,128]{3,2,1,0:T(8,128)S(1)} async-done(((f32[8,6,8,128]{3,2,1,0:T(8,128)}), f32[8,6,8,128]{3,2,1,0:T(8,128)S(1)}, u32[]{:S(2)}, u32[]{:S(2)}) %all-to-all-start.1) | async-done | bytes 196640 | tf_op jit(solution)/shard_map/all_to_all | solution.py:686
  41.7 1.0 %shard_map.137 = f32[16,8,2,128]{3,2,1,0:T(2,128)} custom-call(f32[8,6,8,128]{3,2,1,0:T(8,128)S(1)} %all-to-all-done.1.s_ref, f32[2,8,128]{2,1,0:T(8,128)S(1)} %get-tuple-element.72.rate_ref, f32[2048,128]{1,0:T(8,128)} %get-tuple-element.50.y_hbm.done_hbm), custom_call_target="tpu_custom_call" | custom-call | flops 100000 | bytes 1000000 | tf_op jit(solution)/shard_map/pallas_call | solution.py:21
  42.7 5.4 %all-to-all-start.2 = ((f32[128,2,128]{2,1,0:T(2,128)}), f32[128,2,128]{2,1,0:T(2,128)S(1)}, u32[]{:S(2)}, u32[]{:S(2)}) async-start(f32[128,2,128]{2,1,0:T(2,128)} %bitcast.24), calls=%async_computation.2 | async-start | bytes 262144 | tf_op jit(solution)/shard_map/all_to_all | solution.py:696
  48.3 3.5 %collective-permute-start.3 = (f32[136,128]{1,0:T(8,128)S(1)}, f32[136,128]{1,0:T(8,128)S(1)}, u32[]{:S(2)}, u32[]{:S(2)}) collective-permute-start(f32[136,128]{1,0:T(8,128)S(1)} %get-tuple-element.59.total_ref), channel_id=1, source_target_pairs={{0,64},{8,72},{16,80},{24,88},{32,96},{40,104},{48,112},{56,120},{... | collective-permute-start | bytes 208904 | tf_op jit(solution)/shard_map/ppermute | solution.py:643
  51.8 3.8 %shard_map.134.loc_ref = f32[2,2048,128]{2,1,0:T(8,128)S(1)} custom-call(f32[256,128]{1,0:T(8,128)S(1)} %bitcast.17, f32[256,128]{1,0:T(8,128)S(1)} %get-tuple-element.49.held_ref, f32[2048,128]{1,0:T(8,128)} %get-tuple-element.50.y_hbm.done_hbm, f32[2048,128]{1,0:T(8,128)} %get-tuple-element.51.z_hbm, f32[16,128,128]{2,1,0:T(8,128)} %get-tuple-element.57.hs_hbm, ...), custom_call_target="tpu_custom_call" | custom-call | flops 16777216 | bytes 4194304 | tf_op jit(solution)/shard_map/pallas_call | solution.py:21
  55.6 3.9 %shard_map.135 = (bf16[256,1024]{1,0:T(8,128)(2,1)}, bf16[256,1024]{1,0:T(8,128)(2,1)}, bf16[256,1024]{1,0:T(8,128)(2,1)}, bf16[256,1024]{1,0:T(8,128)(2,1)}, f32[8,128]{1,0:T(8,128)}) custom-call(s32[1]{0:T(128)} %bitcast.index_ref, f32[256,128]{1,0:T(8,128)S(1)} %bitcast.18, f32[2,2048,128]{2,1,0:T(8,128)S(1)} %shard_map.134.loc_ref, ...), custom_call_target="tpu_custom_call" | custom-call | flops 8388608 | bytes 4194304 | tf_op jit(solution)/shard_map/pallas_call | solution.py:21
  59.5 0.8 %shard_map.138 = (f32[16,128]{1,0:T(8,128)}, f32[16,128]{1,0:T(8,128)}) custom-call(f32[16,8,2,128]{3,2,1,0:T(2,128)S(1)} %bitcast.19, f32[16,128]{1,0:T(8,128)S(1)} %bitcast.23, f32[16,128]{1,0:T(8,128)S(1)} %bitcast.21), custom_call_target="tpu_custom_call" | custom-call | flops 100000 | bytes 1000000 | tf_op jit(solution)/shard_map/pallas_call | solution.py:21
  (13 shorter events, 0.5 us)
Async XLA Ops:
  2.1 14.3 %all-to-all-start = ((f32[8,32,128]{2,1,0:T(8,128)}), f32[8,32,128]{2,1,0:T(8,128)S(1)}, u32[]{:S(2)}, u32[]{:S(2)}) async-start(f32[8,32,128]{2,1,0:T(8,128)} %shard_map.126), calls=%async_computation | async-start | bytes 262144 | tf_op jit(solution)/shard_map/all_to_all | solution.py:618
  19.0 3.2 %collective-permute-start = (f32[264,128]{1,0:T(8,128)S(1)}, f32[264,128]{1,0:T(8,128)S(1)}, u32[]{:S(2)}, u32[]{:S(2)}) collective-permute-start(f32[264,128]{1,0:T(8,128)S(1)} %get-tuple-element.44.total_ref), channel_id=1, source_target_pairs={{0,8},{8,0},{16,24},{24,16},{32,40},{40,32},{48,56},{56,48},{64,72... | collective-permute-start | bytes 405512 | tf_op jit(solution)/shard_map/ppermute | solution.py:643
  22.2 5.9 %collective-permute-start.1 = (f32[264,128]{1,0:T(8,128)S(1)}, f32[264,128]{1,0:T(8,128)S(1)}, u32[]{:S(2)}, u32[]{:S(2)}) collective-permute-start(f32[264,128]{1,0:T(8,128)S(1)} %get-tuple-element.45.total_ref.joined_ref), channel_id=1, source_target_pairs={{0,16},{8,24},{16,0},{24,8},{32,48},{40,56},{48,32},{56,40},{64,80... | collective-permute-start | bytes 405512 | tf_op jit(solution)/shard_map/ppermute | solution.py:643
  26.9 1.6 %collective-permute-start.4 = (f32[2,8,8,128]{3,2,1,0:T(8,128)S(1)}, f32[2,8,8,128]{3,2,1,0:T(8,128)S(1)}, u32[]{:S(2)}, u32[]{:S(2)}) collective-permute-start(f32[2,8,8,128]{3,2,1,0:T(8,128)S(1)} %get-tuple-element.66), channel_id=1, source_target_pairs={{0,8},{8,0},{1,9},{9,1},{2,10},{10,2},{3,11},{11,3},{4,12},{12,4},... | collective-permute-start | bytes 196616 | tf_op jit(solution)/shard_map/ppermute | solution.py:601
  27.6 1.3 %collective-permute-start.5 = (f32[2,8,8,128]{3,2,1,0:T(8,128)S(1)}, f32[2,8,8,128]{3,2,1,0:T(8,128)S(1)}, u32[]{:S(2)}, u32[]{:S(2)}) collective-permute-start(f32[2,8,8,128]{3,2,1,0:T(8,128)S(1)} %get-tuple-element.68), channel_id=1, source_target_pairs={{0,8},{8,0},{1,9},{9,1},{2,10},{10,2},{3,11},{11,3},{4,12},{12,4},... | collective-permute-start | bytes 196616 | tf_op jit(solution)/shard_map/ppermute | solution.py:601
  27.7 1.3 %collective-permute-start.6 = (f32[2,8,8,128]{3,2,1,0:T(8,128)S(1)}, f32[2,8,8,128]{3,2,1,0:T(8,128)S(1)}, u32[]{:S(2)}, u32[]{:S(2)}) collective-permute-start(f32[2,8,8,128]{3,2,1,0:T(8,128)S(1)} %get-tuple-element.70), channel_id=1, source_target_pairs={{0,8},{8,0},{1,9},{9,1},{2,10},{10,2},{3,11},{11,3},{4,12},{12,4},... | collective-permute-start | bytes 196616 | tf_op jit(solution)/shard_map/ppermute | solution.py:601
  29.9 11.7 %all-to-all-start.1 = ((f32[8,6,8,128]{3,2,1,0:T(8,128)}), f32[8,6,8,128]{3,2,1,0:T(8,128)S(1)}, u32[]{:S(2)}, u32[]{:S(2)}) async-start(f32[8,6,8,128]{3,2,1,0:T(8,128)} %shard_map.136), calls=%async_computation.1 | async-start | bytes 393216 | tf_op jit(solution)/shard_map/all_to_all | solution.py:686
  35.8 12.4 %collective-permute-start.2 = (f32[264,128]{1,0:T(8,128)S(1)}, f32[264,128]{1,0:T(8,128)S(1)}, u32[]{:S(2)}, u32[]{:S(2)}) collective-permute-start(f32[264,128]{1,0:T(8,128)S(1)} %get-tuple-element.47.total_ref.joined_ref), channel_id=1, source_target_pairs={{0,32},{8,40},{16,48},{24,56},{32,0},{40,8},{48,16},{56,24},{64,96... | collective-permute-start | bytes 405512 | tf_op jit(solution)/shard_map/ppermute | solution.py:643
  42.7 16.8 %all-to-all-start.2 = ((f32[128,2,128]{2,1,0:T(2,128)}), f32[128,2,128]{2,1,0:T(2,128)S(1)}, u32[]{:S(2)}, u32[]{:S(2)}) async-start(f32[128,2,128]{2,1,0:T(2,128)} %bitcast.24), calls=%async_computation.2 | async-start | bytes 262144 | tf_op jit(solution)/shard_map/all_to_all | solution.py:696
  48.3 7.3 %collective-permute-start.3 = (f32[136,128]{1,0:T(8,128)S(1)}, f32[136,128]{1,0:T(8,128)S(1)}, u32[]{:S(2)}, u32[]{:S(2)}) collective-permute-start(f32[136,128]{1,0:T(8,128)S(1)} %get-tuple-element.59.total_ref), channel_id=1, source_target_pairs={{0,64},{8,72},{16,80},{24,88},{32,96},{40,104},{48,112},{56,120},{... | collective-permute-start | bytes 208904 | tf_op jit(solution)/shard_map/ppermute | solution.py:643
  55.5 4.0 %copy-start = (f32[128,16]{0,1:T(8,128)S(1)}, f32[128,16]{0,1:T(8,128)}, u32[]{:S(2)}) copy-start(f32[128,16]{0,1:T(8,128)} %param.13) | copy-start | bytes 24580
  55.6 4.0 %copy-start.1 = (f32[128,16]{0,1:T(8,128)S(1)}, f32[128,16]{0,1:T(8,128)}, u32[]{:S(2)}) copy-start(f32[128,16]{0,1:T(8,128)} %param.12) | copy-start | bytes 24580

commit v9 on v8

--- a/solution.py
+++ b/solution.py
@@ -170,10 +170,37 @@
     wait_all(copies)
 
 
+def layout_body(
+    index_ref, core_ref, par_ref, total_ref,
+    rate_ref, side_rate_ref, keep_ref, send_ref,
+    sums_ref, turn_ref, rates_ref,
+    *, modes,
+):
+    owners, share = turn_ref.shape[0], turn_ref.shape[1]
+    groups = sums_ref.shape[0] // LANES
+    blocks = par_ref.shape[0] // modes // 2
+    for m in range(modes):
+        for kind in range(2):
+            state = total_ref[pl.ds((kind * modes + m) * blocks, blocks), :]
+            sums_ref[pl.ds(kind * modes + m, blocks, stride=2 * modes), :] = state
+    for group in range(groups):
+        turn_ref[...] = turned(sums_ref, group, owners)
+        part_slices(core_ref[0], turn_ref, keep_ref.at[group], send_ref.at[group])
+    for group in range(groups):
+        for block in range(group * blocks // groups, (group + 1) * blocks // groups):
+            decay = par_ref[pl.ds(block * 2 * modes, modes), :]
+            rates_ref[pl.ds(block * 2 * modes, 2 * modes), :] = jnp.concatenate([decay, decay], axis=0)
+        rates_ref[pl.ds(group * LANES, LANES), :] = rates_ref[pl.ds(group * LANES, LANES), :].T
+        rate_ref[group] = rates_ref[pl.ds(pl.multiple_of(group * LANES + index_ref[0] * share, share), share), :]
+        for chip in range(side_rate_ref.shape[1]):
+            start = group * LANES + (2 * chip + core_ref[0]) * share
+            side_rate_ref[group, chip] = rates_ref[pl.ds(pl.multiple_of(start, share), share), :]
+
+
 def slope_body(
-    index_ref, core_ref, par_ref, x_ref, b_ref, lag_ref, total_ref, joined_ref, hs_in, bs_in, hs_last_ref, bs_last_ref,
-    hs_hbm, bs_hbm, rate_ref, side_rate_ref, keep_s_ref, send_s_ref, keep_a_ref, send_a_ref, keep_b_ref, send_b_ref,
-    hs_ref, bs_ref, up_ref, down_ref, run_ref, sums_ref, turn_ref, rates_ref, snap_sem,
+    core_ref, par_ref, x_ref, b_ref, lag_ref, done_ref, joined_ref, hs_in, bs_in, hs_last_ref, bs_last_ref,
+    hs_hbm, bs_hbm, keep_a_ref, send_a_ref, keep_b_ref, send_b_ref,
+    hs_ref, bs_ref, up_ref, down_ref, run_ref, sums_ref, turn_ref, snap_sem,
 ):
     owners = turn_ref.shape[0]
     groups = sums_ref.shape[0] // LANES
@@ -193,7 +220,6 @@
     ])
     hs_ref[rest:] = hs_last_ref[...]
     bs_ref[: part_spans + 1] = bs_last_ref[...]
-    share = rate_ref.shape[1]
     zero = jnp.zeros((blocks, LANES), jnp.float32)
     SLOPE, SUM0, SUM1, DOWN, POWER, FACTOR, FAR = range(7)
     for m in range(modes):
@@ -215,20 +241,6 @@
 
     def at(m):
         return pl.ds(m * blocks, blocks)
-
-    def totals(kind):
-        return lambda m: total_ref[pl.ds((kind * modes + m) * blocks, blocks), :]
-
-    part(totals(0), totals(1), keep_s_ref, send_s_ref)
-    for group in range(groups):
-        for block in range(group * blocks // groups, (group + 1) * blocks // groups):
-            decay = par_ref[pl.ds(block * 2 * modes, modes), :]
-            rates_ref[pl.ds(block * 2 * modes, 2 * modes), :] = jnp.concatenate([decay, decay], axis=0)
-        rates_ref[pl.ds(group * LANES, LANES), :] = rates_ref[pl.ds(group * LANES, LANES), :].T
-        rate_ref[group] = rates_ref[pl.ds(pl.multiple_of(group * LANES + index_ref[0] * share, share), share), :]
-        for chip in range(side_rate_ref.shape[1]):
-            start = group * LANES + (2 * chip + core_ref[0]) * share
-            side_rate_ref[group, chip] = rates_ref[pl.ds(pl.multiple_of(start, share), share), :]
 
     def near(span, carry):
         late = [x_ref[position(span, r, blocks), :] * (SPAN - 1.0 - r) for r in range(SPAN - 1)]
@@ -637,6 +649,14 @@
         [pltpu.VMEM(heads_at, f32), pltpu.VMEM(tails_at, f32), DMA((2, pieces))],
     )([VMEM] * 4, params, x, b, sk)
 
+    rates, side_rates, own_s, send_s = call(
+        functools.partial(layout_body, modes=modes),
+        [((groups, *tile), f32, VMEM)] + [(side, f32, VMEM)] * 3,
+        8,
+        (size, size),
+        [sums, pltpu.VMEM((owners, *tile), f32), sums],
+    )([SMEM] * 2 + [VMEM] * 2, place, core, params, total)
+
     totals, held, others = [total], [], []
     steps = (owners - 1).bit_length()
     for step in range(steps):
@@ -649,7 +669,7 @@
             [(((modes + 1) * blocks, LANES) if last else total_at, f32, VMEM), ((2 * modes * blocks, LANES), f32, VMEM)],
             8,
             (size, size),
-        )([SMEM] + [VMEM] * (3 + len(held)), place, params, totals[-1], others[-1], *held)
+        )([SMEM] + [VMEM] * (3 + len(held) + (step == 0)), place, params, totals[-1], others[-1], *held, *[side_rates] * (step == 0))
         totals.append(total)
 
     y, z = call(
@@ -660,17 +680,17 @@
         [pltpu.VMEM((blocks, LANES), f32), pltpu.VMEM((2, *signal), f32), DMA, DMA((2, pieces))],
     )([VMEM] * 4 + [HBM], params, x, b, totals[2], skip.reshape(blocks, LANES))
 
-    head_states, tail_states, rates, side_rates, own_s, send_s, own_a, send_a, own_b, send_b = call(
+    head_states, tail_states, own_a, send_a, own_b, send_b = call(
         slope_body,
-        [(heads_at, f32, HBM), (tails_at, f32, HBM), ((groups, *tile), f32, VMEM)] + [(side, f32, VMEM)] * 7,
+        [(heads_at, f32, HBM), (tails_at, f32, HBM)] + [(side, f32, VMEM)] * 4,
         16,
         (100 * size, 16 * size),
         [pltpu.VMEM(heads_at, f32), pltpu.VMEM(tails_at, f32), pltpu.VMEM(heads_at, f32), pltpu.VMEM(heads_at, f32)]
-        + [pltpu.VMEM((7, modes * blocks, LANES), f32), sums, pltpu.VMEM((owners, *tile), f32), sums, DMA((4,))],
-        {8: 0, 9: 1},
+        + [pltpu.VMEM((7, modes * blocks, LANES), f32), sums, pltpu.VMEM((owners, *tile), f32), DMA((4,))],
+        {7: 0, 8: 1},
     )(
-        [SMEM] * 2 + [VMEM] * 6 + [HBM] * 2 + [VMEM] * 2,
-        place, core, params, x, b, lag, totals[0], totals[1], head_states, tail_states, last_heads, last_tails,
+        [SMEM] + [VMEM] * 6 + [HBM] * 2 + [VMEM] * 2,
+        core, params, x, b, lag, side_rates, totals[1], head_states, tail_states, last_heads, last_tails,
     )
 
     (states,) = call(

time: 60.7 us -> 60.6 us (level)
    pallas_call x13 -> x14, Pallas kernels: 24 us -> 24 us  [call(): pl.pallas_call(body, out_shape=[pltpu.HBM(s, t) if w is HBM else jax.Shap...]
  transfers between devices with their start and end apart: 10 -> 10, of which waited for: 6 -> 5; matrix products, arithmetic and copies ran while one was open for 0% -> 0% of each run, Pallas kernels for 30% -> 30%
where the time goes in v9:
time: 60.6 us; the launch traced here: 60.1 us
  starting transfers between devices  27.6 us (46%)
  Pallas kernels  24 us (40%)
  waiting for transfers between devices  7.69 us (13%)
  between operations  0.81 us (1%)
    pallas_call x14, Pallas kernels, call(): pl.pallas_call(body, out_shape=[pltpu.HBM(s, t) if w is HBM else jax.Shap...  24 us
    ppermute x4, starting transfers between devices, on_device(): lax.ppermute(totals[-1], ctx, [(i, i ^ 2 ** step) for i in range(owners)])  7.62 us
    all_to_all x1, starting transfers between devices, on_device(): lax.all_to_all(sent, 'ch', 0, 0, tiled=True)  7.49 us
    all_to_all x1, starting transfers between devices, on_device(): states = lax.all_to_all(states, 'chip', 0, 0, tiled=True)  5.83 us
    all_to_all x1, starting transfers between devices, on_device(): lax.all_to_all(grads.reshape(owners * blocks, *packed[2:]), ('chip', 'cor...  5.42 us
    all_to_all x1, waiting for transfers between devices, on_device(): lax.all_to_all(sent, 'ch', 0, 0, tiled=True)  4.37 us
    all_to_all x1, waiting for transfers between devices, on_device(): states = lax.all_to_all(states, 'chip', 0, 0, tiled=True)  1.74 us
    ppermute x3, starting transfers between devices, change(): lax.ppermute(value, 'core', [(i, cores - 1 - i) for i in range(cores)])  1.22 us
  transfers between devices with their start and end apart: 10, of which 5 were waited for; matrix products, arithmetic and copies ran while one was open for 0% of the time, Pallas kernels for 30%

profile of v9, /device:TPU:1, one launch (start us, length us, event | category | flops | bytes accessed | tf_op | source)
XLA Modules:
  0.0 60.1 jit_solution(13634326204377219198)
XLA Ops:
  0.6 1.4 %shard_map.126 = f32[8,32,128]{2,1,0:T(8,128)} custom-call(f32[16,128]{1,0:T(8,128)} %bitcast.21, f32[16,128]{1,0:T(8,128)} %bitcast.23), custom_call_target="tpu_custom_call" | custom-call | bytes 100000 | tf_op jit(solution)/shard_map/pallas_call | solution.py:21
  2.1 7.5 %all-to-all-start = ((f32[8,32,128]{2,1,0:T(8,128)}), f32[8,32,128]{2,1,0:T(8,128)S(1)}, u32[]{:S(2)}, u32[]{:S(2)}) async-start(f32[8,32,128]{2,1,0:T(8,128)} %shard_map.126), calls=%async_computation | async-start | bytes 262144 | tf_op jit(solution)/shard_map/all_to_all | solution.py:630
  9.6 2.4 %shard_map.127 = (f32[2048,128]{1,0:T(8,128)S(1)}, f32[2048,128]{1,0:T(8,128)S(1)}, f32[8,128]{1,0:T(8,128)S(1)}, f32[128,128]{1,0:T(8,128)S(1)}) custom-call(bf16[256,1024]{1,0:T(8,128)(2,1)} %gate_hbm.3, bf16[256,1024]{1,0:T(8,128)(2,1)} %key_hbm.3, bf16[256,1024]{1,0:T(8,128)(2,1)} %value_hbm.3, bf16[256,1024]{1,0:T(8,128)(2,1)} %cot_hbm.3), custom_call_target="tpu_custom_call" | custom-call | flops 2097152 | bytes 4194304 | tf_op jit(solution)/shard_map/pallas_call | solution.py:21
  12.0 4.4 %all-to-all-done = f32[8,32,128]{2,1,0:T(8,128)S(1)} async-done(((f32[8,32,128]{2,1,0:T(8,128)}), f32[8,32,128]{2,1,0:T(8,128)S(1)}, u32[]{:S(2)}, u32[]{:S(2)}) %all-to-all-start) | async-done | bytes 131104 | tf_op jit(solution)/shard_map/all_to_all | solution.py:630
  16.3 2.6 %shard_map.128 = (f32[264,128]{1,0:T(8,128)S(1)}, f32[16,128,128]{2,1,0:T(8,128)}, f32[17,128,128]{2,1,0:T(8,128)}, f32[4,128,128]{2,1,0:T(8,128)S(1)}, f32[5,128,128]{2,1,0:T(8,128)S(1)}) custom-call(f32[256,128]{1,0:T(8,128)S(1)} %bitcast.11, f32[2048,128]{1,0:T(8,128)S(1)} %get-tuple-element.41.x_ref, f32[2048,128]{1,0:T(8,128)S(1)} %get-tuple-element.42.b_ref, ...), custom_call_target="tpu_custom_call" | custom-call | flops 16777216 | bytes 4194304 | tf_op jit(solution)/shard_map/pallas_call | solution.py:21
  19.0 2.2 %collective-permute-start = (f32[264,128]{1,0:T(8,128)S(1)}, f32[264,128]{1,0:T(8,128)S(1)}, u32[]{:S(2)}, u32[]{:S(2)}) collective-permute-start(f32[264,128]{1,0:T(8,128)S(1)} %get-tuple-element.44.total_ref), channel_id=1, source_target_pairs={{0,8},{8,0},{16,24},{24,16},{32,40},{40,32},{48,56},{56,48},{64,72... | collective-permute-start | bytes 405512 | tf_op jit(solution)/shard_map/ppermute | solution.py:663
  21.2 0.2 shard_map.129
  21.4 0.8 %collective-permute-done.other_ref = f32[264,128]{1,0:T(8,128)S(1)} collective-permute-done((f32[264,128]{1,0:T(8,128)S(1)}, f32[264,128]{1,0:T(8,128)S(1)}, u32[]{:S(2)}, u32[]{:S(2)}) %collective-permute-start) | collective-permute-done | bytes 135200 | tf_op jit(solution)/shard_map/ppermute | solution.py:663
  22.2 0.5 collective-permute-start.1
  22.7 0.6 %collective-permute-start.6 = (f32[2,8,8,128]{3,2,1,0:T(8,128)S(1)}, f32[2,8,8,128]{3,2,1,0:T(8,128)S(1)}, u32[]{:S(2)}, u32[]{:S(2)}) collective-permute-start(f32[2,8,8,128]{3,2,1,0:T(8,128)S(1)} %get-tuple-element.71), channel_id=1, source_target_pairs={{0,8},{8,0},{1,9},{9,1},{2,10},{10,2},{3,11},{11,3},{4,12},{12,4},... | collective-permute-start | bytes 196616 | tf_op jit(solution)/shard_map/ppermute | solution.py:613
  23.4 4.0 %shard_map.134 = (f32[16,128,128]{2,1,0:T(8,128)}, f32[17,128,128]{2,1,0:T(8,128)}, f32[2,8,8,128]{3,2,1,0:T(8,128)S(1)}, f32[2,8,8,128]{3,2,1,0:T(8,128)S(1)}, ...) custom-call(s32[1]{0:T(128)} %bitcast.4.core_ref, ...), custom_call_target="tpu_custom_call", output_to_operand_aliasing={{0}: (7, {}), {1}: (8, {})} | custom-call | flops 26214400 | bytes 4194304 | tf_op jit(solution)/shard_map/pallas_call | solution.py:21
  27.5 0.5 collective-permute-start.5
  28.1 0.6 %collective-permute-done.4.a_other_ref = f32[2,8,8,128]{3,2,1,0:T(8,128)S(1)} collective-permute-done((f32[2,8,8,128]{3,2,1,0:T(8,128)S(1)}, f32[2,8,8,128]{3,2,1,0:T(8,128)S(1)}, u32[]{:S(2)}, u32[]{:S(2)}) %collective-permute-start.4) | collective-permute-done | bytes 65568 | tf_op jit(solution)/shard_map/ppermute | solution.py:613
  28.9 0.9 %shard_map.137 = f32[8,6,8,128]{3,2,1,0:T(8,128)} custom-call(s32[1]{0:T(128)} %bitcast.4.core_ref, f32[2,8,8,128]{3,2,1,0:T(8,128)S(1)} %get-tuple-element.66.a_ref, f32[2,8,8,128]{3,2,1,0:T(8,128)S(1)} %collective-permute-done.4.a_other_ref, f32[2,8,8,128]{3,2,1,0:T(8,128)S(1)} %get-tuple-element.68.b_ref, ...), custom_call_target="tpu_custom_call" | custom-call | flops 262144 | bytes 262144 | tf_op jit(solution)/shard_map/pallas_call | solution.py:21
  29.8 5.8 %all-to-all-start.1 = ((f32[8,6,8,128]{3,2,1,0:T(8,128)}), f32[8,6,8,128]{3,2,1,0:T(8,128)S(1)}, u32[]{:S(2)}, u32[]{:S(2)}) async-start(f32[8,6,8,128]{3,2,1,0:T(8,128)} %shard_map.137), calls=%async_computation.1 | async-start | bytes 393216 | tf_op jit(solution)/shard_map/all_to_all | solution.py:706
  35.6 1.5 %collective-permute-start.2 = (f32[264,128]{1,0:T(8,128)S(1)}, f32[264,128]{1,0:T(8,128)S(1)}, u32[]{:S(2)}, u32[]{:S(2)}) collective-permute-start(f32[264,128]{1,0:T(8,128)S(1)} %get-tuple-element.48.total_ref.joined_ref), channel_id=1, source_target_pairs={{0,32},{8,40},{16,48},{24,56},{32,0},{40,8},{48,16},{56,24},{64,96... | collective-permute-start | bytes 405512 | tf_op jit(solution)/shard_map/ppermute | solution.py:663
  37.1 2.7 %shard_map.133 = (f32[2048,128]{1,0:T(8,128)}, f32[2048,128]{1,0:T(8,128)}) custom-call(f32[256,128]{1,0:T(8,128)S(1)} %bitcast.16, f32[2048,128]{1,0:T(8,128)S(1)} %get-tuple-element.41.x_ref, f32[2048,128]{1,0:T(8,128)S(1)} %get-tuple-element.42.b_ref, f32[264,128]{1,0:T(8,128)S(1)} %get-tuple-element.48.total_ref.joined_ref, f32[8,128]{1,0:T(8,128)} %bitcast.26), custom_call_target="tpu_custom_call" | custom-call | flops 10485760 | bytes 4194304 | tf_op jit(solution)/shard_map/pallas_call | solution.py:21
  39.8 1.7 %all-to-all-done.1.s_ref = f32[8,6,8,128]{3,2,1,0:T(8,128)S(1)} async-done(((f32[8,6,8,128]{3,2,1,0:T(8,128)}), f32[8,6,8,128]{3,2,1,0:T(8,128)S(1)}, u32[]{:S(2)}, u32[]{:S(2)}) %all-to-all-start.1) | async-done | bytes 196640 | tf_op jit(solution)/shard_map/all_to_all | solution.py:706
  41.5 1.0 %shard_map.138 = f32[16,8,2,128]{3,2,1,0:T(2,128)} custom-call(f32[8,6,8,128]{3,2,1,0:T(8,128)S(1)} %all-to-all-done.1.s_ref, f32[2,8,128]{2,1,0:T(8,128)S(1)} %get-tuple-element.72.rate_ref, f32[2048,128]{1,0:T(8,128)} %get-tuple-element.51.y_hbm.done_hbm), custom_call_target="tpu_custom_call" | custom-call | flops 100000 | bytes 1000000 | tf_op jit(solution)/shard_map/pallas_call | solution.py:21
  42.6 5.4 %all-to-all-start.2 = ((f32[128,2,128]{2,1,0:T(2,128)}), f32[128,2,128]{2,1,0:T(2,128)S(1)}, u32[]{:S(2)}, u32[]{:S(2)}) async-start(f32[128,2,128]{2,1,0:T(2,128)} %bitcast.25), calls=%async_computation.2 | async-start | bytes 262144 | tf_op jit(solution)/shard_map/all_to_all | solution.py:716
  48.1 3.5 %collective-permute-start.3 = (f32[136,128]{1,0:T(8,128)S(1)}, f32[136,128]{1,0:T(8,128)S(1)}, u32[]{:S(2)}, u32[]{:S(2)}) collective-permute-start(f32[136,128]{1,0:T(8,128)S(1)} %get-tuple-element.60.total_ref), channel_id=1, source_target_pairs={{0,64},{8,72},{16,80},{24,88},{32,96},{40,104},{48,112},{56,120},{... | collective-permute-start | bytes 208904 | tf_op jit(solution)/shard_map/ppermute | solution.py:663
  51.6 3.8 %shard_map.135.loc_ref = f32[2,2048,128]{2,1,0:T(8,128)S(1)} custom-call(f32[256,128]{1,0:T(8,128)S(1)} %bitcast.18, f32[256,128]{1,0:T(8,128)S(1)} %get-tuple-element.50.held_ref, f32[2048,128]{1,0:T(8,128)} %get-tuple-element.51.y_hbm.done_hbm, f32[2048,128]{1,0:T(8,128)} %get-tuple-element.52.z_hbm, f32[16,128,128]{2,1,0:T(8,128)} %get-tuple-element.58.hs_hbm, ...), custom_call_target="tpu_custom_call" | custom-call | flops 16777216 | bytes 4194304 | tf_op jit(solution)/shard_map/pallas_call | solution.py:21
  55.4 3.9 %shard_map.136 = (bf16[256,1024]{1,0:T(8,128)(2,1)}, bf16[256,1024]{1,0:T(8,128)(2,1)}, bf16[256,1024]{1,0:T(8,128)(2,1)}, bf16[256,1024]{1,0:T(8,128)(2,1)}, f32[8,128]{1,0:T(8,128)}) custom-call(s32[1]{0:T(128)} %bitcast.index_ref, f32[256,128]{1,0:T(8,128)S(1)} %bitcast.19, f32[2,2048,128]{2,1,0:T(8,128)S(1)} %shard_map.135.loc_ref, ...), custom_call_target="tpu_custom_call" | custom-call | flops 8388608 | bytes 4194304 | tf_op jit(solution)/shard_map/pallas_call | solution.py:21
  59.4 0.8 %shard_map.139 = (f32[16,128]{1,0:T(8,128)}, f32[16,128]{1,0:T(8,128)}) custom-call(f32[16,8,2,128]{3,2,1,0:T(2,128)S(1)} %bitcast.20, f32[16,128]{1,0:T(8,128)S(1)} %bitcast.24, f32[16,128]{1,0:T(8,128)S(1)} %bitcast.22), custom_call_target="tpu_custom_call" | custom-call | flops 100000 | bytes 1000000 | tf_op jit(solution)/shard_map/pallas_call | solution.py:21
  (14 shorter events, 0.5 us)
Async XLA Ops:
  2.1 14.3 %all-to-all-start = ((f32[8,32,128]{2,1,0:T(8,128)}), f32[8,32,128]{2,1,0:T(8,128)S(1)}, u32[]{:S(2)}, u32[]{:S(2)}) async-start(f32[8,32,128]{2,1,0:T(8,128)} %shard_map.126), calls=%async_computation | async-start | bytes 262144 | tf_op jit(solution)/shard_map/all_to_all | solution.py:630
  19.0 3.2 %collective-permute-start = (f32[264,128]{1,0:T(8,128)S(1)}, f32[264,128]{1,0:T(8,128)S(1)}, u32[]{:S(2)}, u32[]{:S(2)}) collective-permute-start(f32[264,128]{1,0:T(8,128)S(1)} %get-tuple-element.44.total_ref), channel_id=1, source_target_pairs={{0,8},{8,0},{16,24},{24,16},{32,40},{40,32},{48,56},{56,48},{64,72... | collective-permute-start | bytes 405512 | tf_op jit(solution)/shard_map/ppermute | solution.py:663
  22.2 5.7 %collective-permute-start.1 = (f32[264,128]{1,0:T(8,128)S(1)}, f32[264,128]{1,0:T(8,128)S(1)}, u32[]{:S(2)}, u32[]{:S(2)}) collective-permute-start(f32[264,128]{1,0:T(8,128)S(1)} %get-tuple-element.46.total_ref.joined_ref), channel_id=1, source_target_pairs={{0,16},{8,24},{16,0},{24,8},{32,48},{40,56},{48,32},{56,40},{64,80... | collective-permute-start | bytes 405512 | tf_op jit(solution)/shard_map/ppermute | solution.py:663
  22.7 5.4 %collective-permute-start.6 = (f32[2,8,8,128]{3,2,1,0:T(8,128)S(1)}, f32[2,8,8,128]{3,2,1,0:T(8,128)S(1)}, u32[]{:S(2)}, u32[]{:S(2)}) collective-permute-start(f32[2,8,8,128]{3,2,1,0:T(8,128)S(1)} %get-tuple-element.71), channel_id=1, source_target_pairs={{0,8},{8,0},{1,9},{9,1},{2,10},{10,2},{3,11},{11,3},{4,12},{12,4},... | collective-permute-start | bytes 196616 | tf_op jit(solution)/shard_map/ppermute | solution.py:613
  27.4 1.3 %collective-permute-start.4 = (f32[2,8,8,128]{3,2,1,0:T(8,128)S(1)}, f32[2,8,8,128]{3,2,1,0:T(8,128)S(1)}, u32[]{:S(2)}, u32[]{:S(2)}) collective-permute-start(f32[2,8,8,128]{3,2,1,0:T(8,128)S(1)} %get-tuple-element.67), channel_id=1, source_target_pairs={{0,8},{8,0},{1,9},{9,1},{2,10},{10,2},{3,11},{11,3},{4,12},{12,4},... | collective-permute-start | bytes 196616 | tf_op jit(solution)/shard_map/ppermute | solution.py:613
  27.5 1.4 %collective-permute-start.5 = (f32[2,8,8,128]{3,2,1,0:T(8,128)S(1)}, f32[2,8,8,128]{3,2,1,0:T(8,128)S(1)}, u32[]{:S(2)}, u32[]{:S(2)}) collective-permute-start(f32[2,8,8,128]{3,2,1,0:T(8,128)S(1)} %get-tuple-element.69), channel_id=1, source_target_pairs={{0,8},{8,0},{1,9},{9,1},{2,10},{10,2},{3,11},{11,3},{4,12},{12,4},... | collective-permute-start | bytes 196616 | tf_op jit(solution)/shard_map/ppermute | solution.py:613
  29.8 11.7 %all-to-all-start.1 = ((f32[8,6,8,128]{3,2,1,0:T(8,128)}), f32[8,6,8,128]{3,2,1,0:T(8,128)S(1)}, u32[]{:S(2)}, u32[]{:S(2)}) async-start(f32[8,6,8,128]{3,2,1,0:T(8,128)} %shard_map.137), calls=%async_computation.1 | async-start | bytes 393216 | tf_op jit(solution)/shard_map/all_to_all | solution.py:706
  35.6 12.4 %collective-permute-start.2 = (f32[264,128]{1,0:T(8,128)S(1)}, f32[264,128]{1,0:T(8,128)S(1)}, u32[]{:S(2)}, u32[]{:S(2)}) collective-permute-start(f32[264,128]{1,0:T(8,128)S(1)} %get-tuple-element.48.total_ref.joined_ref), channel_id=1, source_target_pairs={{0,32},{8,40},{16,48},{24,56},{32,0},{40,8},{48,16},{56,24},{64,96... | collective-permute-start | bytes 405512 | tf_op jit(solution)/shard_map/ppermute | solution.py:663
  42.6 16.8 %all-to-all-start.2 = ((f32[128,2,128]{2,1,0:T(2,128)}), f32[128,2,128]{2,1,0:T(2,128)S(1)}, u32[]{:S(2)}, u32[]{:S(2)}) async-start(f32[128,2,128]{2,1,0:T(2,128)} %bitcast.25), calls=%async_computation.2 | async-start | bytes 262144 | tf_op jit(solution)/shard_map/all_to_all | solution.py:716
  48.1 7.3 %collective-permute-start.3 = (f32[136,128]{1,0:T(8,128)S(1)}, f32[136,128]{1,0:T(8,128)S(1)}, u32[]{:S(2)}, u32[]{:S(2)}) collective-permute-start(f32[136,128]{1,0:T(8,128)S(1)} %get-tuple-element.60.total_ref), channel_id=1, source_target_pairs={{0,64},{8,72},{16,80},{24,88},{32,96},{40,104},{48,112},{56,120},{... | collective-permute-start | bytes 208904 | tf_op jit(solution)/shard_map/ppermute | solution.py:663
  55.4 4.0 %copy-start = (f32[128,16]{0,1:T(8,128)S(1)}, f32[128,16]{0,1:T(8,128)}, u32[]{:S(2)}) copy-start(f32[128,16]{0,1:T(8,128)} %param.13) | copy-start | bytes 24580
  55.4 4.0 %copy-start.1 = (f32[128,16]{0,1:T(8,128)S(1)}, f32[128,16]{0,1:T(8,128)}, u32[]{:S(2)}) copy-start(f32[128,16]{0,1:T(8,128)} %param.12) | copy-start | bytes 24580
